TPU v7x, 512 devices: a whole 4x8x8 slice. The times are simulated.
512 devices in a mesh: dp: 8 (over x, y_lo), vseq: 32 (over z, y_hi), aseq: 2 (over core).
Axes of the slice: x: 4, y: 8 (y_hi: 4, y_lo: 2; y = y_hi * 2 + y_lo), z: 8, core: 2. Of those that a mesh axis runs over, the one named last changes fastest.
Arguments:
- video_query: bfloat16 [8, 8192, 1536], P('dp', ('vseq', 'aseq')), may hold values from -6 to 6
- video_key: bfloat16 [8, 8192, 1536], P('dp', ('vseq', 'aseq')), may hold values from -6 to 6
- video_value: bfloat16 [8, 8192, 1536], P('dp', ('vseq', 'aseq')), may hold values from -6 to 6
- video_grad: bfloat16 [8, 8192, 1536], P('dp', ('vseq', 'aseq')), may hold values from -6 to 6
- audio_query: bfloat16 [8, 128, 1536], P('dp', 'vseq'), may hold values from -6 to 6
- audio_key: bfloat16 [8, 128, 1536], P('dp', 'vseq'), may hold values from -6 to 6
- audio_value: bfloat16 [8, 128, 1536], P('dp', 'vseq'), may hold values from -6 to 6
- audio_grad: bfloat16 [8, 128, 1536], P('dp', 'vseq'), may hold values from -6 to 6
- video_pos: int32 [8, 8192], P('dp', ('vseq', 'aseq')), may hold values from 0 to 8191
- audio_pos: int32 [8, 128], P('dp', 'vseq'), may hold values from 0 to 8191
- video_len: int32 [8], P('dp'), may hold values from 4096 to 8192
- audio_len: int32 [8], P('dp'), may hold values from 64 to 128
- gain_vq: float32 [1536], replicated, may hold values from 0.1 to 1.9
- gain_vk: float32 [1536], replicated, may hold values from 0.1 to 1.9
- gain_aq: float32 [1536], replicated, may hold values from 0.1 to 1.9
- gain_ak: float32 [1536], replicated, may hold values from 0.1 to 1.9
Outputs:
- grad_video_query: bfloat16 [8, 8192, 1536], P('dp', ('vseq', 'aseq'))
- grad_video_key: bfloat16 [8, 8192, 1536], P('dp', ('vseq', 'aseq'))
- grad_video_value: bfloat16 [8, 8192, 1536], P('dp', ('vseq', 'aseq'))
- grad_audio_query: bfloat16 [8, 128, 1536], P('dp', 'vseq')
- grad_audio_key: bfloat16 [8, 128, 1536], P('dp', 'vseq')
- grad_audio_value: bfloat16 [8, 128, 1536], P('dp', 'vseq')
- grad_gain_vq: float32 [1536], replicated
- grad_gain_vk: float32 [1536], replicated
- grad_gain_aq: float32 [1536], replicated
- grad_gain_ak: float32 [1536], replicated
All inputs are finite; a program needn't handle non-finite values.
Results may differ from a plain program's by a relative error of at most 0.013.
The roundings to bfloat16 on the way count: a program that leaves them out, or rounds other values in their place, can miss the bound.
Values may be sent and summed in bfloat16 or wider, within the bound.
No kernel may reach another device: no remote copies, remote signals or barrier semaphores. Data moves between devices by JAX's collectives and lax.ppermute only.
A program may use at most 64 MiB of HBM per device.

v0:
```python
import jax
import jax.numpy as jnp
from jax import lax
from jax.sharding import PartitionSpec as P

H = 12
DH = 128


EPS = 1e-06
THETA = 10000.0


def norm_rope(rows, gain, pos):
    count = rows.shape[0]
    heads = rows.astype(jnp.float32).reshape(count, H, DH)
    scaled = heads * lax.rsqrt(jnp.mean(heads * heads, axis=-1, keepdims=True) + EPS)
    scaled = scaled * gain.reshape(H, DH)
    half = DH // 2
    freqs = THETA ** (-jnp.arange(half, dtype=jnp.float32) / half)
    angles = pos.astype(jnp.float32)[:, None] * freqs[None, :]
    cosine = jnp.cos(angles)[:, None, :]
    sine = jnp.sin(angles)[:, None, :]
    first = scaled[:, :, :half]
    second = scaled[:, :, half:]
    turned = jnp.concatenate(
        [first * cosine - second * sine, second * cosine + first * sine], axis=-1
    )
    return turned.reshape(count, H * DH)


def split_heads(rows):
    return rows.reshape(rows.shape[0], H, DH)


def join_heads(rows):
    return rows.reshape(rows.shape[0], H * DH)


def local(
    video_query,
    video_key,
    video_value,
    video_grad,
    audio_query,
    audio_key,
    audio_value,
    audio_grad,
    video_pos,
    audio_pos,
    video_len,
    audio_len,
    gain_vq,
    gain_vk,
    gain_aq,
    gain_ak,
):
    scale = DH ** (-0.5)
    video_rows = video_query.shape[1]
    audio_rows = audio_query.shape[1]
    groups = lax.axis_size("vseq")
    pairs = lax.axis_size("aseq")
    place = lax.axis_index("vseq") * pairs + lax.axis_index("aseq")
    video_mask = (
        place * video_rows + jnp.arange(video_rows, dtype=jnp.int32) < video_len[0]
    ).astype(jnp.float32)
    audio_own = (
        lax.axis_index("vseq") * audio_rows + jnp.arange(audio_rows, dtype=jnp.int32) < audio_len[0]
    ).astype(jnp.float32)
    audio_mask = (jnp.arange(audio_rows * groups, dtype=jnp.int32) < audio_len[0]).astype(
        jnp.float32
    )
    video_cot = video_grad[0] * video_mask.astype(jnp.bfloat16)[:, None]
    audio_cot = audio_grad[0] * audio_own.astype(jnp.bfloat16)[:, None]
    vpos = video_pos[0]
    apos = audio_pos[0]
    normed_vq, back_vq = jax.vjp(
        lambda rows, gain: norm_rope(rows, gain, vpos), video_query[0], gain_vq
    )
    normed_vk, back_vk = jax.vjp(
        lambda rows, gain: norm_rope(rows, gain, vpos), video_key[0], gain_vk
    )
    normed_aq, back_aq = jax.vjp(
        lambda rows, gain: norm_rope(rows, gain, apos), audio_query[0], gain_aq
    )
    normed_ak, back_ak = jax.vjp(
        lambda rows, gain: norm_rope(rows, gain, apos), audio_key[0], gain_ak
    )
    low_vq = normed_vq.astype(jnp.bfloat16)
    low_vk = normed_vk.astype(jnp.bfloat16)
    low_aq = normed_aq.astype(jnp.bfloat16)
    low_ak = normed_ak.astype(jnp.bfloat16)
    own_value = audio_value[0]
    all_q, all_k, all_v, all_c = (
        lax.all_gather(low_aq, "vseq", axis=0, tiled=True),
        lax.all_gather(low_ak, "vseq", axis=0, tiled=True),
        lax.all_gather(own_value, "vseq", axis=0, tiled=True),
        lax.all_gather(audio_cot, "vseq", axis=0, tiled=True),
    )
    heads_vq = split_heads(low_vq)
    heads_ak = split_heads(all_k)
    heads_av = split_heads(all_v)
    heads_vc = split_heads(video_cot)
    scores = (
        jnp.einsum("qhd,khd->hqk", heads_vq, heads_ak, preferred_element_type=jnp.float32) * scale
    )
    expd = jnp.exp(scores) * audio_mask[None, None, :]
    prob = expd / jnp.sum(expd, axis=-1, keepdims=True)
    prob_low = prob.astype(jnp.bfloat16)
    dprob = jnp.einsum("qhd,khd->hqk", heads_vc, heads_av, preferred_element_type=jnp.float32)
    delta = jnp.sum(prob * dprob, axis=-1, keepdims=True)
    dscore = (prob * (dprob - delta)).astype(jnp.bfloat16)
    dq_video = join_heads(
        jnp.einsum("hqk,khd->qhd", dscore, heads_ak, preferred_element_type=jnp.float32) * scale
    )
    dk_audio = join_heads(
        jnp.einsum("hqk,qhd->khd", dscore, heads_vq, preferred_element_type=jnp.float32) * scale
    )
    dv_audio = join_heads(
        jnp.einsum("hqk,qhd->khd", prob_low, heads_vc, preferred_element_type=jnp.float32)
    )
    heads_aq = split_heads(all_q)
    heads_ac = split_heads(all_c)
    heads_vk = split_heads(low_vk)
    heads_vv = split_heads(video_value[0])
    cross = (
        jnp.einsum("qhd,khd->hqk", heads_aq, heads_vk, preferred_element_type=jnp.float32) * scale
    )
    cross_exp = jnp.exp(cross) * video_mask[None, None, :]
    cross_dprob = jnp.einsum("qhd,khd->hqk", heads_ac, heads_vv, preferred_element_type=jnp.float32)
    total = lax.psum(jnp.sum(cross_exp, axis=-1), ("vseq", "aseq"))
    cross_prob = cross_exp / total[:, :, None]
    cross_delta = lax.psum(jnp.sum(cross_prob * cross_dprob, axis=-1), ("vseq", "aseq"))
    cross_dscore = (cross_prob * (cross_dprob - cross_delta[:, :, None])).astype(jnp.bfloat16)
    cross_low = cross_prob.astype(jnp.bfloat16)
    dq_audio = join_heads(
        jnp.einsum("hqk,khd->qhd", cross_dscore, heads_vk, preferred_element_type=jnp.float32)
        * scale
    )
    dk_video = join_heads(
        jnp.einsum("hqk,qhd->khd", cross_dscore, heads_aq, preferred_element_type=jnp.float32)
        * scale
    )
    dv_video = join_heads(
        jnp.einsum("hqk,qhd->khd", cross_low, heads_ac, preferred_element_type=jnp.float32)
    )
    whole_q, whole_k, whole_v = lax.psum((dq_audio, dk_audio, dv_audio), ("vseq", "aseq"))
    begin = lax.axis_index("vseq") * audio_rows
    own_dq = lax.dynamic_slice_in_dim(whole_q, begin, audio_rows, 0)
    own_dk = lax.dynamic_slice_in_dim(whole_k, begin, audio_rows, 0)
    own_dv = lax.dynamic_slice_in_dim(whole_v, begin, audio_rows, 0)
    grad_vq, part_vq = back_vq(dq_video)
    grad_vk, part_vk = back_vk(dk_video)
    grad_aq, part_aq = back_aq(own_dq)
    grad_ak, part_ak = back_ak(own_dk)
    leading = (lax.axis_index("aseq") == 0).astype(jnp.float32)
    sum_vq, sum_vk, sum_aq, sum_ak = lax.psum(
        (part_vq, part_vk, part_aq * leading, part_ak * leading), ("dp", "vseq", "aseq")
    )
    return (
        grad_vq[None],
        grad_vk[None],
        dv_video.astype(jnp.bfloat16)[None],
        grad_aq[None],
        grad_ak[None],
        own_dv.astype(jnp.bfloat16)[None],
        sum_vq,
        sum_vk,
        sum_aq,
        sum_ak,
    )


def solution(mesh):
    in_specs = (
        P("dp", ("vseq", "aseq"), None),
        P("dp", ("vseq", "aseq"), None),
        P("dp", ("vseq", "aseq"), None),
        P("dp", ("vseq", "aseq"), None),
        P("dp", "vseq", None),
        P("dp", "vseq", None),
        P("dp", "vseq", None),
        P("dp", "vseq", None),
        P("dp", ("vseq", "aseq")),
        P("dp", "vseq"),
        P("dp"),
        P("dp"),
        P(),
        P(),
        P(),
        P(),
    )
    out_specs = (
        P("dp", ("vseq", "aseq"), None),
        P("dp", ("vseq", "aseq"), None),
        P("dp", ("vseq", "aseq"), None),
        P("dp", "vseq", None),
        P("dp", "vseq", None),
        P("dp", "vseq", None),
        P(),
        P(),
        P(),
        P(),
    )
    return jax.shard_map(local, mesh=mesh, in_specs=in_specs, out_specs=out_specs, check_vma=False)
```

profile of v0, /device:TPU:1, one launch (start us, length us, event | category | flops | bytes accessed | tf_op | source)
XLA Modules:
  0.0 1476.8 jit_solution(6398816500056792254)
XLA Ops:
  7.2 1.2 copy.88
  16.0 1.0 multiply_cosine_fusion
  17.0 77.0 %all-gather.1 = bf16[32,4,1536]{2,1,0:T(4,128)(2,1)S(1)} all-gather(bf16[1,4,1536]{2,1,0:T(4,128)(2,1)S(1)} %reshape.396), channel_id=1, replica_groups=mesh['dp'=8,'vseq'=32,'aseq'=2] {'vseq'}, dimensions={0}, use_global_device_ids=true | all-gather | bytes 405504 | tf_op jit(solution)/shard_map/all_gather | solution.py:96
  94.6 63.5 %all-gather.2 = bf16[32,4,1536]{2,1,0:T(4,128)(2,1)S(1)} all-gather(bf16[1,4,1536]{2,1,0:T(4,128)(2,1)S(1)} %reshape.398), channel_id=1, replica_groups=mesh['dp'=8,'vseq'=32,'aseq'=2] {'vseq'}, dimensions={0}, use_global_device_ids=true | all-gather | bytes 405504 | tf_op jit(solution)/shard_map/all_gather | solution.py:95
  159.2 66.9 %all-gather.3 = bf16[32,4,1536]{2,1,0:T(4,128)(2,1)S(1)} all-gather(bf16[1,4,1536]{2,1,0:T(4,128)(2,1)S(1)} %fusion.23), channel_id=1, replica_groups=mesh['dp'=8,'vseq'=32,'aseq'=2] {'vseq'}, dimensions={0}, use_global_device_ids=true | all-gather | bytes 405504 | tf_op jit(solution)/shard_map/all_gather | solution.py:98
  226.4 1.1 copy.114
  228.7 66.3 %all-gather = bf16[1,128,1536]{2,0,1:T(2,128)(2,1)S(1)} all-gather(bf16[1,4,1536]{2,0,1:T(2,128)(2,1)} %copy.92), channel_id=2, replica_groups=mesh['dp'=8,'vseq'=32,'aseq'=2] {'vseq'}, dimensions={1}, use_global_device_ids=true | all-gather | bytes 405504 | tf_op jit(solution)/shard_map/all_gather | solution.py:97
  295.1 1.7 copy.93
  297.8 2.2 fusion.16
  302.2 1.4 fusion.6
  303.7 2.8 fusion.10
  306.5 2.3 copy.127
  308.8 3.4 multiply_reduce_fusion.6
  312.1 1.5 multiply_convert_fusion.1
  314.4 1.3 fusion.1
  315.7 2.3 copy.124
  318.6 1.9 fusion.40
  320.5 197.8 %psum.63 = f32[12,128]{1,0:T(8,128)} all-reduce(f32[12,128]{1,0:T(8,128)} %get-tuple-element.90), channel_id=1, replica_groups=mesh['dp'=8,'vseq'=32,'aseq'=2] {'vseq','aseq'}, use_global_device_ids=true, to_apply=%region_8.0 | all-reduce | flops 1536 | bytes 12288 | tf_op jit(solution)/shard_map/psum | solution.py:131
  518.3 3.0 multiply_reduce_fusion.3
  521.3 279.0 %all-reduce.15 = (f32[12,128]{1,0:T(8,128)}, bf16[128,1536]{1,0:T(8,128)(2,1)}) all-reduce(f32[12,128]{1,0:T(8,128)} %get-tuple-element.92, f32[128,1536]{1,0:T(8,128)} %copy.127), channel_id=1, replica_groups=mesh['dp'=8,'vseq'=32,'aseq'=2] {'vseq','aseq'}, use_global_device_ids=true, to_apply=%region_10.0 | all-reduce | flops 198144 | bytes 1191936 | tf_op jit(solution)/shard_map/psum | solution.py:133
  800.4 1.5 multiply_convert_fusion
  801.9 1.3 fusion.2
  803.2 2.3 copy.119
  805.5 1.0 copy-done.5
  807.8 1.7 multiply_add_fusion.1
  809.9 0.9 copy.130
  810.9 2.8 multiply_reduce_fusion
  817.9 0.9 copy.128
  818.8 1.3 fusion.22
  820.2 543.7 %all-reduce.14.cloned.1.call-done = (f32[128,1536]{0,1:T(8,128)}, f32[128,1536]{0,1:T(8,128)}) async-done(((f32[128,1536]{0,1:T(8,128)}, f32[128,1536]{0,1:T(8,128)}), (f32[128,1536]{0,1:T(8,128)}, f32[128,1536]{0,1:T(8,128)})) %all-reduce.14.cloned.1.call-update) | async-done | bytes 1572880 | tf_op jit(solution)/shard_map/psum | solution.py:147
  1363.9 1.4 constant_dynamic-slice_fusion.1
  1371.3 98.7 %all-reduce.8 = (f32[1536]{0:T(1024)}, f32[1536]{0:T(1024)}, f32[1536]{0:T(1024)}, f32[1536]{0:T(1024)}) all-reduce(f32[1536]{0:T(1024)S(1)} %bitcast.97, f32[1536]{0:T(1024)S(1)} %bitcast.96, f32[1536]{0:T(1024)S(1)} %multiply_bitcast_fusion.1, ...), channel_id=1, replica_groups=mesh['dp'=8,'vseq'=32,'aseq'=2] {'dp','vseq','aseq'}, use_global_device_ids=true, to_apply=%region_18.0 | all-reduce | flops 6144 | bytes 49152 | tf_op jit(solution)/shard_map/psum | solution.py:157
  (181 shorter events, 25.7 us)
Async XLA Ops:
  7.2 1356.7 %all-reduce.14.cloned.1.call-start = ((), (), s32[]{:S(2)}) async-start(), calls=%async_computation | async-start | bytes 3145728 | tf_op jit(solution)/shard_map/psum | solution.py:147
  8.6 218.9 %copy-start.26 = (f32[128,12]{0,1:T(8,128)}, f32[128,12]{0,1:T(8,128)S(1)}, u32[]{:S(2)}) copy-start(f32[128,12]{0,1:T(8,128)S(1)} %multiply_reduce_fusion.7) | copy-start | bytes 18436
  8.6 1.0 copy-start.19
  9.9 217.6 %copy-start.28 = (f32[128,12]{0,1:T(8,128)}, f32[128,12]{0,1:T(8,128)S(1)}, u32[]{:S(2)}) copy-start(f32[128,12]{0,1:T(8,128)S(1)} %multiply_reduce_fusion.4) | copy-start | bytes 18436
  10.1 2.6 copy-start.49
  13.5 1.6 copy-start.8
  14.2 0.9 copy-start.36
  14.2 1.5 copy-start.10
  14.2 1.3 copy-start.32
  226.4 1.2 copy-start.20
  227.5 1.0 copy-start.21
  228.7 68.5 %copy-start.7 = (bf16[1,128,1536]{1,2,0:T(8,128)(2,1)}, bf16[1,128,1536]{1,2,0:T(8,128)(2,1)S(1)}, u32[]{:S(2)}) copy-start(bf16[1,128,1536]{1,2,0:T(8,128)(2,1)S(1)} %copy.91) | copy-start | bytes 1179652
  297.8 2.2 copy-start.22
  297.8 2.2 copy-start.24
  300.0 0.8 copy-start.13
  300.0 0.9 copy-start.15
  301.5 0.8 copy-start.2
  312.1 2.3 copy-start.3
  318.6 199.7 %copy-start.17 = (bf16[128,12,128]{0,2,1:T(8,128)(2,1)S(1)}, bf16[128,12,128]{0,2,1:T(8,128)(2,1)}, u32[]{:S(2)}) copy-start(bf16[128,12,128]{0,2,1:T(8,128)(2,1)} %copy.114) | copy-start | bytes 1179652
  805.5 1.0 copy-start.5
  806.9 0.8 copy-start.14
  806.9 0.9 copy-start.16
  807.8 1.7 copy-start.6
  807.8 1.7 copy-start.18
  807.8 1.7 copy-start.34
  810.9 2.8 copy-start.29
  810.9 2.8 copy-start
  810.9 2.8 copy-start.1
  815.3 0.9 copy-start.25
  1365.3 1.1 copy-start.12
  1367.9 0.9 copy-start.47
  1368.8 1.6 copy-start.45
  (26 other events, 17.8 us)
Sparse Core Ops, SparseCore 0:
  805.6 558.1 all-reduce.13
where the time goes:
time: 1480 us
  blocking collectives  849 us (57%)
  waiting for transfers between devices  544 us (37%)
  local copies, waits for them, and re-layouts  35.2 us (2%)
  matrix products  18.5 us (1%)
  between operations  16 us (1%)
    psum x1, waiting for transfers between devices, local(): lax.psum((dq_audio, dk_audio, dv_audio), ('vseq', 'aseq'))  544 us
    psum x1, blocking collectives, local(): lax.psum(jnp.sum(cross_prob * cross_dprob, axis=-1), ('vseq', 'aseq'))  279 us
    psum x1, blocking collectives, local(): total = lax.psum(jnp.sum(cross_exp, axis=-1), ('vseq', 'aseq'))  198 us
    psum x1, blocking collectives, local(): lax.psum((part_vq, part_vk, part_aq * leading, part_ak * leading), ('dp',...  98.7 us
    all_gather x1, blocking collectives, local(): lax.all_gather(low_ak, 'vseq', axis=0, tiled=True)  77 us
    all_gather x1, blocking collectives, local(): lax.all_gather(audio_cot, 'vseq', axis=0, tiled=True)  66.9 us
    all_gather x1, blocking collectives, local(): lax.all_gather(own_value, 'vseq', axis=0, tiled=True)  66.3 us
    all_gather x1, blocking collectives, local(): lax.all_gather(low_aq, 'vseq', axis=0, tiled=True)  63.5 us
  transfers between devices with their start and end apart: 1, of which 1 were waited for; matrix products, arithmetic and copies ran while one was open for 1% of the time, Pallas kernels for 0%

commit v1 on v0

v1 whole, which is shorter than its diff:
```python
import functools

import jax
import jax.numpy as jnp
import numpy as np
from jax import lax
from jax.experimental import pallas as pl
from jax.experimental.pallas import tpu as pltpu
from jax.sharding import PartitionSpec as P

H = 12
DH = 128
HALF = DH // 2
EPS = 1e-06
THETA = 10000.0
SCALE = DH ** (-0.5)
BF = jnp.bfloat16
F32 = jnp.float32
VMEM_LIMIT = 48 * 1024 * 1024


def frequencies():
    freqs = np.power(np.float64(THETA), -(np.arange(HALF, dtype=np.float64) / HALF))
    return jnp.asarray(np.tile(freqs.astype(np.float32), 2).reshape(1, DH))


def sin_cos(angles):
    turns = jnp.floor(angles * F32(2.0 / np.pi) + 0.5)
    rest = angles - turns * F32(1.5703125)
    rest = rest - turns * F32(4.837512969970703125e-4)
    rest = rest - turns * F32(7.54978995489188216e-8)
    sq = rest * rest
    sine = rest + rest * sq * (
        F32(-1.6666654611e-1) + sq * (F32(8.3321608736e-3) + sq * F32(-1.9515295891e-4))
    )
    cosine = (
        1.0
        - 0.5 * sq
        + sq * sq * (F32(4.166664568298827e-2) + sq * (F32(-1.388731625493765e-3) + sq * F32(2.443315711809948e-5)))
    )
    quarter = turns.astype(jnp.int32)
    odd = (quarter & 1) == 1
    flip = (quarter & 2) == 2
    base_s = jnp.where(odd, cosine, sine)
    base_c = jnp.where(odd, -sine, cosine)
    return jnp.where(flip, -base_s, base_s), jnp.where(flip, -base_c, base_c)


def rotary_tables(pos, freqs):
    sine, cosine = sin_cos(pos * freqs)
    lane = lax.broadcasted_iota(jnp.int32, sine.shape, 1)
    return cosine, jnp.where(lane < HALF, -sine, sine)


def swap(rows):
    return pltpu.roll(rows, HALF, 1)


def unit(rows):
    scale = lax.rsqrt(jnp.sum(rows * rows, axis=-1, keepdims=True) * (1.0 / DH) + EPS)
    return rows * scale, scale


def turn(unit_rows, gain, cosine, sine):
    scaled = unit_rows * gain
    return (scaled * cosine + swap(scaled) * sine).astype(BF)


def turn_back(grad, cosine, sine):
    return grad * cosine - swap(grad) * sine


def norm_back(scaled_grad, unit_rows, scale, gain):
    inner = scaled_grad * gain
    mean = jnp.sum(inner * unit_rows, axis=-1, keepdims=True) * (1.0 / DH)
    return scale * (inner - unit_rows * mean)


def low_rows(shape):
    return (lax.broadcasted_iota(jnp.int32, shape, 0) & 7) < 4


def part_rows(both):
    left, right = both[:DH], both[DH:]
    low = low_rows(left.shape)
    one = jnp.where(low, left, pltpu.roll(right, 4, 0))
    two = jnp.where(low, pltpu.roll(left, DH - 4, 0), right)
    return one, two


def join_rows(one, two):
    low = low_rows(one.shape)
    left = jnp.where(low, one, pltpu.roll(two, 4, 0))
    right = jnp.where(low, pltpu.roll(one, DH - 4, 0), two)
    return left, right


def audio_index():
    row = lax.broadcasted_iota(jnp.int32, (DH, DH), 0)
    inside = row & 7
    return jnp.where(inside < 4, 0, 60) + (row >> 3) * 4 + inside


def dot_nt(a, b):
    return lax.dot_general(a, b, (((1,), (1,)), ((), ())), preferred_element_type=F32)


def dot_tn(a, b):
    return lax.dot_general(a, b, (((0,), (0,)), ((), ())), preferred_element_type=F32)


def dot_nn(a, b):
    return lax.dot_general(a, b, (((1,), (0,)), ((), ())), preferred_element_type=F32)


def lanes(head):
    return pl.ds(pl.multiple_of(head * DH, DH), DH)


def first_kernel(
    vlen, alen, own, other, vq, vk, vv, vc, vpos, freqs, gains,
    grad_vq, sums, expo, dprob, raw_aq, low_ac, tables, part_own, part_other,
):
    core = lax.axis_index("aseq")
    place = lax.axis_index("vseq") * 2 + core
    front = core == 0

    def gathered(columns):
        mine, others = own[:, columns], other[:, columns]
        qk = jnp.where(front, mine, others).astype(F32)
        vc = jnp.where(front, others, mine).astype(F32)
        return qk, vc

    row = lax.broadcasted_iota(jnp.int32, (DH, DH), 0)
    lane = lax.broadcasted_iota(jnp.int32, (DH, DH), 1)
    apos, _ = part_rows(own[:, H * DH :].astype(F32))
    apos = jnp.where(lane < HALF, apos * 64.0, apos)
    apos = apos + swap(apos)
    pos = jnp.transpose(jnp.broadcast_to(vpos[...].astype(F32), (DH, DH)))
    tables[0], tables[1] = rotary_tables(pos, freqs[...])
    tables[2], tables[3] = rotary_tables(apos, freqs[...])
    tables[4] = (row + place * DH < vlen[0]).astype(F32)
    tables[5] = (audio_index() < alen[0]).astype(F32)
    sums[...] = jnp.zeros(sums.shape, F32)

    def one_head(head):
        columns = lanes(head)
        cos_v, sin_v, cos_a, sin_a = tables[0], tables[1], tables[2], tables[3]
        mask_v, mask_a = tables[4], tables[5]
        gain_vq, gain_vk = gains[pl.ds(head, 1), :], gains[pl.ds(H + head, 1), :]
        gain_aq, gain_ak = gains[pl.ds(2 * H + head, 1), :], gains[pl.ds(3 * H + head, 1), :]
        qk, vc_audio = gathered(columns)
        aq, ak = part_rows(qk)
        av, ac = part_rows(vc_audio)
        av = av.astype(BF)
        ac = (ac * mask_a).astype(BF)
        raw_aq[:, columns] = aq.astype(BF)
        low_ac[:, columns] = ac
        unit_ak, _ = unit(ak)
        low_ak = turn(unit_ak, gain_ak, cos_a, sin_a)
        unit_aq, _ = unit(aq)
        low_aq = turn(unit_aq, gain_aq, cos_a, sin_a)
        unit_vk, _ = unit(vk[:, columns].astype(F32))
        low_vk = turn(unit_vk, gain_vk, cos_v, sin_v)
        cross = jnp.exp(dot_nt(low_vk, low_aq) * SCALE) * mask_v
        cross_dprob = dot_nt(vv[:, columns], ac)
        expo[head] = cross
        dprob[head] = cross_dprob
        sums[pl.ds(head, 1), :] = jnp.sum(cross, axis=0, keepdims=True)
        sums[pl.ds(H + head, 1), :] = jnp.sum(cross * cross_dprob, axis=0, keepdims=True)
        unit_vq, scale_vq = unit(vq[:, columns].astype(F32))
        low_vq = turn(unit_vq, gain_vq, cos_v, sin_v)
        cot = (vc[:, columns].astype(F32) * mask_v).astype(BF)
        expd = jnp.exp(dot_nt(low_ak, low_vq) * SCALE) * mask_a
        prob = expd * (1.0 / jnp.sum(expd, axis=0, keepdims=True))
        dp = dot_nt(av, cot)
        delta = jnp.sum(prob * dp, axis=0, keepdims=True)
        dscore = (prob * (dp - delta)).astype(BF)
        dq = dot_tn(dscore, low_ak) * SCALE
        dk = dot_nn(dscore, low_vq) * SCALE
        dv = dot_nn(prob.astype(BF), cot)
        back = turn_back(dq, cos_v, sin_v)
        grad_vq[:, columns] = norm_back(back, unit_vq, scale_vq, gain_vq).astype(BF)
        sum_vq = jnp.sum(back * unit_vq, axis=0, keepdims=True)
        sum_ak = jnp.sum(turn_back(dk, cos_a, sin_a) * unit_ak, axis=0, keepdims=True)
        return dk, dv, sum_vq, sum_ak

    for half, part in enumerate((part_own, part_other)):
        base = lax.rem(core + half, 2) * (H // 2)
        part[32] = jnp.zeros(part.shape[1:], F32)

        def pair(step, carry, base=base, part=part):
            found = [one_head(base + 2 * step + e) for e in range(2)]
            for array in range(2):
                left, right = join_rows(found[0][array], found[1][array])
                rows = pl.ds(pl.multiple_of((array * 3 + step) * 8, 8), 8)
                part[0:16, rows, :] = left.reshape(16, 8, DH)
                part[16:32, rows, :] = right.reshape(16, 8, DH)
            for e in range(2):
                part[32, pl.ds(2 * step + e, 1), :] = found[e][2]
                part[32, pl.ds(6 + 2 * step + e, 1), :] = found[e][3]
            return carry

        lax.fori_loop(0, 3, pair, 0)


def second_kernel(
    totals, vk, expo, dprob, raw_aq, low_ac, tables, gains,
    grad_vk, grad_vv, part_own, part_other, sums, deltas,
):
    core = lax.axis_index("aseq")
    whole = jnp.sum(totals[...], axis=0)
    sums[...] = whole
    deltas[...] = 1.0 / whole

    def one_head(head):
        columns = lanes(head)
        cos_v, sin_v, cos_a, sin_a = tables[0], tables[1], tables[2], tables[3]
        gain_vk, gain_aq = gains[pl.ds(H + head, 1), :], gains[pl.ds(2 * H + head, 1), :]
        inverse = deltas[pl.ds(head, 1), :]
        delta = sums[pl.ds(H + head, 1), :] * inverse
        prob = expo[head] * inverse
        dscore = (prob * (dprob[head] - delta)).astype(BF)
        unit_aq, _ = unit(raw_aq[:, columns].astype(F32))
        low_aq = turn(unit_aq, gain_aq, cos_a, sin_a)
        unit_vk, scale_vk = unit(vk[:, columns].astype(F32))
        low_vk = turn(unit_vk, gain_vk, cos_v, sin_v)
        dq = dot_tn(dscore, low_vk) * SCALE
        dk = dot_nn(dscore, low_aq) * SCALE
        grad_vv[:, columns] = dot_nn(prob.astype(BF), low_ac[:, columns]).astype(BF)
        back = turn_back(dk, cos_v, sin_v)
        grad_vk[:, columns] = norm_back(back, unit_vk, scale_vk, gain_vk).astype(BF)
        sum_vk = jnp.sum(back * unit_vk, axis=0, keepdims=True)
        sum_aq = jnp.sum(turn_back(dq, cos_a, sin_a) * unit_aq, axis=0, keepdims=True)
        return dq, sum_vk, sum_aq

    for half, part in enumerate((part_own, part_other)):
        base = lax.rem(core + half, 2) * (H // 2)
        part[32] = jnp.zeros(part.shape[1:], F32)

        def pair(step, carry, base=base, part=part):
            found = [one_head(base + 2 * step + e) for e in range(2)]
            left, right = join_rows(found[0][0], found[1][0])
            rows = pl.ds(pl.multiple_of(step * 8, 8), 8)
            part[0:16, rows, :] = left.reshape(16, 8, DH)
            part[16:32, rows, :] = right.reshape(16, 8, DH)
            for e in range(2):
                part[32, pl.ds(12 + 2 * step + e, 1), :] = found[e][1]
                part[32, pl.ds(18 + 2 * step + e, 1), :] = found[e][2]
            return carry

        lax.fori_loop(0, 3, pair, 0)


def merge_kernel(first, first_got, second, second_got, out):
    gain_rows = first[32, 0:24, :] + first_got[32, 0:24, :] + second[32, 0:24, :] + second_got[32, 0:24, :]

    def block(v, carry):
        out[v, 0:48, :] = (first[v] + first_got[v]).astype(BF)
        tail = jnp.concatenate([second[v] + second_got[v], gain_rows], axis=0)
        out[v, 48:96, :] = tail.astype(BF)
        return carry

    lax.fori_loop(0, 32, block, 0, unroll=4)


def third_kernel(apos, got, aq, ak, freqs, gains, out, gain_out):
    core = lax.axis_index("aseq")
    acc = got[0].astype(F32)
    for v in range(1, 32):
        acc = acc + got[v].astype(F32)
    gain_out[...] = acc[72:96]
    inside = lax.broadcasted_iota(jnp.int32, (8, DH), 0) & 3
    pos = jnp.where(inside < 2, jnp.where(inside == 0, apos[0, 0], apos[0, 1]), jnp.where(inside == 2, apos[0, 2], apos[0, 3]))
    cosine, sine = rotary_tables(pos.astype(F32), freqs[...])
    low = low_rows((8, DH))

    def rows_back(ref, gain_at, grad, at):
        first = core * (H // 2) + 2 * at
        rows = jnp.concatenate([ref[:, lanes(first)].astype(F32), ref[:, lanes(first + 1)].astype(F32)], axis=0)
        gain = jnp.where(low, gains[pl.ds(gain_at * H + first, 1), :], gains[pl.ds(gain_at * H + first + 1, 1), :])
        unit_rows, scale = unit(rows)
        return norm_back(turn_back(grad, cosine, sine), unit_rows, scale, gain)

    for at in range(3):
        dk, dv, dq = (acc[8 * (3 * array + at) : 8 * (3 * array + at) + 8] for array in range(3))
        dq = rows_back(aq, 2, dq, at)
        dk = rows_back(ak, 3, dk, at)
        left = jnp.where(low, dq, pltpu.roll(dk, 4, 0))
        right = jnp.where(low, pltpu.roll(dq, 4, 0), dk)
        out[:, 2 * at * DH : (2 * at + 1) * DH] = jnp.concatenate([left, dv], axis=0).astype(BF)
        out[:, (2 * at + 1) * DH : (2 * at + 2) * DH] = jnp.concatenate([right, pltpu.roll(dv, 4, 0)], axis=0).astype(BF)


def last_kernel(own, other, gains, grad_aq, grad_ak, grad_av, sum_vq, sum_vk, sum_aq, sum_ak):
    front = lax.axis_index("aseq") == 0
    mine, others = own[...].astype(F32), other[...].astype(F32)
    width = mine.shape[1]
    for at, value in enumerate((jnp.where(front, mine, others), jnp.where(front, others, mine))):
        columns = slice(at * width, (at + 1) * width)
        grad_aq[:, columns] = value[0:4].astype(BF)
        grad_ak[:, columns] = value[4:8].astype(BF)
        grad_av[:, columns] = value[8:12].astype(BF)
    for half in range(2):
        total = gains[half]
        for d in range(1, gains.shape[0] // 2):
            total = total + gains[2 * d + half]
        for at, ref in enumerate((sum_vq, sum_ak, sum_vk, sum_aq)):
            ref[6 * half : 6 * half + 6, :] = total[6 * at : 6 * at + 6]


def call(kernel, name, outs, ins, smem=0, scratch=()):
    return pl.pallas_call(
        kernel,
        name=name,
        out_shape=[jax.ShapeDtypeStruct(shape, dtype) for shape, dtype in outs],
        in_specs=[pl.BlockSpec(memory_space=pltpu.SMEM)] * smem
        + [pl.BlockSpec(memory_space=pltpu.VMEM)] * (len(ins) - smem),
        out_specs=[pl.BlockSpec(memory_space=pltpu.VMEM)] * len(outs),
        scratch_shapes=list(scratch),
        compiler_params=pltpu.CompilerParams(vmem_limit_bytes=VMEM_LIMIT),
    )(*ins)


def to_all(rows, axes, count):
    spread = jnp.broadcast_to(rows[None], (count,) + rows.shape)
    return lax.all_to_all(spread, axes, 0, 0, tiled=True)


def local(
    video_query, video_key, video_value, video_grad,
    audio_query, audio_key, audio_value, audio_grad,
    video_pos, audio_pos, video_len, audio_len,
    gain_vq, gain_vk, gain_aq, gain_ak,
):
    F = H * DH
    core = lax.axis_index("aseq")
    groups = lax.axis_size("vseq")
    clips = lax.axis_size("dp")
    exchange = functools.partial(lax.ppermute, axis_name="aseq", perm=[(0, 1), (1, 0)])
    freqs = frequencies()
    gains = jnp.concatenate([gain_vq, gain_vk, gain_aq, gain_ak]).reshape(4 * H, DH)
    mine = jnp.where(
        core == 0,
        jnp.concatenate([audio_query[0], audio_key[0]], axis=0),
        jnp.concatenate([audio_value[0], audio_grad[0]], axis=0),
    )
    places = jnp.tile(audio_pos[0], 2)[:, None]
    lane = jnp.arange(DH, dtype=jnp.int32)[None, :]
    places = jnp.where(lane < HALF, places >> 6, places & 63).astype(BF)
    payload = jnp.concatenate([mine, places], axis=1)
    own = to_all(payload, "vseq", groups).reshape(groups * 8, F + DH)
    other = exchange(own)

    block = (DH, F)
    square = (H, DH, DH)
    grad_vq, sums, expo, dprob, raw_aq, low_ac, tables, first, first_send = call(
        first_kernel,
        "first",
        [
            (block, BF), ((2 * H, DH), F32), (square, F32), (square, F32), (block, BF), (block, BF),
            ((6, DH, DH), F32), ((groups + 1, 48, DH), F32), ((groups + 1, 48, DH), F32),
        ],
        [
            video_len, audio_len, own, other, video_query[0], video_key[0], video_value[0], video_grad[0],
            video_pos, freqs, gains,
        ],
        smem=2,
    )
    sums = sums + exchange(sums)
    first_got = exchange(first_send)
    totals = to_all(sums, "vseq", groups)
    grad_vk, grad_vv, second, second_send = call(
        second_kernel,
        "second",
        [(block, BF), (block, BF), ((groups + 1, 24, DH), F32), ((groups + 1, 24, DH), F32)],
        [totals, video_key[0], expo, dprob, raw_aq, low_ac, tables, gains],
        scratch=[pltpu.VMEM((2 * H, DH), F32), pltpu.VMEM((2 * H, DH), F32)],
    )
    second_got = exchange(second_send)
    (merged,) = call(
        merge_kernel, "merge", [((groups, 96, DH), BF)], [first, first_got, second, second_got]
    )
    got = lax.all_to_all(merged, "vseq", 0, 0, tiled=True)
    half, gain_sums = call(
        third_kernel,
        "third",
        [((16, F // 2), BF), ((2 * H, DH), F32)],
        [audio_pos, got, audio_query[0], audio_key[0], freqs, gains],
        smem=1,
    )
    half_got = exchange(half)
    gain_got = to_all(gain_sums, ("dp", "aseq"), 2 * clips)
    grad_aq, grad_ak, grad_av, sum_vq, sum_vk, sum_aq, sum_ak = call(
        last_kernel,
        "last",
        [((4, F), BF)] * 3 + [((H, DH), F32)] * 4,
        [half, half_got, gain_got],
    )
    return (
        grad_vq[None],
        grad_vk[None],
        grad_vv[None],
        grad_aq[None],
        grad_ak[None],
        grad_av[None],
        sum_vq.reshape(F),
        sum_vk.reshape(F),
        sum_aq.reshape(F),
        sum_ak.reshape(F),
    )


def solution(mesh):
    video = P("dp", ("vseq", "aseq"), None)
    audio = P("dp", "vseq", None)
    in_specs = (
        (video,) * 4
        + (audio,) * 4
        + (P("dp", ("vseq", "aseq")), P("dp", "vseq"), P("dp"), P("dp"))
        + (P(),) * 4
    )
    out_specs = (video,) * 3 + (audio,) * 3 + (P(),) * 4
    return jax.shard_map(local, mesh=mesh, in_specs=in_specs, out_specs=out_specs, check_vma=False)
```

time: 1480 us -> 153 us (0.10)
  blocking collectives: 849 us -> 74.7 us
  waiting for transfers between devices: 544 us -> 19 us
  starting transfers between devices: 0.04 us -> 27.6 us
  local copies, waits for them, and re-layouts: 35.2 us -> 10.4 us
  matrix products: 18.5 us -> 0 us
  Pallas kernels: 0 us -> 17.5 us
    psum x3 -> x0, blocking collectives: 576 us -> none  [the longest x1 279 us: local(): lax.psum(jnp.sum(cross_prob * cross_dprob, axis=-1), ('vseq', 'aseq'))]
    psum x1 -> x0, waiting for transfers between devices: 544 us -> none  [local(): lax.psum((dq_audio, dk_audio, dv_audio), ('vseq', 'aseq'))]
    all_gather x4 -> x0, blocking collectives: 274 us -> none  [the longest x1 77 us: local(): lax.all_gather(low_ak, 'vseq', axis=0, tiled=True)]
    all_to_all x0 -> x2, blocking collectives: none -> 74.7 us  [the longest x1 42 us: to_all(): return lax.all_to_all(spread, axes, 0, 0, tiled=True)]
    pallas_call x0 -> x5, Pallas kernels: none -> 17.5 us  [call(): pl.pallas_call(kernel, name=name, out_shape=[jax.ShapeDtypeStruct(shape,...]
    ppermute x0 -> x5, starting transfers between devices: none -> 15.8 us  [the longest x1 4.9 us: local(): other = exchange(own)]
    dot_general x10 -> x0, matrix products: 15.2 us -> none  [the longest x1 3.03 us: local(): jnp.einsum('qhd,khd->hqk', heads_ac, heads_vv, preferred_element_type=jnp...]
    all_to_all x0 -> x2, waiting for transfers between devices: none -> 15.2 us  [to_all(): return lax.all_to_all(spread, axes, 0, 0, tiled=True)]
  transfers between devices with their start and end apart: 1 -> 7, of which waited for: 1 -> 6; matrix products, arithmetic and copies ran while one was open for 1% -> 0% of each run, Pallas kernels for 0% -> 3%
where the time goes in v1:
time: 153 us; the launch traced here: 152 us
  blocking collectives  74.7 us (49%)
  starting transfers between devices  27.6 us (18%)
  waiting for transfers between devices  19 us (12%)
  Pallas kernels  17.5 us (11%)
  local copies, waits for them, and re-layouts  10.4 us (7%)
  between operations  2.17 us (1%)
    all_to_all x1, blocking collectives, to_all(): return lax.all_to_all(spread, axes, 0, 0, tiled=True)  42 us
    all_to_all x1, blocking collectives, local(): got = lax.all_to_all(merged, 'vseq', 0, 0, tiled=True)  32.7 us
    pallas_call x5, Pallas kernels, call(): pl.pallas_call(kernel, name=name, out_shape=[jax.ShapeDtypeStruct(shape,...  17.5 us
    all_to_all x2, waiting for transfers between devices, to_all(): return lax.all_to_all(spread, axes, 0, 0, tiled=True)  15.2 us
    all_to_all x2, starting transfers between devices, to_all(): return lax.all_to_all(spread, axes, 0, 0, tiled=True)  11.8 us
    unnamed x48, local copies, waits for them, and re-layouts  8.75 us
    ppermute x1, starting transfers between devices, local(): other = exchange(own)  4.9 us
    ppermute x1, starting transfers between devices, local(): second_got = exchange(second_send)  4.11 us
  transfers between devices with their start and end apart: 7, of which 6 were waited for; matrix products, arithmetic and copies ran while one was open for 0% of the time, Pallas kernels for 3%

profile of v1, /device:TPU:1, one launch (start us, length us, event | category | flops | bytes accessed | tf_op | source)
XLA Modules:
  0.0 152.3 jit_solution(12755890743796012238)
XLA Ops:
  0.7 0.6 copy-done.15
  1.6 0.5 copy-done.12
  2.0 0.8 maximum_select_fusion
  3.0 42.0 %all_to_all.20 = bf16[32,8,1664]{2,1,0:T(8,128)(2,1)S(1)} all-to-all(bf16[32,8,1664]{2,1,0:T(8,128)(2,1)S(1)} %broadcast_in_dim.64), channel_id=1, replica_groups=mesh['dp'=8,'vseq'=32,'aseq'=2] {'vseq'}, dimensions={0} | all-to-all | bytes 1703936 | tf_op jit(solution)/shard_map/all_to_all | solution.py:327
  45.0 4.9 %collective-permute-start = (bf16[256,1664]{1,0:T(8,128)(2,1)S(1)}, bf16[256,1664]{1,0:T(8,128)(2,1)S(1)}, u32[]{:S(2)}, u32[]{:S(2)}) collective-permute-start(bf16[256,1664]{1,0:T(8,128)(2,1)S(1)} %bitcast.36), channel_id=1, source_target_pairs={{0,1},{1,0},{2,3},{3,2},{4,5},{5,4},{6,7},{7,6},{8,9},{9,8},{10,11... | collective-permute-start | bytes 2555912 | tf_op jit(solution)/shard_map/ppermute | solution.py:353
  51.3 0.6 collective-permute-done.other
  51.9 0.9 copy-done.19
  52.8 10.8 %first.1 = (bf16[128,1536]{1,0:T(8,128)(2,1)}, f32[24,128]{1,0:T(8,128)S(1)}, f32[12,128,128]{2,1,0:T(8,128)S(1)}, f32[12,128,128]{2,1,0:T(8,128)S(1)}, bf16[128...) custom-call(s32[1]{0:T(128)S(6)} %copy.27.vlen, ...), custom_call_target="tpu_custom_call" | custom-call | tf_op jit(solution)/shard_map/first/pallas_call | solution.py:313
  63.6 0.9 copy-done.1
  64.6 0.7 copy-done.3
  65.3 0.9 copy-done.17
  66.2 2.3 %collective-permute-start.1 = (f32[24,128]{1,0:T(8,128)S(1)}, f32[24,128]{1,0:T(8,128)S(1)}, u32[]{:S(2)}, u32[]{:S(2)}) collective-permute-start(f32[24,128]{1,0:T(8,128)S(1)} %get-tuple-element.33), channel_id=1, source_target_pairs={{0,1},{1,0},{2,3},{3,2},{4,5},{5,4},{6,7},{7,6},{8,9},{9,8},{10,11... | collective-permute-start | bytes 36872 | tf_op jit(solution)/shard_map/ppermute | solution.py:370
  68.5 0.8 collective-permute-done.1
  69.3 0.8 broadcast_in_dim.66
  70.1 6.4 %all-to-all-start.1 = ((f32[32,24,128]{2,1,0:T(8,128)}), f32[32,24,128]{2,1,0:T(8,128)S(1)}, u32[]{:S(2)}, u32[]{:S(2)}) async-start(f32[32,24,128]{2,1,0:T(8,128)} %broadcast_in_dim.66), calls=%async_computation.1 | async-start | bytes 786432 | tf_op jit(solution)/shard_map/all_to_all | solution.py:327
  76.5 2.5 %collective-permute-start.2 = (f32[33,48,128]{2,1,0:T(8,128)}, f32[33,48,128]{2,1,0:T(8,128)S(1)}, u32[]{:S(2)}, u32[]{:S(2)}) collective-permute-start(f32[33,48,128]{2,1,0:T(8,128)} %copy-done.17), channel_id=1, source_target_pairs={{0,1},{1,0},{2,3},{3,2},{4,5},{5,4},{6,7},{7,6},{8,9},{9,8},{10,11... | collective-permute-start | bytes 2433032 | tf_op jit(solution)/shard_map/ppermute | solution.py:371
  79.1 11.6 %all-to-all-done.1.totals = f32[32,24,128]{2,1,0:T(8,128)S(1)} async-done(((f32[32,24,128]{2,1,0:T(8,128)}), f32[32,24,128]{2,1,0:T(8,128)S(1)}, u32[]{:S(2)}, u32[]{:S(2)}) %all-to-all-start.1) | async-done | bytes 393248 | tf_op jit(solution)/shard_map/all_to_all | solution.py:327
  90.7 1.1 copy-done.2
  91.8 1.0 copy-done.4
  92.8 1.0 copy-done.6
  93.8 1.0 copy-done.8
  94.8 5.1 %second.1 = (bf16[128,1536]{1,0:T(8,128)(2,1)}, bf16[128,1536]{1,0:T(8,128)(2,1)}, f32[33,24,128]{2,1,0:T(8,128)S(1)}, f32[33,24,128]{2,1,0:T(8,128)S(1)}) custom-call(f32[32,24,128]{2,1,0:T(8,128)S(1)} %all-to-all-done.1.totals, bf16[128,1536]{1,0:T(8,128)(2,1)S(1)} %bitcast.28, f32[12,128,128]{2,1,0:T(8,128)S(1)} %get-tuple-element.34.expo, ...), custom_call_target="tpu_custom_call" | custom-call | tf_op jit(solution)/shard_map/second/pallas_call | solution.py:313
  99.9 4.1 %collective-permute-start.3 = (f32[33,24,128]{2,1,0:T(8,128)S(1)}, f32[33,24,128]{2,1,0:T(8,128)S(1)}, u32[]{:S(2)}, u32[]{:S(2)}) collective-permute-start(f32[33,24,128]{2,1,0:T(8,128)S(1)} %get-tuple-element.44), channel_id=1, source_target_pairs={{0,1},{1,0},{2,3},{3,2},{4,5},{5,4},{6,7},{7,6},{8,9},{9,8},{10,11... | collective-permute-start | bytes 1216520 | tf_op jit(solution)/shard_map/ppermute | solution.py:380
  104.0 1.3 collective-permute-done.3.second_got
  105.5 32.7 %all_to_all.21.got = bf16[32,96,128]{2,1,0:T(8,128)(2,1)S(1)} all-to-all(bf16[32,96,128]{2,1,0:T(8,128)(2,1)S(1)} %merge.1), channel_id=1, replica_groups=mesh['dp'=8,'vseq'=32,'aseq'=2] {'vseq'}, dimensions={0} | all-to-all | bytes 1572864 | tf_op jit(solution)/shard_map/all_to_all | solution.py:384
  138.2 0.8 third.1
  139.0 0.7 broadcast_in_dim.69
  139.6 5.4 %all-to-all-start.3 = ((f32[16,24,128]{2,1,0:T(8,128)}), f32[16,24,128]{2,1,0:T(8,128)S(1)}, u32[]{:S(2)}, u32[]{:S(2)}) async-start(f32[16,24,128]{2,1,0:T(8,128)} %broadcast_in_dim.69), calls=%async_computation.3 | async-start | bytes 393216 | tf_op jit(solution)/shard_map/all_to_all | solution.py:327
  145.0 2.0 %collective-permute-start.4 = (bf16[16,768]{1,0:T(8,128)(2,1)S(1)}, bf16[16,768]{1,0:T(8,128)(2,1)S(1)}, u32[]{:S(2)}, u32[]{:S(2)}) collective-permute-start(bf16[16,768]{1,0:T(8,128)(2,1)S(1)} %get-tuple-element.45.own), channel_id=1, source_target_pairs={{0,1},{1,0},{2,3},{3,2},{4,5},{5,4},{6,7},{7,6},{8,9},{9,8},{10,11... | collective-permute-start | bytes 73736 | tf_op jit(solution)/shard_map/ppermute | solution.py:392
  147.0 1.1 collective-permute-done.4.other
  148.1 3.6 %all-to-all-done.3.gains = f32[16,24,128]{2,1,0:T(8,128)S(1)} async-done(((f32[16,24,128]{2,1,0:T(8,128)}), f32[16,24,128]{2,1,0:T(8,128)S(1)}, u32[]{:S(2)}, u32[]{:S(2)}) %all-to-all-start.3) | async-done | bytes 196640 | tf_op jit(solution)/shard_map/all_to_all | solution.py:327
  151.7 0.6 last.1
  (51 shorter events, 0.6 us)
Async XLA Ops:
  0.7 0.7 copy-start.15
  1.3 0.7 copy-start.12
  1.3 0.7 copy-start.13
  2.9 48.3 %copy-start.21 = (f32[1536]{0:T(1024)S(1)}, f32[1536]{0:T(1024)}, u32[]{:S(2)}) copy-start(f32[1536]{0:T(1024)} %param.31) | copy-start | bytes 18436
  2.9 48.3 %copy-start.22 = (f32[1536]{0:T(1024)S(1)}, f32[1536]{0:T(1024)}, u32[]{:S(2)}) copy-start(f32[1536]{0:T(1024)} %param.30) | copy-start | bytes 18436
  2.9 48.3 %copy-start.23 = (f32[1536]{0:T(1024)S(1)}, f32[1536]{0:T(1024)}, u32[]{:S(2)}) copy-start(f32[1536]{0:T(1024)} %param.29) | copy-start | bytes 18436
  2.9 49.9 %copy-start = (bf16[1,128,1536]{2,1,0:T(8,128)(2,1)S(1)}, bf16[1,128,1536]{2,1,0:T(8,128)(2,1)}, u32[]{:S(2)}) copy-start(bf16[1,128,1536]{2,1,0:T(8,128)(2,1)} %param.18) | copy-start | bytes 1179652
  2.9 49.9 %copy-start.9 = (bf16[1,128,1536]{2,1,0:T(8,128)(2,1)S(1)}, bf16[1,128,1536]{2,1,0:T(8,128)(2,1)}, u32[]{:S(2)}) copy-start(bf16[1,128,1536]{2,1,0:T(8,128)(2,1)} %param.17) | copy-start | bytes 1179652
  2.9 49.9 %copy-start.10 = (bf16[1,128,1536]{2,1,0:T(8,128)(2,1)S(1)}, bf16[1,128,1536]{2,1,0:T(8,128)(2,1)}, u32[]{:S(2)}) copy-start(bf16[1,128,1536]{2,1,0:T(8,128)(2,1)} %param.19) | copy-start | bytes 1179652
  3.0 49.9 %copy-start.11 = (bf16[1,128,1536]{2,1,0:T(8,128)(2,1)S(1)}, bf16[1,128,1536]{2,1,0:T(8,128)(2,1)}, u32[]{:S(2)}) copy-start(bf16[1,128,1536]{2,1,0:T(8,128)(2,1)} %param.20) | copy-start | bytes 1179652
  45.0 6.9 %copy-start.18 = (bf16[32,8,1664]{2,1,0:T(8,128)(2,1)}, bf16[32,8,1664]{2,1,0:T(8,128)(2,1)S(1)}, u32[]{:S(2)}) copy-start(bf16[32,8,1664]{2,1,0:T(8,128)(2,1)S(1)} %all_to_all.20) | copy-start | bytes 2555908
  45.0 6.2 %copy-start.20 = (f32[1536]{0:T(1024)S(1)}, f32[1536]{0:T(1024)}, u32[]{:S(2)}) copy-start(f32[1536]{0:T(1024)} %param.32) | copy-start | bytes 18436
  45.0 6.9 %collective-permute-start = (bf16[256,1664]{1,0:T(8,128)(2,1)S(1)}, bf16[256,1664]{1,0:T(8,128)(2,1)S(1)}, u32[]{:S(2)}, u32[]{:S(2)}) collective-permute-start(bf16[256,1664]{1,0:T(8,128)(2,1)S(1)} %bitcast.36), channel_id=1, source_target_pairs={{0,1},{1,0},{2,3},{3,2},{4,5},{5,4},{6,7},{7,6},{8,9},{9,8},{10,11... | collective-permute-start | bytes 2555912 | tf_op jit(solution)/shard_map/ppermute | solution.py:353
  51.9 0.9 copy-start.19
  51.9 0.9 copy-start.14
  51.9 0.9 copy-start.16
  63.6 0.9 copy-start.1
  64.6 0.7 copy-start.3
  65.3 0.9 copy-start.17
  66.2 3.9 %copy-start.5 = (bf16[128,1536]{1,0:T(8,128)(2,1)}, bf16[128,1536]{1,0:T(8,128)(2,1)S(1)}, u32[]{:S(2)}) copy-start(bf16[128,1536]{1,0:T(8,128)(2,1)S(1)} %get-tuple-element.37.low_ac) | copy-start | bytes 1179652
  66.2 3.9 %copy-start.7 = (f32[6,128,128]{2,1,0:T(8,128)}, f32[6,128,128]{2,1,0:T(8,128)S(1)}, u32[]{:S(2)}) copy-start(f32[6,128,128]{2,1,0:T(8,128)S(1)} %get-tuple-element.38.tables) | copy-start | bytes 1179652
  66.2 3.1 %collective-permute-start.1 = (f32[24,128]{1,0:T(8,128)S(1)}, f32[24,128]{1,0:T(8,128)S(1)}, u32[]{:S(2)}, u32[]{:S(2)}) collective-permute-start(f32[24,128]{1,0:T(8,128)S(1)} %get-tuple-element.33), channel_id=1, source_target_pairs={{0,1},{1,0},{2,3},{3,2},{4,5},{5,4},{6,7},{7,6},{8,9},{9,8},{10,11... | collective-permute-start | bytes 36872 | tf_op jit(solution)/shard_map/ppermute | solution.py:370
  70.1 20.6 %all-to-all-start.1 = ((f32[32,24,128]{2,1,0:T(8,128)}), f32[32,24,128]{2,1,0:T(8,128)S(1)}, u32[]{:S(2)}, u32[]{:S(2)}) async-start(f32[32,24,128]{2,1,0:T(8,128)} %broadcast_in_dim.66), calls=%async_computation.1 | async-start | bytes 786432 | tf_op jit(solution)/shard_map/all_to_all | solution.py:327
  76.5 27.5 %collective-permute-start.2 = (f32[33,48,128]{2,1,0:T(8,128)}, f32[33,48,128]{2,1,0:T(8,128)S(1)}, u32[]{:S(2)}, u32[]{:S(2)}) collective-permute-start(f32[33,48,128]{2,1,0:T(8,128)} %copy-done.17), channel_id=1, source_target_pairs={{0,1},{1,0},{2,3},{3,2},{4,5},{5,4},{6,7},{7,6},{8,9},{9,8},{10,11... | collective-permute-start | bytes 2433032 | tf_op jit(solution)/shard_map/ppermute | solution.py:371
  90.6 1.1 copy-start.2
  91.8 1.0 copy-start.4
  92.8 1.0 copy-start.6
  93.8 1.0 copy-start.8
  99.9 5.5 %collective-permute-start.3 = (f32[33,24,128]{2,1,0:T(8,128)S(1)}, f32[33,24,128]{2,1,0:T(8,128)S(1)}, u32[]{:S(2)}, u32[]{:S(2)}) collective-permute-start(f32[33,24,128]{2,1,0:T(8,128)S(1)} %get-tuple-element.44), channel_id=1, source_target_pairs={{0,1},{1,0},{2,3},{3,2},{4,5},{5,4},{6,7},{7,6},{8,9},{9,8},{10,11... | collective-permute-start | bytes 1216520 | tf_op jit(solution)/shard_map/ppermute | solution.py:380
  139.6 12.1 %all-to-all-start.3 = ((f32[16,24,128]{2,1,0:T(8,128)}), f32[16,24,128]{2,1,0:T(8,128)S(1)}, u32[]{:S(2)}, u32[]{:S(2)}) async-start(f32[16,24,128]{2,1,0:T(8,128)} %broadcast_in_dim.69), calls=%async_computation.3 | async-start | bytes 393216 | tf_op jit(solution)/shard_map/all_to_all | solution.py:327
  145.0 3.1 %collective-permute-start.4 = (bf16[16,768]{1,0:T(8,128)(2,1)S(1)}, bf16[16,768]{1,0:T(8,128)(2,1)S(1)}, u32[]{:S(2)}, u32[]{:S(2)}) collective-permute-start(bf16[16,768]{1,0:T(8,128)(2,1)S(1)} %get-tuple-element.45.own), channel_id=1, source_target_pairs={{0,1},{1,0},{2,3},{3,2},{4,5},{5,4},{6,7},{7,6},{8,9},{9,8},{10,11... | collective-permute-start | bytes 73736 | tf_op jit(solution)/shard_map/ppermute | solution.py:392

commit v2 on v1

v2 whole, which is shorter than its diff:
```python
import functools

import jax
import jax.numpy as jnp
import numpy as np
from jax import lax
from jax.experimental import pallas as pl
from jax.experimental.pallas import tpu as pltpu
from jax.sharding import PartitionSpec as P

H = 12
DH = 128
HALF = DH // 2
EPS = 1e-06
THETA = 10000.0
SCALE = DH ** (-0.5)
BF = jnp.bfloat16
F32 = jnp.float32
VMEM_LIMIT = 24 * 1024 * 1024
HALF_HEADS = H // 2
WIDTH = HALF_HEADS * DH


def frequencies():
    freqs = np.power(np.float64(THETA), -(np.arange(HALF, dtype=np.float64) / HALF))
    return jnp.asarray(np.tile(freqs.astype(np.float32), 2).reshape(1, DH))


def sin_cos(angles):
    turns = jnp.floor(angles * F32(2.0 / np.pi) + 0.5)
    rest = angles - turns * F32(1.5703125)
    rest = rest - turns * F32(4.837512969970703125e-4)
    rest = rest - turns * F32(7.54978995489188216e-8)
    sq = rest * rest
    sine = rest + rest * sq * (
        F32(-1.6666654611e-1) + sq * (F32(8.3321608736e-3) + sq * F32(-1.9515295891e-4))
    )
    cosine = (
        1.0
        - 0.5 * sq
        + sq * sq * (F32(4.166664568298827e-2) + sq * (F32(-1.388731625493765e-3) + sq * F32(2.443315711809948e-5)))
    )
    quarter = turns.astype(jnp.int32)
    odd = (quarter & 1) == 1
    flip = (quarter & 2) == 2
    base_s = jnp.where(odd, cosine, sine)
    base_c = jnp.where(odd, -sine, cosine)
    return jnp.where(flip, -base_s, base_s), jnp.where(flip, -base_c, base_c)


def rotary_tables(pos, freqs):
    sine, cosine = sin_cos(pos * freqs)
    lane = lax.broadcasted_iota(jnp.int32, sine.shape, 1)
    return cosine, jnp.where(lane < HALF, -sine, sine)


def swap(rows):
    return pltpu.roll(rows, HALF, 1)


def unit(rows):
    scale = lax.rsqrt(jnp.sum(rows * rows, axis=-1, keepdims=True) * (1.0 / DH) + EPS)
    return rows * scale, scale


def turn(unit_rows, gain, cosine, sine):
    scaled = unit_rows * gain
    return (scaled * cosine + swap(scaled) * sine).astype(BF)


def turn_back(grad, cosine, sine):
    return grad * cosine - swap(grad) * sine


def norm_back(scaled_grad, unit_rows, scale, gain):
    inner = scaled_grad * gain
    mean = jnp.sum(inner * unit_rows, axis=-1, keepdims=True) * (1.0 / DH)
    return scale * (inner - unit_rows * mean)


def low_rows(shape):
    return (lax.broadcasted_iota(jnp.int32, shape, 0) & 7) < 4


def part_rows(both):
    left, right = both[:DH], both[DH:]
    low = low_rows(left.shape)
    one = jnp.where(low, left, pltpu.roll(right, 4, 0))
    two = jnp.where(low, pltpu.roll(left, DH - 4, 0), right)
    return one, two


def join_rows(one, two):
    low = low_rows(one.shape)
    left = jnp.where(low, one, pltpu.roll(two, 4, 0))
    right = jnp.where(low, pltpu.roll(one, DH - 4, 0), two)
    return left, right


def audio_index():
    row = lax.broadcasted_iota(jnp.int32, (DH, DH), 0)
    inside = row & 7
    return jnp.where(inside < 4, 0, 60) + (row >> 3) * 4 + inside


def dot_nt(a, b):
    return lax.dot_general(a, b, (((1,), (1,)), ((), ())), preferred_element_type=F32)


def dot_tn(a, b):
    return lax.dot_general(a, b, (((0,), (0,)), ((), ())), preferred_element_type=F32)


def dot_nn(a, b):
    return lax.dot_general(a, b, (((1,), (0,)), ((), ())), preferred_element_type=F32)


def lanes(head):
    return pl.ds(pl.multiple_of(head * DH, DH), DH)


def heads_of(core):
    return core * HALF_HEADS


def fetch(pairs, done):
    copies = [pltpu.make_async_copy(far, near, done.at[at]) for at, (far, near) in enumerate(pairs)]
    for copy in copies:
        copy.start()
    return copies


def finish(copies):
    for copy in copies:
        copy.wait()


def payload_kernel(apos_far, aq_far, ak_far, av_far, ac_far, out, apos, aq, ak, av, ac, done):
    finish(fetch(((apos_far, apos), (aq_far, aq), (ak_far, ak), (av_far, av), (ac_far, ac)), done))
    base = heads_of(lax.axis_index("aseq"))
    for j in range(HALF_HEADS):
        columns = lanes(base + j)
        for at, pair in enumerate(((aq, ak), (av, ac))):
            rows = jnp.concatenate([ref[0, :, columns].astype(F32) for ref in pair], axis=0).astype(BF)
            out[:, 2 * j + at] = jnp.broadcast_to(rows[None], (32, 8, DH))
    inside = lax.broadcasted_iota(jnp.int32, (8, DH), 0) & 3
    lane = lax.broadcasted_iota(jnp.int32, (8, DH), 1)
    pos = own_places(apos, inside)
    pos = jnp.where(lane < HALF, pos >> 6, pos & 63).astype(F32).astype(BF)
    out[:, 2 * HALF_HEADS] = jnp.broadcast_to(pos[None], (32, 8, DH))


def own_places(apos, inside):
    early = jnp.where(inside == 0, apos[0, 0], apos[0, 1])
    late = jnp.where(inside == 2, apos[0, 2], apos[0, 3])
    return jnp.where(inside < 2, early, late)


def send_kernel(vq, vk, vv, vc, out):
    base = heads_of(1 - lax.axis_index("aseq"))
    columns = pl.ds(pl.multiple_of(base * DH, DH), WIDTH)
    for at, ref in enumerate((vq, vk, vv, vc)):
        out[at] = ref[:, columns]


def video_mask(vlen, core):
    place = lax.axis_index("vseq") * 2 + core
    row = lax.broadcasted_iota(jnp.int32, (DH, DH), 0)
    return [(row + where * DH < vlen[0]).astype(F32) for where in (place, place + 1 - 2 * core)]


def video_kernel(
    vlen, vq, vk, vv, vc, got, pos_own, pos_got, freqs, gains,
    queries_far, keys_far, raw_vk_far, unit_vk_far, tables_far,
    queries, keys, raw_vk, unit_vk, tables, done,
):
    core = lax.axis_index("aseq")
    base = heads_of(core)
    masks = video_mask(vlen, core)
    for at, pos in enumerate((pos_own, pos_got)):
        rows = slice(at * DH, (at + 1) * DH)
        spread = jnp.transpose(jnp.broadcast_to(pos[...].astype(F32), (DH, DH)))
        tables[0, rows], tables[1, rows] = rotary_tables(spread, freqs[...])
        tables[2, rows] = masks[at]

    def one_head(j, carry):
        columns = lanes(j)
        own_columns = lanes(base + j)
        for at in range(2):
            rows = slice(at * DH, (at + 1) * DH)
            take = (lambda ref, index: ref[:, own_columns]) if at == 0 else (lambda ref, index: got[index, :, columns])
            cosine, sine, mask = tables[0, rows], tables[1, rows], tables[2, rows]
            query, key = take(vq, 0), take(vk, 1)
            queries[j, 0, rows] = query
            raw_vk[j, rows] = key
            keys[j, 1, rows] = take(vv, 2)
            queries[j, 2, rows] = (take(vc, 3).astype(F32) * mask).astype(BF)
            unit_query, _ = unit(query.astype(F32))
            unit_key, _ = unit(key.astype(F32))
            queries[j, 1, rows] = turn(unit_query, gains[pl.ds(base + j, 1), :], cosine, sine)
            keys[j, 0, rows] = turn(unit_key, gains[pl.ds(H + base + j, 1), :], cosine, sine)
            unit_vk[j, rows] = unit_key
        return carry

    lax.fori_loop(0, HALF_HEADS, one_head, 0)
    finish(
        fetch(
            (
                (queries, queries_far), (keys, keys_far), (raw_vk, raw_vk_far), (unit_vk, unit_vk_far),
                (tables, tables_far),
            ),
            done,
        )
    )


def audio_tables(gathered, freqs, alen):
    lane = lax.broadcasted_iota(jnp.int32, (DH, DH), 1)
    apos, _ = part_rows(gathered[:, 2 * HALF_HEADS].astype(F32).reshape(2 * DH, DH))
    apos = jnp.where(lane < HALF, apos * 64.0, apos)
    apos = apos + swap(apos)
    cosine, sine = rotary_tables(apos, freqs[...])
    return cosine, sine, (audio_index() < alen[0]).astype(F32)


def scores_kernel(alen, vlen, gathered, keys, freqs, gains, sums, tables, mask):
    core = lax.axis_index("aseq")
    base = heads_of(core)
    tables[0], tables[1], tables[2] = audio_tables(gathered, freqs, alen)
    mask[0:DH], mask[DH : 2 * DH] = video_mask(vlen, core)
    found = []
    for j in range(HALF_HEADS):
        aq, _ = part_rows(gathered[:, 2 * j].astype(F32).reshape(2 * DH, DH))
        _, ac = part_rows(gathered[:, 2 * j + 1].astype(F32).reshape(2 * DH, DH))
        rows, _ = unit(aq)
        query = turn(rows, gains[pl.ds(2 * H + base + j, 1), :], tables[0], tables[1])
        cross = jnp.exp(dot_nt(keys[j, 0], query) * SCALE) * mask[...]
        dprob = dot_nt(keys[j, 1], (ac * tables[2]).astype(BF))
        found.append((jnp.sum(cross, axis=0, keepdims=True), jnp.sum(cross * dprob, axis=0, keepdims=True)))
    rows = [pair[0] for pair in found] + [pair[1] for pair in found]
    for at in range(3):
        block = jnp.concatenate(rows[4 * at : 4 * at + 4], axis=0)
        sums[:, at] = jnp.broadcast_to(block[None], (32, 4, DH))


def queries_kernel(
    alen, gathered, freqs, gains, queries_far, keys_far, video_far,
    scores_far, audio_far, tables_far, part_far, gain_far, other_far, grad_own,
    queries, keys, video_tables, scores, audio, tables, part, gain_rows, grad_other, done_in, done_out,
):
    coming = fetch(((video_far, video_tables), (keys_far, keys), (queries_far, queries)), done_in)
    base = heads_of(lax.axis_index("aseq"))
    tables[0], tables[1], tables[2] = audio_tables(gathered, freqs, alen)
    gain_rows[...] = jnp.zeros(gain_rows.shape, F32)
    finish(coming)

    def one_head(j):
        columns = lanes(j)
        cos_v, sin_v, mask_v = video_tables[0], video_tables[1], video_tables[2]
        cos_a, sin_a, mask_a = tables[0], tables[1], tables[2]
        aq, ak = part_rows(gathered[:, 2 * j].astype(F32).reshape(2 * DH, DH))
        av, ac = part_rows(gathered[:, 2 * j + 1].astype(F32).reshape(2 * DH, DH))
        av = av.astype(BF)
        ac = (ac * mask_a).astype(BF)
        unit_aq, _ = unit(aq)
        low_aq = turn(unit_aq, gains[pl.ds(2 * H + base + j, 1), :], cos_a, sin_a)
        unit_ak, _ = unit(ak)
        low_ak = turn(unit_ak, gains[pl.ds(3 * H + base + j, 1), :], cos_a, sin_a)
        scores[j, 0 : 2 * DH] = jnp.exp(dot_nt(keys[j, 0], low_aq) * SCALE) * mask_v
        scores[j, 2 * DH : 4 * DH] = dot_nt(keys[j, 1], ac)
        scores[j, 4 * DH : 5 * DH] = unit_aq
        audio[j, 0] = low_aq
        audio[j, 1] = ac
        rows, cots = queries[j, 1], queries[j, 2]
        expd = jnp.exp(dot_nt(low_ak, rows) * SCALE) * jnp.concatenate([mask_a, mask_a], axis=1)
        prob = expd * (1.0 / jnp.sum(expd, axis=0, keepdims=True))
        dp = dot_nt(av, cots)
        delta = jnp.sum(prob * dp, axis=0, keepdims=True)
        dscore = (prob * (dp - delta)).astype(BF)
        dk = dot_nn(dscore, rows) * SCALE
        dv = dot_nn(prob.astype(BF), cots)
        back = turn_back(dot_tn(dscore, low_ak) * SCALE, cos_v, sin_v)
        unit_vq, scale_vq = unit(queries[j, 0].astype(F32))
        grad = norm_back(back, unit_vq, scale_vq, gains[pl.ds(base + j, 1), :]).astype(BF)
        grad_own[:, columns] = grad[:DH]
        grad_other[:, columns] = grad[DH:]
        gain_rows[pl.ds(j, 1), :] = jnp.sum(back * unit_vq, axis=0, keepdims=True)
        gain_rows[pl.ds(18 + j, 1), :] = jnp.sum(turn_back(dk, cos_a, sin_a) * unit_ak, axis=0, keepdims=True)
        return dk, dv

    def pair(step, carry):
        found = [one_head(2 * step + e) for e in range(2)]
        for array in range(2):
            left, right = join_rows(found[0][array], found[1][array])
            part[0:16, array * 3 + step] = left.reshape(16, 8, DH).astype(BF)
            part[16:32, array * 3 + step] = right.reshape(16, 8, DH).astype(BF)
        return carry

    lax.fori_loop(0, 3, pair, 0)
    finish(
        fetch(
            (
                (scores, scores_far), (audio, audio_far), (tables, tables_far), (part, part_far),
                (gain_rows, gain_far), (grad_other, other_far),
            ),
            done_out,
        )
    )


def back_kernel(
    totals, scores_far, audio_far, keys_far, unit_vk_far, video_far, tables_far, part_far, gain_far, merged,
    scores, audio, keys, unit_vk, video_tables, tables, gain_rows, done,
):
    first = [(scores_far.at[j], scores.at[j]) for j in range(HALF_HEADS)]
    second = [(audio_far.at[j, 0], audio.at[j]) for j in range(HALF_HEADS)]
    third = [(keys_far.at[j, 0], keys.at[j]) for j in range(HALF_HEADS)]
    fourth = [(unit_vk_far.at[j], unit_vk.at[j]) for j in range(HALF_HEADS)]
    order = [pair for head in zip(first, third, second, fourth) for pair in head]
    order[4:4] = [(video_far, video_tables), (tables_far, tables), (gain_far, gain_rows)]
    order.append((part_far, merged.at[:, 3:9]))
    copies = fetch(order, done)
    blocks = [jnp.sum(totals[:, at], axis=0) for at in range(3)]
    rows = [blocks[r // 4][r % 4 : r % 4 + 1] for r in range(2 * HALF_HEADS)]
    found = []
    for j in range(HALF_HEADS):
        finish(copies[:7] if j == 0 else copies[4 * j + 3 : 4 * j + 7])
        inverse = 1.0 / rows[j]
        delta = rows[HALF_HEADS + j] * inverse
        dscore = (scores[j, 0 : 2 * DH] * inverse * (scores[j, 2 * DH : 4 * DH] - delta)).astype(BF)
        dq = dot_tn(dscore, keys[j]) * SCALE
        dk = dot_nn(dscore, audio[j]) * SCALE
        back = turn_back(dk, video_tables[0], video_tables[1])
        gain_rows[6 + j : 7 + j, :] = jnp.sum(back * unit_vk[j], axis=0, keepdims=True)
        back = turn_back(dq, tables[0], tables[1])
        gain_rows[12 + j : 13 + j, :] = jnp.sum(back * scores[j, 4 * DH : 5 * DH], axis=0, keepdims=True)
        found.append(dq)
        if j % 2 == 1:
            left, right = join_rows(found[j - 1], found[j])
            merged[0:16, j // 2] = left.reshape(16, 8, DH).astype(BF)
            merged[16:32, j // 2] = right.reshape(16, 8, DH).astype(BF)
    for at in range(3):
        block = gain_rows[8 * at : 8 * at + 8, :].astype(BF)
        merged[:, 9 + at] = jnp.broadcast_to(block[None], (32, 8, DH))
    finish(copies[-1:])


def keys_kernel(
    totals, scores_far, audio_far, raw_vk_far, video_far, query_far, gains,
    key_own, value_own, other, scores, audio, raw_vk, video_tables, sums, done,
):
    copies = fetch(
        (
            (scores_far.at[:, 0 : 4 * DH], scores), (audio_far, audio), (raw_vk_far, raw_vk),
            (video_far.at[0:2], video_tables), (query_far, other.at[0]),
        ),
        done,
    )
    base = heads_of(lax.axis_index("aseq"))
    for at in range(3):
        sums[4 * at : 4 * at + 4, :] = jnp.sum(totals[:, at], axis=0)
    finish(copies)

    def one_head(j, carry):
        columns = lanes(j)
        cosine, sine = video_tables[0], video_tables[1]
        inverse = 1.0 / sums[pl.ds(j, 1), :]
        delta = sums[pl.ds(HALF_HEADS + j, 1), :] * inverse
        prob = scores[j, 0 : 2 * DH] * inverse
        dscore = (prob * (scores[j, 2 * DH : 4 * DH] - delta)).astype(BF)
        dk = dot_nn(dscore, audio[j, 0]) * SCALE
        dv = dot_nn(prob.astype(BF), audio[j, 1]).astype(BF)
        unit_vk, scale_vk = unit(raw_vk[j].astype(F32))
        gain = gains[pl.ds(H + base + j, 1), :]
        grad = norm_back(turn_back(dk, cosine, sine), unit_vk, scale_vk, gain).astype(BF)
        key_own[:, columns] = grad[:DH]
        value_own[:, columns] = dv[:DH]
        other[1, :, columns] = grad[DH:]
        other[2, :, columns] = dv[DH:]
        return carry

    lax.fori_loop(0, HALF_HEADS, one_head, 0)


def place_kernel(query_own, key_own, value_own, got, grad_vq, grad_vk, grad_vv):
    core = lax.axis_index("aseq")
    own = pl.ds(pl.multiple_of(heads_of(core) * DH, DH), WIDTH)
    other = pl.ds(pl.multiple_of(heads_of(1 - core) * DH, DH), WIDTH)
    for at, (mine, grad) in enumerate(((query_own, grad_vq), (key_own, grad_vk), (value_own, grad_vv))):
        grad[:, own] = mine[...]
        grad[:, other] = got[at]


def audio_kernel(apos_far, aq_far, ak_far, freqs_far, gains_far, after, got, out, gain_out, apos, aq, ak, freqs, gains, done):
    copies = fetch(((apos_far, apos), (aq_far, aq), (ak_far, ak), (freqs_far, freqs), (gains_far, gains)), done)
    base = heads_of(lax.axis_index("aseq"))
    acc = got[0].astype(F32)
    for v in range(1, 32):
        acc = acc + got[v].astype(F32)
    gain_out[...] = jnp.broadcast_to(acc[9:12].reshape(1, 24, DH), gain_out.shape)
    finish(copies)
    pos = own_places(apos, lax.broadcasted_iota(jnp.int32, (8, DH), 0) & 3)
    cosine, sine = rotary_tables(pos.astype(F32), freqs[...])
    low = low_rows((8, DH))

    def rows_back(ref, gain_at, grad, at):
        first = base + 2 * at
        rows = jnp.concatenate([ref[0, :, lanes(first + e)].astype(F32) for e in range(2)], axis=0)
        gain = jnp.where(low, gains[pl.ds(gain_at * H + first, 1), :], gains[pl.ds(gain_at * H + first + 1, 1), :])
        unit_rows, scale = unit(rows)
        return norm_back(turn_back(grad, cosine, sine), unit_rows, scale, gain)

    for at in range(3):
        dq = rows_back(aq, 2, acc[at], at)
        dk = rows_back(ak, 3, acc[3 + at], at)
        dv = acc[6 + at]
        left = jnp.where(low, dq, pltpu.roll(dk, 4, 0))
        right = jnp.where(low, pltpu.roll(dq, 4, 0), dk)
        out[:, 2 * at * DH : (2 * at + 1) * DH] = jnp.concatenate([left, dv], axis=0).astype(BF)
        out[:, (2 * at + 1) * DH : (2 * at + 2) * DH] = jnp.concatenate([right, pltpu.roll(dv, 4, 0)], axis=0).astype(BF)


def last_kernel(own, other, gains, grad_aq, grad_ak, grad_av, sum_vq, sum_vk, sum_aq, sum_ak):
    front = lax.axis_index("aseq") == 0
    mine, others = own[...].astype(F32), other[...].astype(F32)
    for at, value in enumerate((jnp.where(front, mine, others), jnp.where(front, others, mine))):
        columns = slice(at * WIDTH, (at + 1) * WIDTH)
        grad_aq[:, columns] = value[0:4].astype(BF)
        grad_ak[:, columns] = value[4:8].astype(BF)
        grad_av[:, columns] = value[8:12].astype(BF)
    for half in range(2):
        total = gains[half]
        for d in range(1, gains.shape[0] // 2):
            total = total + gains[2 * d + half]
        for at, ref in enumerate((sum_vq, sum_vk, sum_aq, sum_ak)):
            ref[6 * half : 6 * half + 6, :] = total[6 * at : 6 * at + 6]


NEAR, FAR = pltpu.VMEM, pltpu.HBM


def call(kernel, name, outs, ins, smem=0, far=0, scratch=()):
    def shape_of(shape, dtype, space=None):
        return jax.ShapeDtypeStruct(shape, dtype) if space is None else space(shape, dtype)

    ins = [pltpu.with_memory_space_constraint(x, FAR) if smem <= at < smem + far else x for at, x in enumerate(ins)]
    return pl.pallas_call(
        kernel,
        name=name,
        out_shape=[shape_of(*out) for out in outs],
        in_specs=[pl.BlockSpec(memory_space=pltpu.SMEM)] * smem
        + [pl.BlockSpec(memory_space=FAR)] * far
        + [pl.BlockSpec(memory_space=NEAR)] * (len(ins) - smem - far),
        out_specs=[pl.BlockSpec(memory_space=FAR if FAR in out else NEAR) for out in outs],
        scratch_shapes=list(scratch),
        compiler_params=pltpu.CompilerParams(vmem_limit_bytes=VMEM_LIMIT),
    )(*ins)


def local(
    video_query, video_key, video_value, video_grad,
    audio_query, audio_key, audio_value, audio_grad,
    video_pos, audio_pos, video_len, audio_len,
    gain_vq, gain_vk, gain_aq, gain_ak,
):
    F = H * DH
    groups = lax.axis_size("vseq")
    clips = lax.axis_size("dp")
    exchange = functools.partial(lax.ppermute, axis_name="aseq", perm=[(0, 1), (1, 0)])
    to_group = functools.partial(lax.all_to_all, axis_name="vseq", split_axis=0, concat_axis=0, tiled=True)
    freqs = frequencies()
    gains = jnp.concatenate([gain_vq, gain_vk, gain_aq, gain_ak]).reshape(4 * H, DH)
    video = [video_query[0], video_key[0], video_value[0], video_grad[0]]
    half = (DH, WIDTH)
    tiles = (groups, 2 * HALF_HEADS, 8, DH)
    six = (HALF_HEADS, 2 * DH, DH)
    queries_shape, keys_shape = (HALF_HEADS, 3, 2 * DH, DH), (HALF_HEADS, 2, 2 * DH, DH)
    scores_shape, audio_shape = (HALF_HEADS, 5 * DH, DH), (HALF_HEADS, 2, DH, DH)
    video_tables_shape, tables_shape = (3, 2 * DH, DH), (3, DH, DH)
    part_shape, gain_shape = (groups, 6, 8, DH), (24, DH)
    dmas = lambda count: pltpu.SemaphoreType.DMA((count,))

    (payload,) = call(
        payload_kernel,
        "payload",
        [((groups, 2 * HALF_HEADS + 1, 8, DH), BF)],
        [audio_pos, audio_query, audio_key, audio_value, audio_grad],
        far=5,
        scratch=[pltpu.SMEM((1, 4), jnp.int32)] + [pltpu.VMEM((1, 4, F), BF)] * 4 + [dmas(5)],
    )
    gathered = to_group(payload)

    (send,) = call(send_kernel, "send", [((4, DH, WIDTH), BF)], video)
    video_got = exchange(send)
    pos_got = exchange(video_pos)
    queries, keys, raw_vk, unit_vk, video_tables = call(
        video_kernel,
        "video",
        [
            (queries_shape, BF, FAR), (keys_shape, BF, FAR), (six, BF, FAR), (six, F32, FAR),
            (video_tables_shape, F32, FAR),
        ],
        [video_len, *video, video_got, video_pos, pos_got, freqs, gains],
        smem=1,
        scratch=[
            pltpu.VMEM(queries_shape, BF), pltpu.VMEM(keys_shape, BF), pltpu.VMEM(six, BF), pltpu.VMEM(six, F32),
            pltpu.VMEM(video_tables_shape, F32), dmas(5),
        ],
    )

    (sums,) = call(
        scores_kernel,
        "scores",
        [((groups, 3, 4, DH), F32)],
        [audio_len, video_len, gathered, keys, freqs, gains],
        smem=2,
        scratch=[pltpu.VMEM(tables_shape, F32), pltpu.VMEM((2 * DH, DH), F32)],
    )
    totals = to_group(sums)

    far_queries = [queries, keys, video_tables]
    scores, audio, tables, part, gain_part, query_other, query_own = call(
        lambda alen, queries, keys, video, *rest: queries_kernel(alen, *rest[:3], queries, keys, video, *rest[3:]),
        "queries",
        [
            (scores_shape, F32, FAR), (audio_shape, BF, FAR), (tables_shape, F32, FAR), (part_shape, BF, FAR),
            (gain_shape, F32, FAR), (half, BF, FAR), (half, BF),
        ],
        [audio_len, *far_queries, gathered, freqs, gains],
        smem=1,
        far=3,
        scratch=[
            pltpu.VMEM(queries_shape, BF), pltpu.VMEM(keys_shape, BF), pltpu.VMEM(video_tables_shape, F32),
            pltpu.VMEM(scores_shape, F32), pltpu.VMEM(audio_shape, BF), pltpu.VMEM(tables_shape, F32),
            pltpu.VMEM(part_shape, BF), pltpu.VMEM(gain_shape, F32), pltpu.VMEM(half, BF), dmas(3), dmas(6),
        ],
    )

    (merged,) = call(
        lambda *refs: back_kernel(refs[8], *refs[:8], *refs[9:]),
        "back",
        [(tiles, BF)],
        [scores, audio, keys, unit_vk, video_tables, tables, part, gain_part, totals],
        far=8,
        scratch=[
            pltpu.VMEM(scores_shape, F32), pltpu.VMEM((HALF_HEADS, DH, DH), BF), pltpu.VMEM(six, BF),
            pltpu.VMEM(six, F32), pltpu.VMEM(video_tables_shape, F32), pltpu.VMEM(tables_shape, F32),
            pltpu.VMEM(gain_shape, F32), dmas(4 * HALF_HEADS + 4),
        ],
    )
    got = to_group(merged)

    key_own, value_own, other = call(
        lambda *refs: keys_kernel(refs[5], *refs[:5], *refs[6:]),
        "keys",
        [(half, BF), (half, BF), ((3, DH, WIDTH), BF)],
        [scores, audio, raw_vk, video_tables, query_other, totals, gains],
        far=5,
        scratch=[
            pltpu.VMEM((HALF_HEADS, 4 * DH, DH), F32), pltpu.VMEM(audio_shape, BF), pltpu.VMEM(six, BF),
            pltpu.VMEM((2, 2 * DH, DH), F32), pltpu.VMEM((16, DH), F32), dmas(5),
        ],
    )
    other_got = exchange(other)
    grad_vq, grad_vk, grad_vv = call(
        place_kernel, "place", [((DH, F), BF)] * 3, [query_own, key_own, value_own, other_got]
    )

    audio_half, gain_rows = call(
        audio_kernel,
        "audio",
        [((16, WIDTH), BF), ((2 * clips, 24, DH), F32)],
        [audio_pos, audio_query, audio_key, freqs, gains, grad_vv, got],
        far=6,
        scratch=[
            pltpu.SMEM((1, 4), jnp.int32), pltpu.VMEM((1, 4, F), BF), pltpu.VMEM((1, 4, F), BF),
            pltpu.VMEM((1, DH), F32), pltpu.VMEM((4 * H, DH), F32), dmas(5),
        ],
    )
    gain_got = lax.all_to_all(gain_rows, ("dp", "aseq"), 0, 0, tiled=True)
    audio_got = exchange(audio_half)
    grad_aq, grad_ak, grad_av, sum_vq, sum_vk, sum_aq, sum_ak = call(
        last_kernel,
        "last",
        [((4, F), BF)] * 3 + [((H, DH), F32)] * 4,
        [audio_half, audio_got, gain_got],
    )
    return (
        grad_vq[None],
        grad_vk[None],
        grad_vv[None],
        grad_aq[None],
        grad_ak[None],
        grad_av[None],
        sum_vq.reshape(F),
        sum_vk.reshape(F),
        sum_aq.reshape(F),
        sum_ak.reshape(F),
    )


def solution(mesh):
    video = P("dp", ("vseq", "aseq"), None)
    audio = P("dp", "vseq", None)
    in_specs = (
        (video,) * 4
        + (audio,) * 4
        + (P("dp", ("vseq", "aseq")), P("dp", "vseq"), P("dp"), P("dp"))
        + (P(),) * 4
    )
    out_specs = (video,) * 3 + (audio,) * 3 + (P(),) * 4
    return jax.shard_map(local, mesh=mesh, in_specs=in_specs, out_specs=out_specs, check_vma=False)
```

time: 153 us -> 119 us (0.78)
  blocking collectives: 74.7 us -> 0 us
  starting transfers between devices: 27.6 us -> 48.5 us
  waiting for transfers between devices: 19 us -> 39.6 us
  local copies, waits for them, and re-layouts: 10.4 us -> 1.19 us
  Pallas kernels: 17.5 us -> 26.4 us
    all_to_all x2 -> x0, blocking collectives: 74.7 us -> none  [the longest x1 42 us: to_all(): return lax.all_to_all(spread, axes, 0, 0, tiled=True)]
    all_to_all x2 -> x4, starting transfers between devices: 11.8 us -> 37.8 us  [the longest x1 16.7 us: local(): gathered = to_group(payload)]
    all_to_all x2 -> x4, waiting for transfers between devices: 15.2 us -> 37 us  [the longest x1 15.2 us: local(): gathered = to_group(payload)]
    pallas_call x5 -> x10, Pallas kernels: 17.5 us -> 26.4 us  [call(): pl.pallas_call(kernel, name=name, out_shape=[shape_of(*out) for out in ou...]
    unnamed x48 -> x24, local copies, waits for them, and re-layouts: 8.75 us -> 1.19 us
    ppermute x5 -> x4, starting transfers between devices: 15.8 us -> 10.7 us  [the longest x1 3.87 us: local(): other_got = exchange(other)]
    ppermute x5 -> x4, waiting for transfers between devices: 3.84 us -> 2.67 us  [the longest x1 1.61 us: local(): other_got = exchange(other)]
  transfers between devices with their start and end apart: 7 -> 8, of which waited for: 6 -> 6; matrix products, arithmetic and copies ran while one was open for 0% -> 0% of each run, Pallas kernels for 3% -> 13%
where the time goes in v2:
time: 119 us; the launch traced here: 118 us
  starting transfers between devices  48.5 us (41%)
  waiting for transfers between devices  39.6 us (33%)
  Pallas kernels  26.4 us (22%)
  between operations  2.26 us (2%)
  local copies, waits for them, and re-layouts  1.19 us (1%)
    pallas_call x10, Pallas kernels, call(): pl.pallas_call(kernel, name=name, out_shape=[shape_of(*out) for out in ou...  26.4 us
    all_to_all x1, starting transfers between devices, local(): gathered = to_group(payload)  16.7 us
    all_to_all x1, waiting for transfers between devices, local(): gathered = to_group(payload)  15.2 us
    all_to_all x1, waiting for transfers between devices, local(): got = to_group(merged)  13.6 us
    all_to_all x1, starting transfers between devices, local(): totals = to_group(sums)  8.18 us
    all_to_all x1, starting transfers between devices, local(): got = to_group(merged)  7.09 us
    all_to_all x1, starting transfers between devices, local(): gain_got = lax.all_to_all(gain_rows, ('dp', 'aseq'), 0, 0, tiled=True)  5.89 us
    all_to_all x1, waiting for transfers between devices, local(): totals = to_group(sums)  4.55 us
  transfers between devices with their start and end apart: 8, of which 6 were waited for; matrix products, arithmetic and copies ran while one was open for 0% of the time, Pallas kernels for 13%

profile of v2, /device:TPU:1, one launch (start us, length us, event | category | flops | bytes accessed | tf_op | source)
XLA Modules:
  0.0 118.0 jit_solution(13034408933358973013)
XLA Ops:
  0.7 2.0 %payload.1 = bf16[32,13,8,128]{3,2,1,0:T(8,128)(2,1)} custom-call(s32[1,4]{1,0:T(1,128)} %apos_far.3, bf16[1,4,1536]{2,1,0:T(4,128)(2,1)} %aq_far.3, bf16[1,4,1536]{2,1,0:T(4,128)(2,1)} %ak_far.3, bf16[1,4,1536]{2,1,0:T(4,128)(2,1)} %av_far.1, bf16[1,4,1536]{2,1,0:T(4,128)(2,1)} %ac_far.1), custom_call_target="tpu_custom_call" | custom-call | tf_op jit(solution)/shard_map/payload/pallas_call | solution.py:447
  2.7 0.0 copy-start.7
  2.7 0.0 copy-start.8
  2.7 0.0 copy-start.9
  2.7 0.0 copy-start.10
  2.7 0.0 copy-start.11
  2.7 0.0 copy-start.6
  2.7 16.7 %all-to-all-start = ((bf16[32,13,8,128]{3,2,1,0:T(8,128)(2,1)}), bf16[32,13,8,128]{3,2,1,0:T(8,128)(2,1)S(1)}, u32[]{:S(2)}, u32[]{:S(2)}) async-start(bf16[32,13,8,128]{3,2,1,0:T(8,128)(2,1)} %payload.1), calls=%async_computation | async-start | bytes 1703936 | tf_op jit(solution)/shard_map/all_to_all | solution.py:491
  19.4 0.1 send.1
  19.5 2.9 %collective-permute-start = (bf16[4,128,768]{2,1,0:T(8,128)(2,1)S(1)}, bf16[4,128,768]{2,1,0:T(8,128)(2,1)S(1)}, u32[]{:S(2)}, u32[]{:S(2)}) collective-permute-start(bf16[4,128,768]{2,1,0:T(8,128)(2,1)S(1)} %send.1), channel_id=1, source_target_pairs={{0,1},{1,0},{2,3},{3,2},{4,5},{5,4},{6,7},{7,6},{8,9},{9,8},{10,11... | collective-permute-start | bytes 2359304 | tf_op jit(solution)/shard_map/ppermute | solution.py:494
  22.4 1.9 %collective-permute-start.1 = (s32[1,128]{1,0:T(1,128)S(1)}, s32[1,128]{1,0:T(1,128)S(1)}, u32[]{:S(2)}, u32[]{:S(2)}) collective-permute-start(s32[1,128]{1,0:T(1,128)S(1)} %copy-done.7), channel_id=1, source_target_pairs={{0,1},{1,0},{2,3},{3,2},{4,5},{5,4},{6,7},{7,6},{8,9},{9,8},{10,11... | collective-permute-start | bytes 1544 | tf_op jit(solution)/shard_map/ppermute | solution.py:495
  25.7 0.0 collective-permute-done.1.pos_got
  25.7 4.0 %video.1 = (bf16[6,3,256,128]{3,2,1,0:T(8,128)(2,1)}, bf16[6,2,256,128]{3,2,1,0:T(8,128)(2,1)}, bf16[6,256,128]{2,1,0:T(8,128)(2,1)}, f32[6,256,128]{2,1,0:T(8,128)}, f32[3,256,128]{2,1,0:T(8,128)}) custom-call(s32[1]{0:T(128)S(6)} %copy.27.vlen, bf16[128,1536]{1,0:T(8,128)(2,1)S(1)} %bitcast.19, bf16[128,1536]{1,0:T(8,128)(2,1)S(1)} %bitcast.21, ...), custom_call_target="tpu_custom_call" | custom-call | tf_op jit(solution)/shard_map/video/pallas_call | solution.py:447
  29.8 15.2 %all-to-all-done.rest_0_.gathered = bf16[32,13,8,128]{3,2,1,0:T(8,128)(2,1)S(1)} async-done(((bf16[32,13,8,128]{3,2,1,0:T(8,128)(2,1)}), bf16[32,13,8,128]{3,2,1,0:T(8,128)(2,1)S(1)}, u32[]{:S(2)}, u32[]{:S(2)}) %all-to-all-start) | async-done | bytes 852000 | tf_op jit(solution)/shard_map/all_to_all | solution.py:491
  45.0 1.1 copy-done
  46.1 2.2 %scores.1 = f32[32,3,4,128]{3,2,1,0:T(4,128)} custom-call(s32[1]{0:T(128)S(6)} %copy.28.alen, s32[1]{0:T(128)S(6)} %copy.27.vlen, bf16[32,13,8,128]{3,2,1,0:T(8,128)(2,1)S(1)} %all-to-all-done.rest_0_.gathered, bf16[6,2,256,128]{3,2,1,0:T(8,128)(2,1)S(1)} %copy-done, f32[1,128]{1,0:T(1,128)S(1)} %copy-done.6, ...), custom_call_target="tpu_custom_call" | custom-call | tf_op jit(solution)/shard_map/scores/pallas_call | solution.py:447
  48.4 8.2 %all-to-all-start.1 = ((f32[32,3,4,128]{3,2,1,0:T(4,128)}), f32[32,3,4,128]{3,2,1,0:T(4,128)S(1)}, u32[]{:S(2)}, u32[]{:S(2)}) async-start(f32[32,3,4,128]{3,2,1,0:T(4,128)} %scores.1), calls=%async_computation.1 | async-start | bytes 393216 | tf_op jit(solution)/shard_map/all_to_all | solution.py:519
  56.6 7.0 %queries.1 = (f32[6,640,128]{2,1,0:T(8,128)}, bf16[6,2,128,128]{3,2,1,0:T(8,128)(2,1)}, f32[3,128,128]{2,1,0:T(8,128)}, bf16[32,6,8,128]{3,2,1,0:T(8,128)(2,1)},...) custom-call(s32[1]{0:T(128)S(6)} %copy.28.alen, ...), custom_call_target="tpu_custom_call" | custom-call | tf_op jit(solution)/shard_map/queries/pallas_call | solution.py:447
  63.5 4.5 %all-to-all-done.1.refs_5_.refs_8_ = f32[32,3,4,128]{3,2,1,0:T(4,128)S(1)} async-done(((f32[32,3,4,128]{3,2,1,0:T(4,128)}), f32[32,3,4,128]{3,2,1,0:T(4,128)S(1)}, u32[]{:S(2)}, u32[]{:S(2)}) %all-to-all-start.1) | async-done | bytes 196640 | tf_op jit(solution)/shard_map/all_to_all | solution.py:519
  68.1 4.2 %back.1 = bf16[32,12,8,128]{3,2,1,0:T(8,128)(2,1)} custom-call(f32[6,640,128]{2,1,0:T(8,128)} %get-tuple-element.41.refs_0_, bf16[6,2,128,128]{3,2,1,0:T(8,128)(2,1)} %get-tuple-element.42.refs_1_, bf16[6,2,256,128]{3,2,1,0:T(8,128)(2,1)} %get-tuple-element.38.keys.refs_2_, f32[6,256,128]{2,1,0:T(8,128)} %get-tuple-element.51.refs_3_, ...), custom_call_target="tpu_custom_call" | custom-call | tf_op jit(solution)/shard_map/back/pallas_call | solution.py:447
  72.3 7.1 %all-to-all-start.2 = ((bf16[32,12,8,128]{3,2,1,0:T(8,128)(2,1)}), bf16[32,12,8,128]{3,2,1,0:T(8,128)(2,1)S(1)}, u32[]{:S(2)}, u32[]{:S(2)}) async-start(bf16[32,12,8,128]{3,2,1,0:T(8,128)(2,1)} %back.1), calls=%async_computation.2 | async-start | bytes 1572864 | tf_op jit(solution)/shard_map/all_to_all | solution.py:551
  79.4 3.7 %keys.1 = (bf16[128,768]{1,0:T(8,128)(2,1)S(1)}, bf16[128,768]{1,0:T(8,128)(2,1)S(1)}, bf16[3,128,768]{2,1,0:T(8,128)(2,1)S(1)}) custom-call(f32[6,640,128]{2,1,0:T(8,128)} %get-tuple-element.41.refs_0_, bf16[6,2,128,128]{3,2,1,0:T(8,128)(2,1)} %get-tuple-element.42.refs_1_, bf16[6,256,128]{2,1,0:T(8,128)(2,1)} %get-tuple-element.43.refs_2_, ...), custom_call_target="tpu_custom_call" | custom-call | tf_op jit(solution)/shard_map/keys/pallas_call | solution.py:447
  83.1 3.9 %collective-permute-start.2 = (bf16[3,128,768]{2,1,0:T(8,128)(2,1)S(1)}, bf16[3,128,768]{2,1,0:T(8,128)(2,1)S(1)}, u32[]{:S(2)}, u32[]{:S(2)}) collective-permute-start(bf16[3,128,768]{2,1,0:T(8,128)(2,1)S(1)} %get-tuple-element.47), channel_id=1, source_target_pairs={{0,1},{1,0},{2,3},{3,2},{4,5},{5,4},{6,7},{7,6},{8,9},{9,8},{10,11... | collective-permute-start | bytes 1769480 | tf_op jit(solution)/shard_map/ppermute | solution.py:564
  87.0 1.6 %collective-permute-done.2.got = bf16[3,128,768]{2,1,0:T(8,128)(2,1)S(1)} collective-permute-done((bf16[3,128,768]{2,1,0:T(8,128)(2,1)S(1)}, bf16[3,128,768]{2,1,0:T(8,128)(2,1)S(1)}, u32[]{:S(2)}, u32[]{:S(2)}) %collective-permute-start.2) | collective-permute-done | bytes 589856 | tf_op jit(solution)/shard_map/ppermute | solution.py:564
  88.6 1.1 place.1
  89.7 13.6 %all-to-all-done.2.got = bf16[32,12,8,128]{3,2,1,0:T(8,128)(2,1)S(1)} async-done(((bf16[32,12,8,128]{3,2,1,0:T(8,128)(2,1)}), bf16[32,12,8,128]{3,2,1,0:T(8,128)(2,1)S(1)}, u32[]{:S(2)}, u32[]{:S(2)}) %all-to-all-start.2) | async-done | bytes 786464 | tf_op jit(solution)/shard_map/all_to_all | solution.py:551
  103.3 1.5 %audio.1 = (bf16[16,768]{1,0:T(8,128)(2,1)S(1)}, f32[16,24,128]{2,1,0:T(8,128)}) custom-call(s32[1,4]{1,0:T(1,128)} %apos_far.3, bf16[1,4,1536]{2,1,0:T(4,128)(2,1)} %aq_far.3, bf16[1,4,1536]{2,1,0:T(4,128)(2,1)} %ak_far.3, f32[1,128]{1,0:T(1,128)} %constant.2.clone.freqs.rest_1_.freqs_far, f32[48,128]{1,0:T(8,128)} %copy-done.5, ...), custom_call_target="tpu_custom_call" | custom-call | tf_op jit(solution)/shard_map/audio/pallas_call | solution.py:447
  104.8 5.9 %all-to-all-start.3 = ((f32[16,24,128]{2,1,0:T(8,128)}), f32[16,24,128]{2,1,0:T(8,128)S(1)}, u32[]{:S(2)}, u32[]{:S(2)}) async-start(f32[16,24,128]{2,1,0:T(8,128)} %get-tuple-element.56), calls=%async_computation.3 | async-start | bytes 393216 | tf_op jit(solution)/shard_map/all_to_all | solution.py:580
  110.7 2.0 %collective-permute-start.3 = (bf16[16,768]{1,0:T(8,128)(2,1)S(1)}, bf16[16,768]{1,0:T(8,128)(2,1)S(1)}, u32[]{:S(2)}, u32[]{:S(2)}) collective-permute-start(bf16[16,768]{1,0:T(8,128)(2,1)S(1)} %get-tuple-element.55.own), channel_id=1, source_target_pairs={{0,1},{1,0},{2,3},{3,2},{4,5},{5,4},{6,7},{7,6},{8,9},{9,8},{10,11... | collective-permute-start | bytes 73736 | tf_op jit(solution)/shard_map/ppermute | solution.py:581
  112.7 1.1 collective-permute-done.3.other
  113.7 3.6 %all-to-all-done.3.gains = f32[16,24,128]{2,1,0:T(8,128)S(1)} async-done(((f32[16,24,128]{2,1,0:T(8,128)}), f32[16,24,128]{2,1,0:T(8,128)S(1)}, u32[]{:S(2)}, u32[]{:S(2)}) %all-to-all-start.3) | async-done | bytes 196640 | tf_op jit(solution)/shard_map/all_to_all | solution.py:580
  117.4 0.6 last.1
  (19 shorter events, 0.0 us)
Async XLA Ops:
  0.6 18.8 %copy-start.1 = (bf16[1,128,1536]{2,1,0:T(8,128)(2,1)S(1)}, bf16[1,128,1536]{2,1,0:T(8,128)(2,1)}, u32[]{:S(2)}) copy-start(bf16[1,128,1536]{2,1,0:T(8,128)(2,1)} %param.17) | copy-start | bytes 1179652
  0.7 18.8 %copy-start.2 = (bf16[1,128,1536]{2,1,0:T(8,128)(2,1)S(1)}, bf16[1,128,1536]{2,1,0:T(8,128)(2,1)}, u32[]{:S(2)}) copy-start(bf16[1,128,1536]{2,1,0:T(8,128)(2,1)} %param.18) | copy-start | bytes 1179652
  0.7 18.8 %copy-start.3 = (bf16[1,128,1536]{2,1,0:T(8,128)(2,1)S(1)}, bf16[1,128,1536]{2,1,0:T(8,128)(2,1)}, u32[]{:S(2)}) copy-start(bf16[1,128,1536]{2,1,0:T(8,128)(2,1)} %param.19) | copy-start | bytes 1179652
  0.7 18.8 %copy-start.4 = (bf16[1,128,1536]{2,1,0:T(8,128)(2,1)S(1)}, bf16[1,128,1536]{2,1,0:T(8,128)(2,1)}, u32[]{:S(2)}) copy-start(bf16[1,128,1536]{2,1,0:T(8,128)(2,1)} %param.20) | copy-start | bytes 1179652
  2.7 19.7 %copy-start.7 = (s32[1,128]{1,0:T(1,128)S(1)}, s32[1,128]{1,0:T(1,128)}, u32[]{:S(2)}) copy-start(s32[1,128]{1,0:T(1,128)} %pos_own.1) | copy-start | bytes 1540
  2.7 21.7 %copy-start.8 = (f32[1536]{0:T(1024)S(1)}, f32[1536]{0:T(1024)}, u32[]{:S(2)}) copy-start(f32[1536]{0:T(1024)} %param.32) | copy-start | bytes 18436
  2.7 21.7 %copy-start.9 = (f32[1536]{0:T(1024)S(1)}, f32[1536]{0:T(1024)}, u32[]{:S(2)}) copy-start(f32[1536]{0:T(1024)} %param.31) | copy-start | bytes 18436
  2.7 21.6 %copy-start.10 = (f32[1536]{0:T(1024)S(1)}, f32[1536]{0:T(1024)}, u32[]{:S(2)}) copy-start(f32[1536]{0:T(1024)} %param.30) | copy-start | bytes 18436
  2.7 21.6 %copy-start.11 = (f32[1536]{0:T(1024)S(1)}, f32[1536]{0:T(1024)}, u32[]{:S(2)}) copy-start(f32[1536]{0:T(1024)} %param.29) | copy-start | bytes 18436
  2.7 23.0 %copy-start.6 = (f32[1,128]{1,0:T(1,128)S(1)}, f32[1,128]{1,0:T(1,128)}, u32[]{:S(2)}) copy-start(f32[1,128]{1,0:T(1,128)} %constant.2.clone.freqs.rest_1_.freqs_far) | copy-start | bytes 1540
  2.7 42.3 %all-to-all-start = ((bf16[32,13,8,128]{3,2,1,0:T(8,128)(2,1)}), bf16[32,13,8,128]{3,2,1,0:T(8,128)(2,1)S(1)}, u32[]{:S(2)}, u32[]{:S(2)}) async-start(bf16[32,13,8,128]{3,2,1,0:T(8,128)(2,1)} %payload.1), calls=%async_computation | async-start | bytes 1703936 | tf_op jit(solution)/shard_map/all_to_all | solution.py:491
  19.5 6.2 %collective-permute-start = (bf16[4,128,768]{2,1,0:T(8,128)(2,1)S(1)}, bf16[4,128,768]{2,1,0:T(8,128)(2,1)S(1)}, u32[]{:S(2)}, u32[]{:S(2)}) collective-permute-start(bf16[4,128,768]{2,1,0:T(8,128)(2,1)S(1)} %send.1), channel_id=1, source_target_pairs={{0,1},{1,0},{2,3},{3,2},{4,5},{5,4},{6,7},{7,6},{8,9},{9,8},{10,11... | collective-permute-start | bytes 2359304 | tf_op jit(solution)/shard_map/ppermute | solution.py:494
  22.4 3.3 %collective-permute-start.1 = (s32[1,128]{1,0:T(1,128)S(1)}, s32[1,128]{1,0:T(1,128)S(1)}, u32[]{:S(2)}, u32[]{:S(2)}) collective-permute-start(s32[1,128]{1,0:T(1,128)S(1)} %copy-done.7), channel_id=1, source_target_pairs={{0,1},{1,0},{2,3},{3,2},{4,5},{5,4},{6,7},{7,6},{8,9},{9,8},{10,11... | collective-permute-start | bytes 1544 | tf_op jit(solution)/shard_map/ppermute | solution.py:495
  24.4 55.0 %copy-start.5 = (f32[48,128]{1,0:T(8,128)}, f32[48,128]{1,0:T(8,128)S(1)}, u32[]{:S(2)}) copy-start(f32[48,128]{1,0:T(8,128)S(1)} %pad_maximum_fusion.gains.rest_2_.refs_6_.gains_far) | copy-start | bytes 73732
  45.0 1.1 copy-start
  48.4 19.7 %all-to-all-start.1 = ((f32[32,3,4,128]{3,2,1,0:T(4,128)}), f32[32,3,4,128]{3,2,1,0:T(4,128)S(1)}, u32[]{:S(2)}, u32[]{:S(2)}) async-start(f32[32,3,4,128]{3,2,1,0:T(4,128)} %scores.1), calls=%async_computation.1 | async-start | bytes 393216 | tf_op jit(solution)/shard_map/all_to_all | solution.py:519
  72.3 31.0 %all-to-all-start.2 = ((bf16[32,12,8,128]{3,2,1,0:T(8,128)(2,1)}), bf16[32,12,8,128]{3,2,1,0:T(8,128)(2,1)S(1)}, u32[]{:S(2)}, u32[]{:S(2)}) async-start(bf16[32,12,8,128]{3,2,1,0:T(8,128)(2,1)} %back.1), calls=%async_computation.2 | async-start | bytes 1572864 | tf_op jit(solution)/shard_map/all_to_all | solution.py:551
  83.1 5.5 %collective-permute-start.2 = (bf16[3,128,768]{2,1,0:T(8,128)(2,1)S(1)}, bf16[3,128,768]{2,1,0:T(8,128)(2,1)S(1)}, u32[]{:S(2)}, u32[]{:S(2)}) collective-permute-start(bf16[3,128,768]{2,1,0:T(8,128)(2,1)S(1)} %get-tuple-element.47), channel_id=1, source_target_pairs={{0,1},{1,0},{2,3},{3,2},{4,5},{5,4},{6,7},{7,6},{8,9},{9,8},{10,11... | collective-permute-start | bytes 1769480 | tf_op jit(solution)/shard_map/ppermute | solution.py:564
  104.8 12.6 %all-to-all-start.3 = ((f32[16,24,128]{2,1,0:T(8,128)}), f32[16,24,128]{2,1,0:T(8,128)S(1)}, u32[]{:S(2)}, u32[]{:S(2)}) async-start(f32[16,24,128]{2,1,0:T(8,128)} %get-tuple-element.56), calls=%async_computation.3 | async-start | bytes 393216 | tf_op jit(solution)/shard_map/all_to_all | solution.py:580
  110.7 3.1 %collective-permute-start.3 = (bf16[16,768]{1,0:T(8,128)(2,1)S(1)}, bf16[16,768]{1,0:T(8,128)(2,1)S(1)}, u32[]{:S(2)}, u32[]{:S(2)}) collective-permute-start(bf16[16,768]{1,0:T(8,128)(2,1)S(1)} %get-tuple-element.55.own), channel_id=1, source_target_pairs={{0,1},{1,0},{2,3},{3,2},{4,5},{5,4},{6,7},{7,6},{8,9},{9,8},{10,11... | collective-permute-start | bytes 73736 | tf_op jit(solution)/shard_map/ppermute | solution.py:581

commit v3 on v2

v3 whole, which is shorter than its diff:
```python
import functools

import jax
import jax.numpy as jnp
import numpy as np
from jax import lax
from jax.experimental import pallas as pl
from jax.experimental.pallas import tpu as pltpu
from jax.sharding import PartitionSpec as P

H = 12
DH = 128
HALF = DH // 2
EPS = 1e-06
THETA = 10000.0
SCALE = DH ** (-0.5)
BF = jnp.bfloat16
F32 = jnp.float32
VMEM_LIMIT = 24 * 1024 * 1024
HALF_HEADS = H // 2
WIDTH = HALF_HEADS * DH


def frequencies():
    freqs = np.power(np.float64(THETA), -(np.arange(HALF, dtype=np.float64) / HALF))
    return jnp.asarray(np.tile(freqs.astype(np.float32), 2).reshape(1, DH))


def sin_cos(angles):
    turns = jnp.floor(angles * F32(2.0 / np.pi) + 0.5)
    rest = angles - turns * F32(1.5703125)
    rest = rest - turns * F32(4.837512969970703125e-4)
    rest = rest - turns * F32(7.54978995489188216e-8)
    sq = rest * rest
    sine = rest + rest * sq * (
        F32(-1.6666654611e-1) + sq * (F32(8.3321608736e-3) + sq * F32(-1.9515295891e-4))
    )
    cosine = (
        1.0
        - 0.5 * sq
        + sq * sq * (F32(4.166664568298827e-2) + sq * (F32(-1.388731625493765e-3) + sq * F32(2.443315711809948e-5)))
    )
    quarter = turns.astype(jnp.int32)
    odd = (quarter & 1) == 1
    flip = (quarter & 2) == 2
    base_s = jnp.where(odd, cosine, sine)
    base_c = jnp.where(odd, -sine, cosine)
    return jnp.where(flip, -base_s, base_s), jnp.where(flip, -base_c, base_c)


def rotary_tables(pos, freqs):
    sine, cosine = sin_cos(pos * freqs)
    lane = lax.broadcasted_iota(jnp.int32, sine.shape, 1)
    return cosine, jnp.where(lane < HALF, -sine, sine)


def swap(rows):
    return pltpu.roll(rows, HALF, 1)


def unit(rows):
    scale = lax.rsqrt(jnp.sum(rows * rows, axis=-1, keepdims=True) * (1.0 / DH) + EPS)
    return rows * scale, scale


def turn(unit_rows, gain, cosine, sine):
    scaled = unit_rows * gain
    return (scaled * cosine + swap(scaled) * sine).astype(BF)


def turn_back(grad, cosine, sine):
    return grad * cosine - swap(grad) * sine


def norm_back(scaled_grad, unit_rows, scale, gain):
    inner = scaled_grad * gain
    mean = jnp.sum(inner * unit_rows, axis=-1, keepdims=True) * (1.0 / DH)
    return scale * (inner - unit_rows * mean)


def low_rows(shape):
    return (lax.broadcasted_iota(jnp.int32, shape, 0) & 7) < 4


def part_rows(both):
    left, right = both[:DH], both[DH:]
    low = low_rows(left.shape)
    one = jnp.where(low, left, pltpu.roll(right, 4, 0))
    two = jnp.where(low, pltpu.roll(left, DH - 4, 0), right)
    return one, two


def join_rows(one, two):
    low = low_rows(one.shape)
    left = jnp.where(low, one, pltpu.roll(two, 4, 0))
    right = jnp.where(low, pltpu.roll(one, DH - 4, 0), two)
    return left, right


def audio_index():
    row = lax.broadcasted_iota(jnp.int32, (DH, DH), 0)
    inside = row & 7
    return jnp.where(inside < 4, 0, 60) + (row >> 3) * 4 + inside


def dot_nt(a, b):
    return lax.dot_general(a, b, (((1,), (1,)), ((), ())), preferred_element_type=F32)


def dot_tn(a, b):
    return lax.dot_general(a, b, (((0,), (0,)), ((), ())), preferred_element_type=F32)


def dot_nn(a, b):
    return lax.dot_general(a, b, (((1,), (0,)), ((), ())), preferred_element_type=F32)


def lanes(head):
    return pl.ds(pl.multiple_of(head * DH, DH), DH)


def heads_of(core):
    return core * HALF_HEADS


def fetch(pairs, done):
    copies = [pltpu.make_async_copy(far, near, done.at[at]) for at, (far, near) in enumerate(pairs)]
    for copy in copies:
        copy.start()
    return copies


def finish(copies):
    for copy in copies:
        copy.wait()


def spread_tile(out, at, rows):
    out[:, at] = jnp.broadcast_to(rows.astype(BF)[None], (32, 8, DH))


def payload_kernel(apos_far, aq_far, ac_far, ak_far, av_far, out, apos, aq, ac, ak, av, done):
    finish(fetch(((aq_far, aq), (ac_far, ac), (ak_far, ak), (av_far, av), (apos_far, apos)), done))
    base = heads_of(lax.axis_index("aseq"))
    for j in range(HALF_HEADS):
        columns = lanes(base + j)
        for at, pair in enumerate(((aq, ac), (ak, av))):
            spread_tile(out, 2 * j + at, jnp.concatenate([ref[0, :, columns].astype(F32) for ref in pair], axis=0))
    inside = lax.broadcasted_iota(jnp.int32, (8, DH), 0) & 3
    lane = lax.broadcasted_iota(jnp.int32, (8, DH), 1)
    pos = own_places(apos, inside)
    spread_tile(out, 2 * HALF_HEADS, jnp.where(lane < HALF, pos >> 6, pos & 63).astype(F32))


def own_places(apos, inside):
    early = jnp.where(inside == 0, apos[0, 0], apos[0, 1])
    late = jnp.where(inside == 2, apos[0, 2], apos[0, 3])
    return jnp.where(inside < 2, early, late)


def send_kernel(vq, vk, vv, vc, vpos, out):
    columns = pl.ds(pl.multiple_of(heads_of(1 - lax.axis_index("aseq")) * DH, DH), WIDTH)
    for at, ref in enumerate((vq, vk, vv, vc)):
        out[at * DH : (at + 1) * DH] = ref[:, columns]
    row = lax.broadcasted_iota(jnp.int32, (16, DH), 0)
    pos = jnp.broadcast_to(vpos[...], (16, DH))
    places = jnp.where(row == 0, pos >> 6, pos & 63).astype(F32).astype(BF)
    out[4 * DH : 4 * DH + 16] = jnp.concatenate([places] * HALF_HEADS, axis=1)


def video_mask(vlen, core):
    place = lax.axis_index("vseq") * 2 + core
    row = lax.broadcasted_iota(jnp.int32, (DH, DH), 0)
    return [(row + where * DH < vlen[0]).astype(F32) for where in (place, place + 1 - 2 * core)]


def video_kernel(
    vlen, vq, vk, vv, vc, got, pos_own, freqs, gains,
    keys, queries_far, keys_far, raw_vk_far, unit_vk_far, tables_far,
    queries, raw_vk, unit_vk, tables, done,
):
    core = lax.axis_index("aseq")
    base = heads_of(core)
    masks = video_mask(vlen, core)
    places = got[4 * DH : 4 * DH + 16, 0:DH].astype(F32)
    for at, pos in enumerate((pos_own[...].astype(F32), places[0:1] * 64.0 + places[1:2])):
        rows = slice(at * DH, (at + 1) * DH)
        spread = jnp.transpose(jnp.broadcast_to(pos, (DH, DH)))
        tables[0, rows], tables[1, rows] = rotary_tables(spread, freqs[...])
        tables[2, rows] = masks[at]

    def one_head(j, carry):
        columns = lanes(j)
        own_columns = lanes(base + j)
        for at in range(2):
            rows = slice(at * DH, (at + 1) * DH)
            take = (lambda ref, index: ref[:, own_columns]) if at == 0 else (lambda ref, index: got[index * DH : (index + 1) * DH, columns])
            cosine, sine, mask = tables[0, rows], tables[1, rows], tables[2, rows]
            query, key = take(vq, 0), take(vk, 1)
            queries[j, 0, rows] = query
            raw_vk[j, rows] = key
            keys[j, 1, rows] = take(vv, 2)
            queries[j, 2, rows] = (take(vc, 3).astype(F32) * mask).astype(BF)
            unit_query, _ = unit(query.astype(F32))
            unit_key, _ = unit(key.astype(F32))
            queries[j, 1, rows] = turn(unit_query, gains[pl.ds(base + j, 1), :], cosine, sine)
            keys[j, 0, rows] = turn(unit_key, gains[pl.ds(H + base + j, 1), :], cosine, sine)
            unit_vk[j, rows] = unit_key
        return carry

    lax.fori_loop(0, HALF_HEADS, one_head, 0)
    finish(
        fetch(
            (
                (queries, queries_far), (keys, keys_far), (raw_vk, raw_vk_far), (unit_vk, unit_vk_far),
                (tables, tables_far),
            ),
            done,
        )
    )


def audio_tables(gathered, freqs, alen):
    lane = lax.broadcasted_iota(jnp.int32, (DH, DH), 1)
    apos, _ = part_rows(gathered[:, 2 * HALF_HEADS].astype(F32).reshape(2 * DH, DH))
    apos = jnp.where(lane < HALF, apos * 64.0, apos)
    apos = apos + swap(apos)
    cosine, sine = rotary_tables(apos, freqs[...])
    return cosine, sine, (audio_index() < alen[0]).astype(F32)


def scores_kernel(alen, vlen, gathered, keys, freqs, gains, sums, gathered_far, tables, mask, done):
    copies = fetch([(gathered, gathered_far)], done)
    core = lax.axis_index("aseq")
    base = heads_of(core)
    tables[0], tables[1], tables[2] = audio_tables(gathered, freqs, alen)
    mask[0:DH], mask[DH : 2 * DH] = video_mask(vlen, core)
    found = []
    for j in range(HALF_HEADS):
        aq, ac = part_rows(gathered[:, 2 * j].astype(F32).reshape(2 * DH, DH))
        rows, _ = unit(aq)
        query = turn(rows, gains[pl.ds(2 * H + base + j, 1), :], tables[0], tables[1])
        cross = jnp.exp(dot_nt(keys[j, 0], query) * SCALE) * mask[...]
        dprob = dot_nt(keys[j, 1], (ac * tables[2]).astype(BF))
        found.append((jnp.sum(cross, axis=0, keepdims=True), jnp.sum(cross * dprob, axis=0, keepdims=True)))
    rows = [pair[0] for pair in found] + [pair[1] for pair in found]
    for at in range(3):
        block = jnp.concatenate(rows[4 * at : 4 * at + 4], axis=0)
        sums[:, at] = jnp.broadcast_to(block[None], (32, 4, DH))
    finish(copies)


EXPO, DPROB, UNIT_AQ, UNIT_VK, HEAD_ROWS = 0, 2 * DH, 4 * DH, 5 * DH, 7 * DH
TABLES = HALF_HEADS * HEAD_ROWS
COS_V, SIN_V, COS_A, SIN_A, GAINS = TABLES, TABLES + 256, TABLES + 512, TABLES + 640, TABLES + 768
GAIN_VK, GAIN_AQ, GAIN_SUMS, ALL_ROWS = GAINS, GAINS + 8, GAINS + 16, GAINS + 40


def rows_of(j, start, count):
    return pl.ds(pl.multiple_of(j * HEAD_ROWS + start, DH), count)


def queries_kernel(
    alen, vlen, queries_far, keys_far, unit_vk_far, video_far, gathered_far, freqs, gains,
    shared, part_far, grad_far, audio_far,
    queries, keys, gathered, masks, part, grads, audio, done_in, done_step, done_out,
):
    def coming(step):
        heads, rows = pl.ds(2 * step, 2), pl.ds(4 * step, 4)
        pairs = (
            (gathered_far.at[:, rows], gathered.at[:, rows]),
            (keys_far.at[heads], keys.at[heads]),
            (queries_far.at[heads], queries.at[heads]),
        )
        return [pltpu.make_async_copy(far, near, done_step.at[step, at]) for at, (far, near) in enumerate(pairs)]

    places = 2 * HALF_HEADS
    tables = fetch(
        [
            (gathered_far.at[:, places : places + 1], gathered.at[:, places : places + 1]),
            (video_far.at[0 : 2 * 2 * DH], shared.at[COS_V : COS_V + 4 * DH]),
        ],
        done_in,
    )
    for step in range(3):
        for copy in coming(step):
            copy.start()
    units = fetch(
        [(unit_vk_far.at[j], shared.at[j * HEAD_ROWS + UNIT_VK : (j + 1) * HEAD_ROWS]) for j in range(HALF_HEADS)],
        done_in.at[2 : 2 + HALF_HEADS],
    )
    core = lax.axis_index("aseq")
    base = heads_of(core)
    masks[DH : 2 * DH], masks[2 * DH : 3 * DH] = video_mask(vlen, core)
    shared[GAINS:ALL_ROWS] = jnp.zeros((ALL_ROWS - GAINS, DH), F32)
    tables[0].wait()
    shared[COS_A:SIN_A], shared[SIN_A:GAINS], masks[0:DH] = audio_tables(gathered, freqs, alen)
    tables[1].wait()

    def one_head(j):
        cos_v, sin_v, mask_v = shared[COS_V:SIN_V], shared[SIN_V:COS_A], masks[DH : 3 * DH]
        cos_a, sin_a, mask_a = shared[COS_A:SIN_A], shared[SIN_A:GAINS], masks[0:DH]
        gain_aq = gains[pl.ds(2 * H + base + j, 1), :]
        shared[pl.ds(GAIN_VK + j, 1), :] = gains[pl.ds(H + base + j, 1), :]
        shared[pl.ds(GAIN_AQ + j, 1), :] = gain_aq
        aq, ac = part_rows(gathered[:, 2 * j].astype(F32).reshape(2 * DH, DH))
        ak, av = part_rows(gathered[:, 2 * j + 1].astype(F32).reshape(2 * DH, DH))
        av = av.astype(BF)
        ac = (ac * mask_a).astype(BF)
        unit_aq, _ = unit(aq)
        low_aq = turn(unit_aq, gain_aq, cos_a, sin_a)
        unit_ak, _ = unit(ak)
        low_ak = turn(unit_ak, gains[pl.ds(3 * H + base + j, 1), :], cos_a, sin_a)
        shared[rows_of(j, EXPO, 2 * DH), :] = jnp.exp(dot_nt(keys[j, 0], low_aq) * SCALE) * mask_v
        shared[rows_of(j, DPROB, 2 * DH), :] = dot_nt(keys[j, 1], ac)
        shared[rows_of(j, UNIT_AQ, DH), :] = unit_aq
        audio[j, 0] = low_aq
        audio[j, 1] = ac
        rows, cots = queries[j, 1], queries[j, 2]
        expd = jnp.exp(dot_nt(low_ak, rows) * SCALE) * jnp.concatenate([mask_a, mask_a], axis=1)
        prob = expd * (1.0 / jnp.sum(expd, axis=0, keepdims=True))
        dp = dot_nt(av, cots)
        delta = jnp.sum(prob * dp, axis=0, keepdims=True)
        dscore = (prob * (dp - delta)).astype(BF)
        dk = dot_nn(dscore, rows) * SCALE
        dv = dot_nn(prob.astype(BF), cots)
        back = turn_back(dot_tn(dscore, low_ak) * SCALE, cos_v, sin_v)
        unit_vq, scale_vq = unit(queries[j, 0].astype(F32))
        grads[j] = norm_back(back, unit_vq, scale_vq, gains[pl.ds(base + j, 1), :]).astype(BF)
        shared[pl.ds(GAIN_SUMS + j, 1), :] = jnp.sum(back * unit_vq, axis=0, keepdims=True)
        sum_ak = jnp.sum(turn_back(dk, cos_a, sin_a) * unit_ak, axis=0, keepdims=True)
        shared[pl.ds(GAIN_SUMS + 18 + j, 1), :] = sum_ak
        return dk, dv

    def going(step):
        heads = pl.ds(2 * step, 2)
        tiles = [(part.at[:, at + step], part_far.at[:, at + step]) for at in (0, 3)]
        pairs = tiles + [(grads.at[heads], grad_far.at[heads]), (audio.at[heads], audio_far.at[heads])]
        return [pltpu.make_async_copy(near, far, done_out.at[step, at]) for at, (near, far) in enumerate(pairs)]

    def pair(step, carry):
        finish(coming(step))
        found = [one_head(2 * step + e) for e in range(2)]
        for array in range(2):
            left, right = join_rows(found[0][array], found[1][array])
            part[0:16, array * 3 + step] = left.reshape(16, 8, DH).astype(BF)
            part[16:32, array * 3 + step] = right.reshape(16, 8, DH).astype(BF)
        for copy in going(step):
            copy.start()
        return carry

    lax.fori_loop(0, 3, pair, 0)
    finish(units)
    for step in range(3):
        finish(going(step))


def back_kernel(part_far, totals, shared, merged_far, merged, gain_rows, done):
    coming = fetch([(part_far, merged.at[:, 3:9])], done)
    copies = []
    gain_rows[...] = shared[GAIN_SUMS:ALL_ROWS]
    blocks = [jnp.sum(totals[:, at], axis=0) for at in range(3)]
    rows = [blocks[r // 4][r % 4 : r % 4 + 1] for r in range(2 * HALF_HEADS)]
    found = []
    for j in range(HALF_HEADS):
        start = j * HEAD_ROWS
        cos_v, sin_v = shared[COS_V:SIN_V], shared[SIN_V:COS_A]
        cos_a, sin_a = shared[COS_A:SIN_A], shared[SIN_A:GAINS]
        inverse = 1.0 / rows[j]
        delta = rows[HALF_HEADS + j] * inverse
        prob = shared[start + EXPO : start + DPROB] * inverse
        dscore = (prob * (shared[start + DPROB : start + UNIT_AQ] - delta)).astype(BF)
        unit_aq, unit_vk = shared[start + UNIT_AQ : start + UNIT_VK], shared[start + UNIT_VK : start + HEAD_ROWS]
        low_vk = turn(unit_vk, shared[GAIN_VK + j : GAIN_VK + j + 1], cos_v, sin_v)
        low_aq = turn(unit_aq, shared[GAIN_AQ + j : GAIN_AQ + j + 1], cos_a, sin_a)
        dq = dot_tn(dscore, low_vk) * SCALE
        dk = dot_nn(dscore, low_aq) * SCALE
        back = turn_back(dk, cos_v, sin_v)
        gain_rows[6 + j : 7 + j, :] = jnp.sum(back * unit_vk, axis=0, keepdims=True)
        back = turn_back(dq, cos_a, sin_a)
        gain_rows[12 + j : 13 + j, :] = jnp.sum(back * unit_aq, axis=0, keepdims=True)
        found.append(dq)
        if j % 2 == 1:
            left, right = join_rows(found[j - 1], found[j])
            merged[0:16, j // 2] = left.reshape(16, 8, DH).astype(BF)
            merged[16:32, j // 2] = right.reshape(16, 8, DH).astype(BF)
            if j == HALF_HEADS - 1:
                finish(coming)
                copies += fetch([(merged.at[:, 0:9], merged_far.at[:, 0:9])], done.at[1:2])
    for at in range(3):
        spread_tile(merged, 9 + at, gain_rows[8 * at : 8 * at + 8, :])
    copies += fetch([(merged.at[:, 9:12], merged_far.at[:, 9:12])], done.at[2:3])
    finish(copies)


def keys_kernel(
    vlen, raw_vk_far, keys_far, video_far, grad_far, audio_far, totals, gains,
    key_own, value_own, other, raw_vk, keys, tables, audio, mask, sums, done,
):
    copies = fetch(
        (
            (raw_vk_far, raw_vk), (keys_far, keys), (video_far.at[0 : 2 * 2 * DH], tables), (audio_far, audio),
            (grad_far.at[:, DH : 2 * DH], other.at[0]),
        ),
        done,
    )
    core = lax.axis_index("aseq")
    base = heads_of(core)
    mask[0:DH], mask[DH : 2 * DH] = video_mask(vlen, core)
    for at in range(3):
        sums[4 * at : 4 * at + 4, :] = jnp.sum(totals[:, at], axis=0)
    finish(copies)

    def one_head(j, carry):
        cos_v, sin_v = tables[0 : 2 * DH], tables[2 * DH : 4 * DH]
        inverse = 1.0 / sums[pl.ds(j, 1), :]
        delta = sums[pl.ds(HALF_HEADS + j, 1), :] * inverse
        expo = jnp.exp(dot_nt(keys[j, 0], audio[j, 0]) * SCALE) * mask[...]
        prob = expo * inverse
        dscore = (prob * (dot_nt(keys[j, 1], audio[j, 1]) - delta)).astype(BF)
        dk = dot_nn(dscore, audio[j, 0]) * SCALE
        dv = dot_nn(prob.astype(BF), audio[j, 1]).astype(BF)
        unit_vk, scale_vk = unit(raw_vk[j].astype(F32))
        grad = norm_back(turn_back(dk, cos_v, sin_v), unit_vk, scale_vk, gains[pl.ds(H + base + j, 1), :]).astype(BF)
        key_own[j], value_own[j] = grad[:DH], dv[:DH]
        other[1, j], other[2, j] = grad[DH:], dv[DH:]
        return carry

    lax.fori_loop(0, HALF_HEADS, one_head, 0)


def place_kernel(query_own, key_own, value_own, got, grad_vq, grad_vk, grad_vv):
    core = lax.axis_index("aseq")
    for j in range(HALF_HEADS):
        own, other = lanes(heads_of(core) + j), lanes(heads_of(1 - core) + j)
        for at, (mine, grad) in enumerate(((query_own, grad_vq), (key_own, grad_vk), (value_own, grad_vv))):
            grad[:, own] = mine[j, 0:DH]
            grad[:, other] = got[at, j]


def add_peers(got):
    total = got[0].astype(F32)
    for v in range(1, 32):
        total = total + got[v].astype(F32)
    return total


def audio_kernel(
    apos_far, aq_far, ak_far, freqs_far, gains_far, after, got, out, gain_out, apos, aq, ak, freqs, gains, done
):
    copies = fetch(((apos_far, apos), (aq_far, aq), (ak_far, ak), (freqs_far, freqs), (gains_far, gains)), done)
    base = heads_of(lax.axis_index("aseq"))
    acc = add_peers(got)
    gain_out[...] = jnp.broadcast_to(acc[9:12].reshape(1, 24, DH), gain_out.shape)
    finish(copies)
    pos = own_places(apos, lax.broadcasted_iota(jnp.int32, (8, DH), 0) & 3)
    cosine, sine = rotary_tables(pos.astype(F32), freqs[...])
    low = low_rows((8, DH))

    def rows_back(ref, gain_at, grad, at):
        first = base + 2 * at
        rows = jnp.concatenate([ref[0, :, lanes(first + e)].astype(F32) for e in range(2)], axis=0)
        gain = jnp.where(low, gains[pl.ds(gain_at * H + first, 1), :], gains[pl.ds(gain_at * H + first + 1, 1), :])
        unit_rows, scale = unit(rows)
        return norm_back(turn_back(grad, cosine, sine), unit_rows, scale, gain)

    for at in range(3):
        dq = rows_back(aq, 2, acc[at], at)
        dk = rows_back(ak, 3, acc[3 + at], at)
        dv = acc[6 + at]
        left = jnp.where(low, dq, pltpu.roll(dk, 4, 0))
        right = jnp.where(low, pltpu.roll(dq, 4, 0), dk)
        out[:, 2 * at * DH : (2 * at + 1) * DH] = jnp.concatenate([left, dv], axis=0).astype(BF)
        out[:, (2 * at + 1) * DH : (2 * at + 2) * DH] = jnp.concatenate([right, pltpu.roll(dv, 4, 0)], axis=0).astype(BF)


def last_kernel(own, other, gains, grad_aq, grad_ak, grad_av, sum_vq, sum_vk, sum_aq, sum_ak):
    front = lax.axis_index("aseq") == 0
    mine, others = own[...].astype(F32), other[...].astype(F32)
    for at, value in enumerate((jnp.where(front, mine, others), jnp.where(front, others, mine))):
        columns = slice(at * WIDTH, (at + 1) * WIDTH)
        grad_aq[:, columns] = value[0:4].astype(BF)
        grad_ak[:, columns] = value[4:8].astype(BF)
        grad_av[:, columns] = value[8:12].astype(BF)
    for half in range(2):
        total = gains[half]
        for d in range(1, gains.shape[0] // 2):
            total = total + gains[2 * d + half]
        for at, ref in enumerate((sum_vq, sum_vk, sum_aq, sum_ak)):
            ref[6 * half : 6 * half + 6, :] = total[6 * at : 6 * at + 6]


NEAR, FAR = pltpu.VMEM, pltpu.HBM


def call(kernel, name, outs, ins, smem=0, far=0, scratch=()):
    def shape_of(shape, dtype, space=None):
        return jax.ShapeDtypeStruct(shape, dtype) if space is None else space(shape, dtype)

    ins = [pltpu.with_memory_space_constraint(x, FAR) if smem <= at < smem + far else x for at, x in enumerate(ins)]
    return pl.pallas_call(
        kernel,
        name=name,
        out_shape=[shape_of(*out) for out in outs],
        in_specs=[pl.BlockSpec(memory_space=pltpu.SMEM)] * smem
        + [pl.BlockSpec(memory_space=FAR)] * far
        + [pl.BlockSpec(memory_space=NEAR)] * (len(ins) - smem - far),
        out_specs=[pl.BlockSpec(memory_space=FAR if FAR in out else NEAR) for out in outs],
        scratch_shapes=list(scratch),
        compiler_params=pltpu.CompilerParams(vmem_limit_bytes=VMEM_LIMIT),
    )(*ins)


def local(
    video_query, video_key, video_value, video_grad,
    audio_query, audio_key, audio_value, audio_grad,
    video_pos, audio_pos, video_len, audio_len,
    gain_vq, gain_vk, gain_aq, gain_ak,
):
    F = H * DH
    groups = lax.axis_size("vseq")
    clips = lax.axis_size("dp")
    exchange = functools.partial(lax.ppermute, axis_name="aseq", perm=[(0, 1), (1, 0)])
    to_group = functools.partial(lax.all_to_all, axis_name="vseq", split_axis=0, concat_axis=0, tiled=True)
    freqs = frequencies()
    gains = jnp.concatenate([gain_vq, gain_vk, gain_aq, gain_ak]).reshape(4 * H, DH)
    video = [video_query[0], video_key[0], video_value[0], video_grad[0]]
    half = (HALF_HEADS, DH, DH)
    tiles = (groups, 2 * HALF_HEADS, 8, DH)
    six = (HALF_HEADS, 2 * DH, DH)
    queries_shape, keys_shape = (HALF_HEADS, 3, 2 * DH, DH), (HALF_HEADS, 2, 2 * DH, DH)
    own_rows = pltpu.VMEM((1, 4, F), BF)
    places = pltpu.SMEM((1, 4), jnp.int32)
    dmas = lambda count: pltpu.SemaphoreType.DMA((count,))

    (payload,) = call(
        payload_kernel,
        "payload",
        [((groups, 2 * HALF_HEADS + 1, 8, DH), BF)],
        [audio_pos, audio_query, audio_grad, audio_key, audio_value],
        far=5,
        scratch=[places] + [own_rows] * 4 + [dmas(5)],
    )
    gathered = to_group(payload)

    (send,) = call(send_kernel, "send", [((4 * DH + 16, WIDTH), BF)], [*video, video_pos])
    video_got = exchange(send)
    keys_near, queries, keys, raw_vk, unit_vk, video_tables = call(
        video_kernel,
        "video",
        [
            (keys_shape, BF, NEAR), (queries_shape, BF, FAR), (keys_shape, BF, FAR), (six, BF, FAR), (six, F32, FAR),
            ((3, 2 * DH, DH), F32, FAR),
        ],
        [video_len, *video, video_got, video_pos, freqs, gains],
        smem=1,
        scratch=[
            pltpu.VMEM(queries_shape, BF), pltpu.VMEM(six, BF), pltpu.VMEM(six, F32),
            pltpu.VMEM((3, 2 * DH, DH), F32), dmas(5),
        ],
    )

    gathered_shape = (groups, 2 * HALF_HEADS + 1, 8, DH)
    sums, gathered = call(
        scores_kernel,
        "scores",
        [((groups, 3, 4, DH), F32), (gathered_shape, BF, FAR)],
        [audio_len, video_len, gathered, keys_near, freqs, gains],
        smem=2,
        scratch=[pltpu.VMEM((3, DH, DH), F32), pltpu.VMEM((2 * DH, DH), F32), dmas(1)],
    )
    totals = to_group(sums)

    video_tables = video_tables.reshape(6 * DH, DH)
    part_shape, audio_shape = (groups, 6, 8, DH), (HALF_HEADS, 2, DH, DH)
    shared, part, query_grad, audio = call(
        queries_kernel,
        "queries",
        [((ALL_ROWS, DH), F32, NEAR), (part_shape, BF, FAR), (six, BF, FAR), (audio_shape, BF, FAR)],
        [audio_len, video_len, queries, keys, unit_vk, video_tables, gathered, freqs, gains],
        smem=2,
        far=5,
        scratch=[
            pltpu.VMEM(queries_shape, BF), pltpu.VMEM(keys_shape, BF), pltpu.VMEM(gathered_shape, BF),
            pltpu.VMEM((3 * DH, DH), F32), pltpu.VMEM(part_shape, BF), pltpu.VMEM(six, BF),
            pltpu.VMEM(audio_shape, BF), dmas(2 + HALF_HEADS), pltpu.SemaphoreType.DMA((3, 3)), pltpu.SemaphoreType.DMA((3, 4)),
        ],
    )

    (merged,) = call(
        back_kernel,
        "back",
        [(tiles, BF, FAR)],
        [part, totals, shared],
        far=1,
        scratch=[pltpu.VMEM(tiles, BF), pltpu.VMEM((24, DH), F32), dmas(3)],
    )
    got = to_group(merged)

    key_own, value_own, other = call(
        keys_kernel,
        "keys",
        [(half, BF), (half, BF), ((3, *half), BF)],
        [video_len, raw_vk, keys, video_tables, query_grad, audio, totals, gains],
        smem=1,
        far=5,
        scratch=[
            pltpu.VMEM(six, BF), pltpu.VMEM(keys_shape, BF), pltpu.VMEM((4 * DH, DH), F32),
            pltpu.VMEM(audio_shape, BF), pltpu.VMEM((2 * DH, DH), F32), pltpu.VMEM((16, DH), F32), dmas(5),
        ],
    )
    other_got = exchange(other)
    grad_vq, grad_vk, grad_vv = call(
        place_kernel, "place", [((DH, F), BF)] * 3, [query_grad, key_own, value_own, other_got]
    )

    audio_half, gain_rows = call(
        audio_kernel,
        "audio",
        [((16, WIDTH), BF), ((2 * clips, 24, DH), F32)],
        [audio_pos, audio_query, audio_key, freqs, gains, grad_vv, got],
        far=6,
        scratch=[places, own_rows, own_rows, pltpu.VMEM((1, DH), F32), pltpu.VMEM((4 * H, DH), F32), dmas(5)],
    )
    gain_got = lax.all_to_all(gain_rows, ("dp", "aseq"), 0, 0, tiled=True)
    audio_got = exchange(audio_half)
    grad_aq, grad_ak, grad_av, sum_vq, sum_vk, sum_aq, sum_ak = call(
        last_kernel,
        "last",
        [((4, F), BF)] * 3 + [((H, DH), F32)] * 4,
        [audio_half, audio_got, gain_got],
    )
    return (
        grad_vq[None],
        grad_vk[None],
        grad_vv[None],
        grad_aq[None],
        grad_ak[None],
        grad_av[None],
        sum_vq.reshape(F),
        sum_vk.reshape(F),
        sum_aq.reshape(F),
        sum_ak.reshape(F),
    )


def solution(mesh):
    video = P("dp", ("vseq", "aseq"), None)
    audio = P("dp", "vseq", None)
    in_specs = (
        (video,) * 4
        + (audio,) * 4
        + (P("dp", ("vseq", "aseq")), P("dp", "vseq"), P("dp"), P("dp"))
        + (P(),) * 4
    )
    out_specs = (video,) * 3 + (audio,) * 3 + (P(),) * 4
    return jax.shard_map(local, mesh=mesh, in_specs=in_specs, out_specs=out_specs, check_vma=False)
```

time: 119 us -> 116 us (0.975)
  waiting for transfers between devices: 39.6 us -> 36.1 us
  local copies, waits for them, and re-layouts: 1.19 us -> 4.67 us
  starting transfers between devices: 48.5 us -> 46.6 us
    unnamed x24 -> x26, local copies, waits for them, and re-layouts: 1.19 us -> 4.67 us
    all_to_all x1, waiting for transfers between devices: 15.2 us -> 12.1 us  [local(): gathered = to_group(payload)]
    ppermute x1 -> x0, starting transfers between devices: 1.92 us -> none  [local(): pos_got = exchange(video_pos)]
  transfers between devices with their start and end apart: 8 -> 7, of which waited for: 6 -> 7; matrix products, arithmetic and copies ran while one was open for 0% -> 0% of each run, Pallas kernels for 13% -> 14%
where the time goes in v3:
time: 116 us; the launch traced here: 115 us
  starting transfers between devices  46.6 us (40%)
  waiting for transfers between devices  36.1 us (31%)
  Pallas kernels  25.5 us (22%)
  local copies, waits for them, and re-layouts  4.67 us (4%)
  between operations  2.17 us (2%)
    pallas_call x10, Pallas kernels, call(): pl.pallas_call(kernel, name=name, out_shape=[shape_of(*out) for out in ou...  25.5 us
    all_to_all x1, starting transfers between devices, local(): gathered = to_group(payload)  16.5 us
    all_to_all x1, waiting for transfers between devices, local(): got = to_group(merged)  12.6 us
    all_to_all x1, waiting for transfers between devices, local(): gathered = to_group(payload)  12.1 us
    all_to_all x1, starting transfers between devices, local(): totals = to_group(sums)  8.19 us
    all_to_all x1, starting transfers between devices, local(): got = to_group(merged)  7.18 us
    all_to_all x1, starting transfers between devices, local(): gain_got = lax.all_to_all(gain_rows, ('dp', 'aseq'), 0, 0, tiled=True)  5.98 us
    unnamed x26, local copies, waits for them, and re-layouts  4.67 us
  transfers between devices with their start and end apart: 7, of which 7 were waited for; matrix products, arithmetic and copies ran while one was open for 0% of the time, Pallas kernels for 14%

profile of v3, /device:TPU:1, one launch (start us, length us, event | category | flops | bytes accessed | tf_op | source)
XLA Modules:
  0.0 115.1 jit_solution(22182915693172196)
XLA Ops:
  0.6 0.0 copy-start.6
  0.7 0.0 copy-start.8
  0.7 1.9 %payload.1 = bf16[32,13,8,128]{3,2,1,0:T(8,128)(2,1)} custom-call(s32[1,4]{1,0:T(1,128)} %apos_far.3, bf16[1,4,1536]{2,1,0:T(4,128)(2,1)} %aq_far.3, bf16[1,4,1536]{2,1,0:T(4,128)(2,1)} %ac_far.1, bf16[1,4,1536]{2,1,0:T(4,128)(2,1)} %ak_far.3, bf16[1,4,1536]{2,1,0:T(4,128)(2,1)} %av_far.1), custom_call_target="tpu_custom_call" | custom-call | tf_op jit(solution)/shard_map/payload/pallas_call | solution.py:501
  2.6 16.5 %all-to-all-start = ((bf16[32,13,8,128]{3,2,1,0:T(8,128)(2,1)}), bf16[32,13,8,128]{3,2,1,0:T(8,128)(2,1)S(1)}, u32[]{:S(2)}, u32[]{:S(2)}) async-start(bf16[32,13,8,128]{3,2,1,0:T(8,128)(2,1)} %payload.1), calls=%async_computation | async-start | bytes 1703936 | tf_op jit(solution)/shard_map/all_to_all | solution.py:544
  19.1 0.0 copy-start
  19.1 1.0 copy-done
  20.1 1.0 copy-done.1
  21.1 1.0 copy-done.2
  22.1 1.0 copy-done.3
  23.1 0.7 copy-done.7
  23.8 0.1 send.1
  23.8 2.9 %collective-permute-start = (bf16[528,768]{1,0:T(8,128)(2,1)S(1)}, bf16[528,768]{1,0:T(8,128)(2,1)S(1)}, u32[]{:S(2)}, u32[]{:S(2)}) collective-permute-start(bf16[528,768]{1,0:T(8,128)(2,1)S(1)} %send.1), channel_id=1, source_target_pairs={{0,1},{1,0},{2,3},{3,2},{4,5},{5,4},{6,7},{7,6},{8,9},{9,8},{10,11... | collective-permute-start | bytes 2433032 | tf_op jit(solution)/shard_map/ppermute | solution.py:547
  28.0 0.6 collective-permute-done.got
  28.6 4.0 %video.1 = (bf16[6,2,256,128]{3,2,1,0:T(8,128)(2,1)S(1)}, bf16[6,3,256,128]{3,2,1,0:T(8,128)(2,1)}, bf16[6,2,256,128]{3,2,1,0:T(8,128)(2,1)}, bf16[6,256,128]{2,...) custom-call(s32[1]{0:T(128)S(6)} %copy.27.vlen, bf16[128,1536]{1,0:T(8,128)(2,1)S(1)} %bitcast.20, ...), custom_call_target="tpu_custom_call" | custom-call | tf_op jit(solution)/shard_map/video/pallas_call | solution.py:501
  32.7 12.1 %all-to-all-done.gathered = bf16[32,13,8,128]{3,2,1,0:T(8,128)(2,1)S(1)} async-done(((bf16[32,13,8,128]{3,2,1,0:T(8,128)(2,1)}), bf16[32,13,8,128]{3,2,1,0:T(8,128)(2,1)S(1)}, u32[]{:S(2)}, u32[]{:S(2)}) %all-to-all-start) | async-done | bytes 852000 | tf_op jit(solution)/shard_map/all_to_all | solution.py:544
  44.7 2.3 %scores.1 = (f32[32,3,4,128]{3,2,1,0:T(4,128)}, bf16[32,13,8,128]{3,2,1,0:T(8,128)(2,1)}) custom-call(s32[1]{0:T(128)S(6)} %copy.28.alen, s32[1]{0:T(128)S(6)} %copy.27.vlen, bf16[32,13,8,128]{3,2,1,0:T(8,128)(2,1)S(1)} %all-to-all-done.gathered, bf16[6,2,256,128]{3,2,1,0:T(8,128)(2,1)S(1)} %get-tuple-element.41.keys, f32[1,128]{1,0:T(1,128)S(1)} %copy-done.6, ...), custom_call_target="tpu_custom_call" | custom-call | tf_op jit(solution)/shard_map/scores/pallas_call | solution.py:501
  47.0 8.2 %all-to-all-start.1 = ((f32[32,3,4,128]{3,2,1,0:T(4,128)}), f32[32,3,4,128]{3,2,1,0:T(4,128)S(1)}, u32[]{:S(2)}, u32[]{:S(2)}) async-start(f32[32,3,4,128]{3,2,1,0:T(4,128)} %get-tuple-element.46), calls=%async_computation.1 | async-start | bytes 393216 | tf_op jit(solution)/shard_map/all_to_all | solution.py:572
  55.2 6.9 %queries.1 = (f32[6184,128]{1,0:T(8,128)S(1)}, bf16[32,6,8,128]{3,2,1,0:T(8,128)(2,1)}, bf16[6,256,128]{2,1,0:T(8,128)(2,1)}, bf16[6,2,128,128]{3,2,1,0:T(8,128)(2,1)}) custom-call(s32[1]{0:T(128)S(6)} %copy.28.alen, s32[1]{0:T(128)S(6)} %copy.27.vlen, bf16[6,3,256,128]{3,2,1,0:T(8,128)(2,1)} %get-tuple-element.37.queries_far, ...), custom_call_target="tpu_custom_call" | custom-call | tf_op jit(solution)/shard_map/queries/pallas_call | solution.py:501
  62.1 4.6 %all-to-all-done.1.totals = f32[32,3,4,128]{3,2,1,0:T(4,128)S(1)} async-done(((f32[32,3,4,128]{3,2,1,0:T(4,128)}), f32[32,3,4,128]{3,2,1,0:T(4,128)S(1)}, u32[]{:S(2)}, u32[]{:S(2)}) %all-to-all-start.1) | async-done | bytes 196640 | tf_op jit(solution)/shard_map/all_to_all | solution.py:572
  66.7 2.5 %back.1 = bf16[32,12,8,128]{3,2,1,0:T(8,128)(2,1)} custom-call(bf16[32,6,8,128]{3,2,1,0:T(8,128)(2,1)} %get-tuple-element.53.part_far, f32[32,3,4,128]{3,2,1,0:T(4,128)S(1)} %all-to-all-done.1.totals, f32[6184,128]{1,0:T(8,128)S(1)} %get-tuple-element.54.shared), custom_call_target="tpu_custom_call" | custom-call | tf_op jit(solution)/shard_map/back/pallas_call | solution.py:501
  69.2 7.2 %all-to-all-start.2 = ((bf16[32,12,8,128]{3,2,1,0:T(8,128)(2,1)}), bf16[32,12,8,128]{3,2,1,0:T(8,128)(2,1)S(1)}, u32[]{:S(2)}, u32[]{:S(2)}) async-start(bf16[32,12,8,128]{3,2,1,0:T(8,128)(2,1)} %back.1), calls=%async_computation.2 | async-start | bytes 1572864 | tf_op jit(solution)/shard_map/all_to_all | solution.py:598
  76.4 4.5 %keys.1 = (bf16[6,128,128]{2,1,0:T(8,128)(2,1)S(1)}, bf16[6,128,128]{2,1,0:T(8,128)(2,1)S(1)}, bf16[3,6,128,128]{3,2,1,0:T(8,128)(2,1)S(1)}) custom-call(s32[1]{0:T(128)S(6)} %copy.27.vlen, bf16[6,256,128]{2,1,0:T(8,128)(2,1)} %get-tuple-element.44.raw_vk_far, bf16[6,2,256,128]{3,2,1,0:T(8,128)(2,1)} %get-tuple-element.38.keys_far, f32[768,128]{1,0:T(8,128)} %bitcast.28, ...), custom_call_target="tpu_custom_call" | custom-call | tf_op jit(solution)/shard_map/keys/pallas_call | solution.py:501
  80.8 3.9 %collective-permute-start.1 = (bf16[3,6,128,128]{3,2,1,0:T(8,128)(2,1)S(1)}, bf16[3,6,128,128]{3,2,1,0:T(8,128)(2,1)S(1)}, u32[]{:S(2)}, u32[]{:S(2)}) collective-permute-start(bf16[3,6,128,128]{3,2,1,0:T(8,128)(2,1)S(1)} %get-tuple-element.49), channel_id=1, source_target_pairs={{0,1},{1,0},{2,3},{3,2},{4,5},{5,4},{6,7},{7,6},{8,9},{9,8},{10,11... | collective-permute-start | bytes 1769480 | tf_op jit(solution)/shard_map/ppermute | solution.py:612
  84.7 1.6 %collective-permute-done.1.got = bf16[3,6,128,128]{3,2,1,0:T(8,128)(2,1)S(1)} collective-permute-done((bf16[3,6,128,128]{3,2,1,0:T(8,128)(2,1)S(1)}, bf16[3,6,128,128]{3,2,1,0:T(8,128)(2,1)S(1)}, u32[]{:S(2)}, u32[]{:S(2)}) %collective-permute-start.1) | collective-permute-done | bytes 589856 | tf_op jit(solution)/shard_map/ppermute | solution.py:612
  86.3 1.3 %place.1 = (bf16[128,1536]{1,0:T(8,128)(2,1)}, bf16[128,1536]{1,0:T(8,128)(2,1)}, bf16[128,1536]{1,0:T(8,128)(2,1)}) custom-call(bf16[6,256,128]{2,1,0:T(8,128)(2,1)S(1)} %copy-done.4, bf16[6,128,128]{2,1,0:T(8,128)(2,1)S(1)} %get-tuple-element.47.key_own, bf16[6,128,128]{2,1,0:T(8,128)(2,1)S(1)} %get-tuple-element.48.value_own, ...), custom_call_target="tpu_custom_call" | custom-call | tf_op jit(solution)/shard_map/place/pallas_call | solution.py:501
  87.6 12.6 %all-to-all-done.2.got = bf16[32,12,8,128]{3,2,1,0:T(8,128)(2,1)S(1)} async-done(((bf16[32,12,8,128]{3,2,1,0:T(8,128)(2,1)}), bf16[32,12,8,128]{3,2,1,0:T(8,128)(2,1)S(1)}, u32[]{:S(2)}, u32[]{:S(2)}) %all-to-all-start.2) | async-done | bytes 786464 | tf_op jit(solution)/shard_map/all_to_all | solution.py:598
  100.3 1.5 %audio.1 = (bf16[16,768]{1,0:T(8,128)(2,1)S(1)}, f32[16,24,128]{2,1,0:T(8,128)}) custom-call(s32[1,4]{1,0:T(1,128)} %apos_far.3, bf16[1,4,1536]{2,1,0:T(4,128)(2,1)} %aq_far.3, bf16[1,4,1536]{2,1,0:T(4,128)(2,1)} %ak_far.3, f32[1,128]{1,0:T(1,128)} %constant.2.clone.freqs.freqs_far, f32[48,128]{1,0:T(8,128)} %copy-done.5, ...), custom_call_target="tpu_custom_call" | custom-call | tf_op jit(solution)/shard_map/audio/pallas_call | solution.py:501
  101.8 6.0 %all-to-all-start.3 = ((f32[16,24,128]{2,1,0:T(8,128)}), f32[16,24,128]{2,1,0:T(8,128)S(1)}, u32[]{:S(2)}, u32[]{:S(2)}) async-start(f32[16,24,128]{2,1,0:T(8,128)} %get-tuple-element.56), calls=%async_computation.3 | async-start | bytes 393216 | tf_op jit(solution)/shard_map/all_to_all | solution.py:625
  107.8 2.0 %collective-permute-start.2 = (bf16[16,768]{1,0:T(8,128)(2,1)S(1)}, bf16[16,768]{1,0:T(8,128)(2,1)S(1)}, u32[]{:S(2)}, u32[]{:S(2)}) collective-permute-start(bf16[16,768]{1,0:T(8,128)(2,1)S(1)} %get-tuple-element.55.own), channel_id=1, source_target_pairs={{0,1},{1,0},{2,3},{3,2},{4,5},{5,4},{6,7},{7,6},{8,9},{9,8},{10,11... | collective-permute-start | bytes 73736 | tf_op jit(solution)/shard_map/ppermute | solution.py:626
  109.8 1.1 collective-permute-done.2.other
  110.9 3.6 %all-to-all-done.3.gains = f32[16,24,128]{2,1,0:T(8,128)S(1)} async-done(((f32[16,24,128]{2,1,0:T(8,128)}), f32[16,24,128]{2,1,0:T(8,128)S(1)}, u32[]{:S(2)}, u32[]{:S(2)}) %all-to-all-start.3) | async-done | bytes 196640 | tf_op jit(solution)/shard_map/all_to_all | solution.py:625
  114.5 0.6 last.1
  (19 shorter events, 0.0 us)
Async XLA Ops:
  0.6 28.0 %copy-start.6 = (f32[1,128]{1,0:T(1,128)S(1)}, f32[1,128]{1,0:T(1,128)}, u32[]{:S(2)}) copy-start(f32[1,128]{1,0:T(1,128)} %constant.2.clone.freqs.freqs_far) | copy-start | bytes 1540
  0.7 28.0 %copy-start.8 = (s32[1,128]{1,0:T(1,128)S(1)}, s32[1,128]{1,0:T(1,128)}, u32[]{:S(2)}) copy-start(s32[1,128]{1,0:T(1,128)} %pos_own.1) | copy-start | bytes 1540
  0.7 27.3 %copy-start.9 = (f32[1536]{0:T(1024)S(1)}, f32[1536]{0:T(1024)}, u32[]{:S(2)}) copy-start(f32[1536]{0:T(1024)} %param.32) | copy-start | bytes 18436
  0.7 27.3 %copy-start.10 = (f32[1536]{0:T(1024)S(1)}, f32[1536]{0:T(1024)}, u32[]{:S(2)}) copy-start(f32[1536]{0:T(1024)} %param.31) | copy-start | bytes 18436
  0.7 27.3 %copy-start.11 = (f32[1536]{0:T(1024)S(1)}, f32[1536]{0:T(1024)}, u32[]{:S(2)}) copy-start(f32[1536]{0:T(1024)} %param.30) | copy-start | bytes 18436
  0.7 27.3 %copy-start.12 = (f32[1536]{0:T(1024)S(1)}, f32[1536]{0:T(1024)}, u32[]{:S(2)}) copy-start(f32[1536]{0:T(1024)} %param.29) | copy-start | bytes 18436
  2.6 42.1 %all-to-all-start = ((bf16[32,13,8,128]{3,2,1,0:T(8,128)(2,1)}), bf16[32,13,8,128]{3,2,1,0:T(8,128)(2,1)S(1)}, u32[]{:S(2)}, u32[]{:S(2)}) async-start(bf16[32,13,8,128]{3,2,1,0:T(8,128)(2,1)} %payload.1), calls=%async_computation | async-start | bytes 1703936 | tf_op jit(solution)/shard_map/all_to_all | solution.py:544
  19.1 1.0 copy-start
  20.1 1.0 copy-start.1
  21.1 1.0 copy-start.2
  22.1 1.0 copy-start.3
  23.1 0.7 copy-start.7
  23.8 4.8 %collective-permute-start = (bf16[528,768]{1,0:T(8,128)(2,1)S(1)}, bf16[528,768]{1,0:T(8,128)(2,1)S(1)}, u32[]{:S(2)}, u32[]{:S(2)}) collective-permute-start(bf16[528,768]{1,0:T(8,128)(2,1)S(1)} %send.1), channel_id=1, source_target_pairs={{0,1},{1,0},{2,3},{3,2},{4,5},{5,4},{6,7},{7,6},{8,9},{9,8},{10,11... | collective-permute-start | bytes 2433032 | tf_op jit(solution)/shard_map/ppermute | solution.py:547
  28.0 48.3 %copy-start.5 = (f32[48,128]{1,0:T(8,128)}, f32[48,128]{1,0:T(8,128)S(1)}, u32[]{:S(2)}) copy-start(f32[48,128]{1,0:T(8,128)S(1)} %pad_maximum_fusion.gains.gains_far) | copy-start | bytes 73732
  47.0 19.7 %all-to-all-start.1 = ((f32[32,3,4,128]{3,2,1,0:T(4,128)}), f32[32,3,4,128]{3,2,1,0:T(4,128)S(1)}, u32[]{:S(2)}, u32[]{:S(2)}) async-start(f32[32,3,4,128]{3,2,1,0:T(4,128)} %get-tuple-element.46), calls=%async_computation.1 | async-start | bytes 393216 | tf_op jit(solution)/shard_map/all_to_all | solution.py:572
  69.2 17.2 %copy-start.4 = (bf16[6,256,128]{2,1,0:T(8,128)(2,1)S(1)}, bf16[6,256,128]{2,1,0:T(8,128)(2,1)}, u32[]{:S(2)}) copy-start(bf16[6,256,128]{2,1,0:T(8,128)(2,1)} %get-tuple-element.43.grad_far.query_own) | copy-start | bytes 1179652
  69.2 31.1 %all-to-all-start.2 = ((bf16[32,12,8,128]{3,2,1,0:T(8,128)(2,1)}), bf16[32,12,8,128]{3,2,1,0:T(8,128)(2,1)S(1)}, u32[]{:S(2)}, u32[]{:S(2)}) async-start(bf16[32,12,8,128]{3,2,1,0:T(8,128)(2,1)} %back.1), calls=%async_computation.2 | async-start | bytes 1572864 | tf_op jit(solution)/shard_map/all_to_all | solution.py:598
  80.8 5.5 %collective-permute-start.1 = (bf16[3,6,128,128]{3,2,1,0:T(8,128)(2,1)S(1)}, bf16[3,6,128,128]{3,2,1,0:T(8,128)(2,1)S(1)}, u32[]{:S(2)}, u32[]{:S(2)}) collective-permute-start(bf16[3,6,128,128]{3,2,1,0:T(8,128)(2,1)S(1)} %get-tuple-element.49), channel_id=1, source_target_pairs={{0,1},{1,0},{2,3},{3,2},{4,5},{5,4},{6,7},{7,6},{8,9},{9,8},{10,11... | collective-permute-start | bytes 1769480 | tf_op jit(solution)/shard_map/ppermute | solution.py:612
  101.8 12.7 %all-to-all-start.3 = ((f32[16,24,128]{2,1,0:T(8,128)}), f32[16,24,128]{2,1,0:T(8,128)S(1)}, u32[]{:S(2)}, u32[]{:S(2)}) async-start(f32[16,24,128]{2,1,0:T(8,128)} %get-tuple-element.56), calls=%async_computation.3 | async-start | bytes 393216 | tf_op jit(solution)/shard_map/all_to_all | solution.py:625
  107.8 3.1 %collective-permute-start.2 = (bf16[16,768]{1,0:T(8,128)(2,1)S(1)}, bf16[16,768]{1,0:T(8,128)(2,1)S(1)}, u32[]{:S(2)}, u32[]{:S(2)}) collective-permute-start(bf16[16,768]{1,0:T(8,128)(2,1)S(1)} %get-tuple-element.55.own), channel_id=1, source_target_pairs={{0,1},{1,0},{2,3},{3,2},{4,5},{5,4},{6,7},{7,6},{8,9},{9,8},{10,11... | collective-permute-start | bytes 73736 | tf_op jit(solution)/shard_map/ppermute | solution.py:626

commit v4 on v3

--- a/solution.py
+++ b/solution.py
@@ -123,6 +123,19 @@
     return core * HALF_HEADS
 
 
+def side_by_side(steps):
+    steps, results = list(steps), {}
+    running = dict(enumerate(steps))
+    while running:
+        for at in list(running):
+            try:
+                next(running[at])
+            except StopIteration as end:
+                results[at] = end.value
+                del running[at]
+    return [results[at] for at in range(len(steps))]
+
+
 def fetch(pairs, done):
     copies = [pltpu.make_async_copy(far, near, done.at[at]) for at, (far, near) in enumerate(pairs)]
     for copy in copies:
@@ -139,17 +152,22 @@
     out[:, at] = jnp.broadcast_to(rows.astype(BF)[None], (32, 8, DH))
 
 
-def payload_kernel(apos_far, aq_far, ac_far, ak_far, av_far, out, apos, aq, ac, ak, av, done):
+def payload_kernel(apos_far, aq_far, ac_far, ak_far, av_far, out_far, out, apos, aq, ac, ak, av, done, sent):
     finish(fetch(((aq_far, aq), (ac_far, ac), (ak_far, ak), (av_far, av), (apos_far, apos)), done))
     base = heads_of(lax.axis_index("aseq"))
+    inside = lax.broadcasted_iota(jnp.int32, (8, DH), 0) & 3
+    lane = lax.broadcasted_iota(jnp.int32, (8, DH), 1)
+    pos = own_places(apos, inside)
+    spread_tile(out, 2 * HALF_HEADS, jnp.where(lane < HALF, pos >> 6, pos & 63).astype(F32))
+    copies = []
     for j in range(HALF_HEADS):
         columns = lanes(base + j)
         for at, pair in enumerate(((aq, ac), (ak, av))):
             spread_tile(out, 2 * j + at, jnp.concatenate([ref[0, :, columns].astype(F32) for ref in pair], axis=0))
-    inside = lax.broadcasted_iota(jnp.int32, (8, DH), 0) & 3
-    lane = lax.broadcasted_iota(jnp.int32, (8, DH), 1)
-    pos = own_places(apos, inside)
-    spread_tile(out, 2 * HALF_HEADS, jnp.where(lane < HALF, pos >> 6, pos & 63).astype(F32))
+        if j % 2 == 1:
+            tiles = slice(2 * j - 2, 2 * j + 2 + (j == HALF_HEADS - 1))
+            copies += fetch([(out.at[:, tiles], out_far.at[:, tiles])], sent.at[j // 2 : j // 2 + 1])
+    finish(copies)
 
 
 def own_places(apos, inside):
@@ -235,14 +253,23 @@
     base = heads_of(core)
     tables[0], tables[1], tables[2] = audio_tables(gathered, freqs, alen)
     mask[0:DH], mask[DH : 2 * DH] = video_mask(vlen, core)
-    found = []
-    for j in range(HALF_HEADS):
+
+    def one_head(j):
         aq, ac = part_rows(gathered[:, 2 * j].astype(F32).reshape(2 * DH, DH))
+        ac = (ac * tables[2]).astype(BF)
+        yield
         rows, _ = unit(aq)
+        yield
         query = turn(rows, gains[pl.ds(2 * H + base + j, 1), :], tables[0], tables[1])
-        cross = jnp.exp(dot_nt(keys[j, 0], query) * SCALE) * mask[...]
-        dprob = dot_nt(keys[j, 1], (ac * tables[2]).astype(BF))
-        found.append((jnp.sum(cross, axis=0, keepdims=True), jnp.sum(cross * dprob, axis=0, keepdims=True)))
+        yield
+        cross = dot_nt(keys[j, 0], query)
+        dprob = dot_nt(keys[j, 1], ac)
+        yield
+        cross = jnp.exp(cross * SCALE) * mask[...]
+        yield
+        return jnp.sum(cross, axis=0, keepdims=True), jnp.sum(cross * dprob, axis=0, keepdims=True)
+
+    found = side_by_side(one_head(j) for j in range(HALF_HEADS))
     rows = [pair[0] for pair in found] + [pair[1] for pair in found]
     for at in range(3):
         block = jnp.concatenate(rows[4 * at : 4 * at + 4], axis=0)
@@ -307,27 +334,41 @@
         ak, av = part_rows(gathered[:, 2 * j + 1].astype(F32).reshape(2 * DH, DH))
         av = av.astype(BF)
         ac = (ac * mask_a).astype(BF)
+        yield
+        unit_ak, _ = unit(ak)
         unit_aq, _ = unit(aq)
+        unit_vq, scale_vq = unit(queries[j, 0].astype(F32))
+        yield
+        low_ak = turn(unit_ak, gains[pl.ds(3 * H + base + j, 1), :], cos_a, sin_a)
         low_aq = turn(unit_aq, gain_aq, cos_a, sin_a)
-        unit_ak, _ = unit(ak)
-        low_ak = turn(unit_ak, gains[pl.ds(3 * H + base + j, 1), :], cos_a, sin_a)
-        shared[rows_of(j, EXPO, 2 * DH), :] = jnp.exp(dot_nt(keys[j, 0], low_aq) * SCALE) * mask_v
-        shared[rows_of(j, DPROB, 2 * DH), :] = dot_nt(keys[j, 1], ac)
-        shared[rows_of(j, UNIT_AQ, DH), :] = unit_aq
         audio[j, 0] = low_aq
         audio[j, 1] = ac
+        shared[rows_of(j, UNIT_AQ, DH), :] = unit_aq
+        yield
         rows, cots = queries[j, 1], queries[j, 2]
-        expd = jnp.exp(dot_nt(low_ak, rows) * SCALE) * jnp.concatenate([mask_a, mask_a], axis=1)
+        expd = dot_nt(low_ak, rows)
+        dp = dot_nt(av, cots)
+        yield
+        expd = jnp.exp(expd * SCALE) * jnp.concatenate([mask_a, mask_a], axis=1)
         prob = expd * (1.0 / jnp.sum(expd, axis=0, keepdims=True))
-        dp = dot_nt(av, cots)
+        yield
+        cross = dot_nt(keys[j, 0], low_aq)
+        shared[rows_of(j, DPROB, 2 * DH), :] = dot_nt(keys[j, 1], ac)
         delta = jnp.sum(prob * dp, axis=0, keepdims=True)
         dscore = (prob * (dp - delta)).astype(BF)
-        dk = dot_nn(dscore, rows) * SCALE
+        yield
+        dq = dot_tn(dscore, low_ak)
+        dk = dot_nn(dscore, rows)
         dv = dot_nn(prob.astype(BF), cots)
-        back = turn_back(dot_tn(dscore, low_ak) * SCALE, cos_v, sin_v)
-        unit_vq, scale_vq = unit(queries[j, 0].astype(F32))
+        yield
+        shared[rows_of(j, EXPO, 2 * DH), :] = jnp.exp(cross * SCALE) * mask_v
+        yield
+        back = turn_back(dq * SCALE, cos_v, sin_v)
+        dk = dk * SCALE
+        shared[pl.ds(GAIN_SUMS + j, 1), :] = jnp.sum(back * unit_vq, axis=0, keepdims=True)
+        yield
         grads[j] = norm_back(back, unit_vq, scale_vq, gains[pl.ds(base + j, 1), :]).astype(BF)
-        shared[pl.ds(GAIN_SUMS + j, 1), :] = jnp.sum(back * unit_vq, axis=0, keepdims=True)
+        yield
         sum_ak = jnp.sum(turn_back(dk, cos_a, sin_a) * unit_ak, axis=0, keepdims=True)
         shared[pl.ds(GAIN_SUMS + 18 + j, 1), :] = sum_ak
         return dk, dv
@@ -340,7 +381,7 @@
 
     def pair(step, carry):
         finish(coming(step))
-        found = [one_head(2 * step + e) for e in range(2)]
+        found = side_by_side(one_head(2 * step + e) for e in range(2))
         for array in range(2):
             left, right = join_rows(found[0][array], found[1][array])
             part[0:16, array * 3 + step] = left.reshape(16, 8, DH).astype(BF)
@@ -357,36 +398,44 @@
 
 def back_kernel(part_far, totals, shared, merged_far, merged, gain_rows, done):
     coming = fetch([(part_far, merged.at[:, 3:9])], done)
-    copies = []
+    copies, found = [], []
     gain_rows[...] = shared[GAIN_SUMS:ALL_ROWS]
     blocks = [jnp.sum(totals[:, at], axis=0) for at in range(3)]
     rows = [blocks[r // 4][r % 4 : r % 4 + 1] for r in range(2 * HALF_HEADS)]
-    found = []
-    for j in range(HALF_HEADS):
+
+    def one_head(j):
         start = j * HEAD_ROWS
         cos_v, sin_v = shared[COS_V:SIN_V], shared[SIN_V:COS_A]
         cos_a, sin_a = shared[COS_A:SIN_A], shared[SIN_A:GAINS]
+        unit_aq, unit_vk = shared[start + UNIT_AQ : start + UNIT_VK], shared[start + UNIT_VK : start + HEAD_ROWS]
+        low_vk = turn(unit_vk, shared[GAIN_VK + j : GAIN_VK + j + 1], cos_v, sin_v)
+        low_aq = turn(unit_aq, shared[GAIN_AQ + j : GAIN_AQ + j + 1], cos_a, sin_a)
+        yield
         inverse = 1.0 / rows[j]
         delta = rows[HALF_HEADS + j] * inverse
         prob = shared[start + EXPO : start + DPROB] * inverse
         dscore = (prob * (shared[start + DPROB : start + UNIT_AQ] - delta)).astype(BF)
-        unit_aq, unit_vk = shared[start + UNIT_AQ : start + UNIT_VK], shared[start + UNIT_VK : start + HEAD_ROWS]
-        low_vk = turn(unit_vk, shared[GAIN_VK + j : GAIN_VK + j + 1], cos_v, sin_v)
-        low_aq = turn(unit_aq, shared[GAIN_AQ + j : GAIN_AQ + j + 1], cos_a, sin_a)
-        dq = dot_tn(dscore, low_vk) * SCALE
-        dk = dot_nn(dscore, low_aq) * SCALE
-        back = turn_back(dk, cos_v, sin_v)
+        yield
+        dk = dot_nn(dscore, low_aq)
+        dq = dot_tn(dscore, low_vk)
+        yield
+        back = turn_back(dk * SCALE, cos_v, sin_v)
         gain_rows[6 + j : 7 + j, :] = jnp.sum(back * unit_vk, axis=0, keepdims=True)
+        yield
+        dq = dq * SCALE
         back = turn_back(dq, cos_a, sin_a)
         gain_rows[12 + j : 13 + j, :] = jnp.sum(back * unit_aq, axis=0, keepdims=True)
-        found.append(dq)
-        if j % 2 == 1:
-            left, right = join_rows(found[j - 1], found[j])
-            merged[0:16, j // 2] = left.reshape(16, 8, DH).astype(BF)
-            merged[16:32, j // 2] = right.reshape(16, 8, DH).astype(BF)
-            if j == HALF_HEADS - 1:
-                finish(coming)
-                copies += fetch([(merged.at[:, 0:9], merged_far.at[:, 0:9])], done.at[1:2])
+        return dq
+
+    for at in range(2):
+        three = range(3 * at, 3 * at + 3)
+        found += side_by_side(one_head(j) for j in three)
+        for pair in ((0,), (1, 2))[at]:
+            left, right = join_rows(found[2 * pair], found[2 * pair + 1])
+            merged[0:16, pair] = left.reshape(16, 8, DH).astype(BF)
+            merged[16:32, pair] = right.reshape(16, 8, DH).astype(BF)
+    finish(coming)
+    copies += fetch([(merged.at[:, 0:9], merged_far.at[:, 0:9])], done.at[1:2])
     for at in range(3):
         spread_tile(merged, 9 + at, gain_rows[8 * at : 8 * at + 8, :])
     copies += fetch([(merged.at[:, 9:12], merged_far.at[:, 9:12])], done.at[2:3])
@@ -438,20 +487,23 @@
             grad[:, other] = got[at, j]
 
 
-def add_peers(got):
-    total = got[0].astype(F32)
+def add_peers(got, tiles):
+    total = got[0, tiles].astype(F32)
     for v in range(1, 32):
-        total = total + got[v].astype(F32)
+        total = total + got[v, tiles].astype(F32)
     return total
 
 
 def audio_kernel(
-    apos_far, aq_far, ak_far, freqs_far, gains_far, after, got, out, gain_out, apos, aq, ak, freqs, gains, done
+    apos_far, aq_far, ak_far, freqs_far, gains_far, after, got, out, gain_far,
+    apos, aq, ak, freqs, gains, gain_out, done,
 ):
     copies = fetch(((apos_far, apos), (aq_far, aq), (ak_far, ak), (freqs_far, freqs), (gains_far, gains)), done)
     base = heads_of(lax.axis_index("aseq"))
-    acc = add_peers(got)
-    gain_out[...] = jnp.broadcast_to(acc[9:12].reshape(1, 24, DH), gain_out.shape)
+    acc = add_peers(got, slice(9, 12))
+    gain_out[...] = jnp.broadcast_to(acc.reshape(1, 24, DH), gain_out.shape)
+    sent = fetch([(gain_out, gain_far)], done.at[5:6])
+    acc = add_peers(got, slice(0, 9))
     finish(copies)
     pos = own_places(apos, lax.broadcasted_iota(jnp.int32, (8, DH), 0) & 3)
     cosine, sine = rotary_tables(pos.astype(F32), freqs[...])
@@ -472,6 +524,7 @@
         right = jnp.where(low, pltpu.roll(dq, 4, 0), dk)
         out[:, 2 * at * DH : (2 * at + 1) * DH] = jnp.concatenate([left, dv], axis=0).astype(BF)
         out[:, (2 * at + 1) * DH : (2 * at + 2) * DH] = jnp.concatenate([right, pltpu.roll(dv, 4, 0)], axis=0).astype(BF)
+    finish(sent)
 
 
 def last_kernel(own, other, gains, grad_aq, grad_ak, grad_av, sum_vq, sum_vk, sum_aq, sum_ak):
@@ -529,6 +582,7 @@
     tiles = (groups, 2 * HALF_HEADS, 8, DH)
     six = (HALF_HEADS, 2 * DH, DH)
     queries_shape, keys_shape = (HALF_HEADS, 3, 2 * DH, DH), (HALF_HEADS, 2, 2 * DH, DH)
+    gathered_shape = (groups, 2 * HALF_HEADS + 1, 8, DH)
     own_rows = pltpu.VMEM((1, 4, F), BF)
     places = pltpu.SMEM((1, 4), jnp.int32)
     dmas = lambda count: pltpu.SemaphoreType.DMA((count,))
@@ -536,10 +590,10 @@
     (payload,) = call(
         payload_kernel,
         "payload",
-        [((groups, 2 * HALF_HEADS + 1, 8, DH), BF)],
+        [(gathered_shape, BF, FAR)],
         [audio_pos, audio_query, audio_grad, audio_key, audio_value],
         far=5,
-        scratch=[places] + [own_rows] * 4 + [dmas(5)],
+        scratch=[pltpu.VMEM(gathered_shape, BF), places] + [own_rows] * 4 + [dmas(5), dmas(3)],
     )
     gathered = to_group(payload)
 
@@ -560,7 +614,6 @@
         ],
     )
 
-    gathered_shape = (groups, 2 * HALF_HEADS + 1, 8, DH)
     sums, gathered = call(
         scores_kernel,
         "scores",
@@ -617,10 +670,13 @@
     audio_half, gain_rows = call(
         audio_kernel,
         "audio",
-        [((16, WIDTH), BF), ((2 * clips, 24, DH), F32)],
+        [((16, WIDTH), BF), ((2 * clips, 24, DH), F32, FAR)],
         [audio_pos, audio_query, audio_key, freqs, gains, grad_vv, got],
         far=6,
-        scratch=[places, own_rows, own_rows, pltpu.VMEM((1, DH), F32), pltpu.VMEM((4 * H, DH), F32), dmas(5)],
+        scratch=[
+            places, own_rows, own_rows, pltpu.VMEM((1, DH), F32), pltpu.VMEM((4 * H, DH), F32),
+            pltpu.VMEM((2 * clips, 24, DH), F32), dmas(6),
+        ],
     )
     gain_got = lax.all_to_all(gain_rows, ("dp", "aseq"), 0, 0, tiled=True)
     audio_got = exchange(audio_half)

time: 116 us -> 114 us (0.983)
  Pallas kernels: 25.5 us -> 23.9 us
    pallas_call x10, Pallas kernels: 25.5 us -> 23.9 us  [call(): pl.pallas_call(kernel, name=name, out_shape=[shape_of(*out) for out in ou...]
where the time goes in v4:
time: 114 us; the launch traced here: 113 us
  starting transfers between devices  45.9 us (40%)
  waiting for transfers between devices  36.8 us (32%)
  Pallas kernels  23.9 us (21%)
  local copies, waits for them, and re-layouts  4.67 us (4%)
  between operations  2.17 us (2%)
    pallas_call x10, Pallas kernels, call(): pl.pallas_call(kernel, name=name, out_shape=[shape_of(*out) for out in ou...  23.9 us
    all_to_all x1, starting transfers between devices, local(): gathered = to_group(payload)  16.5 us
    all_to_all x1, waiting for transfers between devices, local(): got = to_group(merged)  12.7 us
    all_to_all x1, waiting for transfers between devices, local(): gathered = to_group(payload)  12.1 us
    all_to_all x1, starting transfers between devices, local(): totals = to_group(sums)  8.19 us
    all_to_all x1, starting transfers between devices, local(): got = to_group(merged)  6.51 us
    all_to_all x1, starting transfers between devices, local(): gain_got = lax.all_to_all(gain_rows, ('dp', 'aseq'), 0, 0, tiled=True)  5.89 us
    all_to_all x1, waiting for transfers between devices, local(): totals = to_group(sums)  5.27 us
  transfers between devices with their start and end apart: 7, of which 7 were waited for; matrix products, arithmetic and copies ran while one was open for 0% of the time, Pallas kernels for 14%

profile of v4, /device:TPU:1, one launch (start us, length us, event | category | flops | bytes accessed | tf_op | source)
XLA Modules:
  0.0 113.4 jit_solution(1834452759210911495)
XLA Ops:
  0.6 0.0 copy-start.6
  0.7 0.0 copy-start.8
  0.7 1.8 %payload.1 = bf16[32,13,8,128]{3,2,1,0:T(8,128)(2,1)} custom-call(s32[1,4]{1,0:T(1,128)} %apos_far.3, bf16[1,4,1536]{2,1,0:T(4,128)(2,1)} %aq_far.3, bf16[1,4,1536]{2,1,0:T(4,128)(2,1)} %ac_far.1, bf16[1,4,1536]{2,1,0:T(4,128)(2,1)} %ak_far.3, bf16[1,4,1536]{2,1,0:T(4,128)(2,1)} %av_far.1), custom_call_target="tpu_custom_call" | custom-call | tf_op jit(solution)/shard_map/payload/pallas_call | solution.py:554
  2.6 16.5 %all-to-all-start = ((bf16[32,13,8,128]{3,2,1,0:T(8,128)(2,1)}), bf16[32,13,8,128]{3,2,1,0:T(8,128)(2,1)S(1)}, u32[]{:S(2)}, u32[]{:S(2)}) async-start(bf16[32,13,8,128]{3,2,1,0:T(8,128)(2,1)} %payload.1), calls=%async_computation | async-start | bytes 1703936 | tf_op jit(solution)/shard_map/all_to_all | solution.py:598
  19.1 0.0 copy-start
  19.1 1.0 copy-done
  20.1 1.0 copy-done.1
  21.1 1.0 copy-done.2
  22.1 1.0 copy-done.3
  23.1 0.7 copy-done.7
  23.7 0.1 send.1
  23.8 2.9 %collective-permute-start = (bf16[528,768]{1,0:T(8,128)(2,1)S(1)}, bf16[528,768]{1,0:T(8,128)(2,1)S(1)}, u32[]{:S(2)}, u32[]{:S(2)}) collective-permute-start(bf16[528,768]{1,0:T(8,128)(2,1)S(1)} %send.1), channel_id=1, source_target_pairs={{0,1},{1,0},{2,3},{3,2},{4,5},{5,4},{6,7},{7,6},{8,9},{9,8},{10,11... | collective-permute-start | bytes 2433032 | tf_op jit(solution)/shard_map/ppermute | solution.py:601
  28.0 0.6 collective-permute-done.got
  28.6 4.0 %video.1 = (bf16[6,2,256,128]{3,2,1,0:T(8,128)(2,1)S(1)}, bf16[6,3,256,128]{3,2,1,0:T(8,128)(2,1)}, bf16[6,2,256,128]{3,2,1,0:T(8,128)(2,1)}, bf16[6,256,128]{2,...) custom-call(s32[1]{0:T(128)S(6)} %copy.27.vlen, bf16[128,1536]{1,0:T(8,128)(2,1)S(1)} %bitcast.20, ...), custom_call_target="tpu_custom_call" | custom-call | tf_op jit(solution)/shard_map/video/pallas_call | solution.py:554
  32.6 12.1 %all-to-all-done.gathered = bf16[32,13,8,128]{3,2,1,0:T(8,128)(2,1)S(1)} async-done(((bf16[32,13,8,128]{3,2,1,0:T(8,128)(2,1)}), bf16[32,13,8,128]{3,2,1,0:T(8,128)(2,1)S(1)}, u32[]{:S(2)}, u32[]{:S(2)}) %all-to-all-start) | async-done | bytes 852000 | tf_op jit(solution)/shard_map/all_to_all | solution.py:598
  44.7 2.3 %scores.1 = (f32[32,3,4,128]{3,2,1,0:T(4,128)}, bf16[32,13,8,128]{3,2,1,0:T(8,128)(2,1)}) custom-call(s32[1]{0:T(128)S(6)} %copy.28.alen, s32[1]{0:T(128)S(6)} %copy.27.vlen, bf16[32,13,8,128]{3,2,1,0:T(8,128)(2,1)S(1)} %all-to-all-done.gathered, bf16[6,2,256,128]{3,2,1,0:T(8,128)(2,1)S(1)} %get-tuple-element.41.keys, f32[1,128]{1,0:T(1,128)S(1)} %copy-done.6, ...), custom_call_target="tpu_custom_call" | custom-call | tf_op jit(solution)/shard_map/scores/pallas_call | solution.py:554
  47.0 8.2 %all-to-all-start.1 = ((f32[32,3,4,128]{3,2,1,0:T(4,128)}), f32[32,3,4,128]{3,2,1,0:T(4,128)S(1)}, u32[]{:S(2)}, u32[]{:S(2)}) async-start(f32[32,3,4,128]{3,2,1,0:T(4,128)} %get-tuple-element.46), calls=%async_computation.1 | async-start | bytes 393216 | tf_op jit(solution)/shard_map/all_to_all | solution.py:625
  55.2 6.2 %queries.1 = (f32[6184,128]{1,0:T(8,128)S(1)}, bf16[32,6,8,128]{3,2,1,0:T(8,128)(2,1)}, bf16[6,256,128]{2,1,0:T(8,128)(2,1)}, bf16[6,2,128,128]{3,2,1,0:T(8,128)(2,1)}) custom-call(s32[1]{0:T(128)S(6)} %copy.28.alen, s32[1]{0:T(128)S(6)} %copy.27.vlen, bf16[6,3,256,128]{3,2,1,0:T(8,128)(2,1)} %get-tuple-element.37.queries_far, ...), custom_call_target="tpu_custom_call" | custom-call | tf_op jit(solution)/shard_map/queries/pallas_call | solution.py:554
  61.4 5.3 %all-to-all-done.1.totals = f32[32,3,4,128]{3,2,1,0:T(4,128)S(1)} async-done(((f32[32,3,4,128]{3,2,1,0:T(4,128)}), f32[32,3,4,128]{3,2,1,0:T(4,128)S(1)}, u32[]{:S(2)}, u32[]{:S(2)}) %all-to-all-start.1) | async-done | bytes 196640 | tf_op jit(solution)/shard_map/all_to_all | solution.py:625
  66.7 2.1 %back.1 = bf16[32,12,8,128]{3,2,1,0:T(8,128)(2,1)} custom-call(bf16[32,6,8,128]{3,2,1,0:T(8,128)(2,1)} %get-tuple-element.53.part_far, f32[32,3,4,128]{3,2,1,0:T(4,128)S(1)} %all-to-all-done.1.totals, f32[6184,128]{1,0:T(8,128)S(1)} %get-tuple-element.54.shared), custom_call_target="tpu_custom_call" | custom-call | tf_op jit(solution)/shard_map/back/pallas_call | solution.py:554
  68.8 6.5 %all-to-all-start.2 = ((bf16[32,12,8,128]{3,2,1,0:T(8,128)(2,1)}), bf16[32,12,8,128]{3,2,1,0:T(8,128)(2,1)S(1)}, u32[]{:S(2)}, u32[]{:S(2)}) async-start(bf16[32,12,8,128]{3,2,1,0:T(8,128)(2,1)} %back.1), calls=%async_computation.2 | async-start | bytes 1572864 | tf_op jit(solution)/shard_map/all_to_all | solution.py:651
  75.3 4.5 %keys.1 = (bf16[6,128,128]{2,1,0:T(8,128)(2,1)S(1)}, bf16[6,128,128]{2,1,0:T(8,128)(2,1)S(1)}, bf16[3,6,128,128]{3,2,1,0:T(8,128)(2,1)S(1)}) custom-call(s32[1]{0:T(128)S(6)} %copy.27.vlen, bf16[6,256,128]{2,1,0:T(8,128)(2,1)} %get-tuple-element.44.raw_vk_far, bf16[6,2,256,128]{3,2,1,0:T(8,128)(2,1)} %get-tuple-element.38.keys_far, f32[768,128]{1,0:T(8,128)} %bitcast.28, ...), custom_call_target="tpu_custom_call" | custom-call | tf_op jit(solution)/shard_map/keys/pallas_call | solution.py:554
  79.8 3.9 %collective-permute-start.1 = (bf16[3,6,128,128]{3,2,1,0:T(8,128)(2,1)S(1)}, bf16[3,6,128,128]{3,2,1,0:T(8,128)(2,1)S(1)}, u32[]{:S(2)}, u32[]{:S(2)}) collective-permute-start(bf16[3,6,128,128]{3,2,1,0:T(8,128)(2,1)S(1)} %get-tuple-element.49), channel_id=1, source_target_pairs={{0,1},{1,0},{2,3},{3,2},{4,5},{5,4},{6,7},{7,6},{8,9},{9,8},{10,11... | collective-permute-start | bytes 1769480 | tf_op jit(solution)/shard_map/ppermute | solution.py:665
  83.7 1.6 %collective-permute-done.1.got = bf16[3,6,128,128]{3,2,1,0:T(8,128)(2,1)S(1)} collective-permute-done((bf16[3,6,128,128]{3,2,1,0:T(8,128)(2,1)S(1)}, bf16[3,6,128,128]{3,2,1,0:T(8,128)(2,1)S(1)}, u32[]{:S(2)}, u32[]{:S(2)}) %collective-permute-start.1) | collective-permute-done | bytes 589856 | tf_op jit(solution)/shard_map/ppermute | solution.py:665
  85.3 1.3 %place.1 = (bf16[128,1536]{1,0:T(8,128)(2,1)}, bf16[128,1536]{1,0:T(8,128)(2,1)}, bf16[128,1536]{1,0:T(8,128)(2,1)}) custom-call(bf16[6,256,128]{2,1,0:T(8,128)(2,1)S(1)} %copy-done.4, bf16[6,128,128]{2,1,0:T(8,128)(2,1)S(1)} %get-tuple-element.47.key_own, bf16[6,128,128]{2,1,0:T(8,128)(2,1)S(1)} %get-tuple-element.48.value_own, ...), custom_call_target="tpu_custom_call" | custom-call | tf_op jit(solution)/shard_map/place/pallas_call | solution.py:554
  86.5 12.7 %all-to-all-done.2.got = bf16[32,12,8,128]{3,2,1,0:T(8,128)(2,1)S(1)} async-done(((bf16[32,12,8,128]{3,2,1,0:T(8,128)(2,1)}), bf16[32,12,8,128]{3,2,1,0:T(8,128)(2,1)S(1)}, u32[]{:S(2)}, u32[]{:S(2)}) %all-to-all-start.2) | async-done | bytes 786464 | tf_op jit(solution)/shard_map/all_to_all | solution.py:651
  99.2 1.0 audio.1
  100.2 5.9 %all-to-all-start.3 = ((f32[16,24,128]{2,1,0:T(8,128)}), f32[16,24,128]{2,1,0:T(8,128)S(1)}, u32[]{:S(2)}, u32[]{:S(2)}) async-start(f32[16,24,128]{2,1,0:T(8,128)} %get-tuple-element.56), calls=%async_computation.3 | async-start | bytes 393216 | tf_op jit(solution)/shard_map/all_to_all | solution.py:681
  106.1 2.0 %collective-permute-start.2 = (bf16[16,768]{1,0:T(8,128)(2,1)S(1)}, bf16[16,768]{1,0:T(8,128)(2,1)S(1)}, u32[]{:S(2)}, u32[]{:S(2)}) collective-permute-start(bf16[16,768]{1,0:T(8,128)(2,1)S(1)} %get-tuple-element.55.own), channel_id=1, source_target_pairs={{0,1},{1,0},{2,3},{3,2},{4,5},{5,4},{6,7},{7,6},{8,9},{9,8},{10,11... | collective-permute-start | bytes 73736 | tf_op jit(solution)/shard_map/ppermute | solution.py:682
  108.1 1.1 collective-permute-done.2.other
  109.2 3.6 %all-to-all-done.3.gains = f32[16,24,128]{2,1,0:T(8,128)S(1)} async-done(((f32[16,24,128]{2,1,0:T(8,128)}), f32[16,24,128]{2,1,0:T(8,128)S(1)}, u32[]{:S(2)}, u32[]{:S(2)}) %all-to-all-start.3) | async-done | bytes 196640 | tf_op jit(solution)/shard_map/all_to_all | solution.py:681
  112.8 0.6 last.1
  (19 shorter events, 0.0 us)
Async XLA Ops:
  0.6 28.0 %copy-start.6 = (f32[1,128]{1,0:T(1,128)S(1)}, f32[1,128]{1,0:T(1,128)}, u32[]{:S(2)}) copy-start(f32[1,128]{1,0:T(1,128)} %constant.2.clone.freqs.freqs_far) | copy-start | bytes 1540
  0.7 27.9 %copy-start.8 = (s32[1,128]{1,0:T(1,128)S(1)}, s32[1,128]{1,0:T(1,128)}, u32[]{:S(2)}) copy-start(s32[1,128]{1,0:T(1,128)} %pos_own.1) | copy-start | bytes 1540
  0.7 27.3 %copy-start.9 = (f32[1536]{0:T(1024)S(1)}, f32[1536]{0:T(1024)}, u32[]{:S(2)}) copy-start(f32[1536]{0:T(1024)} %param.32) | copy-start | bytes 18436
  0.7 27.3 %copy-start.10 = (f32[1536]{0:T(1024)S(1)}, f32[1536]{0:T(1024)}, u32[]{:S(2)}) copy-start(f32[1536]{0:T(1024)} %param.31) | copy-start | bytes 18436
  0.7 27.3 %copy-start.11 = (f32[1536]{0:T(1024)S(1)}, f32[1536]{0:T(1024)}, u32[]{:S(2)}) copy-start(f32[1536]{0:T(1024)} %param.30) | copy-start | bytes 18436
  0.7 27.3 %copy-start.12 = (f32[1536]{0:T(1024)S(1)}, f32[1536]{0:T(1024)}, u32[]{:S(2)}) copy-start(f32[1536]{0:T(1024)} %param.29) | copy-start | bytes 18436
  2.6 42.1 %all-to-all-start = ((bf16[32,13,8,128]{3,2,1,0:T(8,128)(2,1)}), bf16[32,13,8,128]{3,2,1,0:T(8,128)(2,1)S(1)}, u32[]{:S(2)}, u32[]{:S(2)}) async-start(bf16[32,13,8,128]{3,2,1,0:T(8,128)(2,1)} %payload.1), calls=%async_computation | async-start | bytes 1703936 | tf_op jit(solution)/shard_map/all_to_all | solution.py:598
  19.1 1.0 copy-start
  20.1 1.0 copy-start.1
  21.1 1.0 copy-start.2
  22.1 1.0 copy-start.3
  23.1 0.7 copy-start.7
  23.8 4.8 %collective-permute-start = (bf16[528,768]{1,0:T(8,128)(2,1)S(1)}, bf16[528,768]{1,0:T(8,128)(2,1)S(1)}, u32[]{:S(2)}, u32[]{:S(2)}) collective-permute-start(bf16[528,768]{1,0:T(8,128)(2,1)S(1)} %send.1), channel_id=1, source_target_pairs={{0,1},{1,0},{2,3},{3,2},{4,5},{5,4},{6,7},{7,6},{8,9},{9,8},{10,11... | collective-permute-start | bytes 2433032 | tf_op jit(solution)/shard_map/ppermute | solution.py:601
  28.0 47.3 %copy-start.5 = (f32[48,128]{1,0:T(8,128)}, f32[48,128]{1,0:T(8,128)S(1)}, u32[]{:S(2)}) copy-start(f32[48,128]{1,0:T(8,128)S(1)} %pad_maximum_fusion.gains.gains_far) | copy-start | bytes 73732
  47.0 19.7 %all-to-all-start.1 = ((f32[32,3,4,128]{3,2,1,0:T(4,128)}), f32[32,3,4,128]{3,2,1,0:T(4,128)S(1)}, u32[]{:S(2)}, u32[]{:S(2)}) async-start(f32[32,3,4,128]{3,2,1,0:T(4,128)} %get-tuple-element.46), calls=%async_computation.1 | async-start | bytes 393216 | tf_op jit(solution)/shard_map/all_to_all | solution.py:625
  68.8 16.5 %copy-start.4 = (bf16[6,256,128]{2,1,0:T(8,128)(2,1)S(1)}, bf16[6,256,128]{2,1,0:T(8,128)(2,1)}, u32[]{:S(2)}) copy-start(bf16[6,256,128]{2,1,0:T(8,128)(2,1)} %get-tuple-element.43.grad_far.query_own) | copy-start | bytes 1179652
  68.8 30.4 %all-to-all-start.2 = ((bf16[32,12,8,128]{3,2,1,0:T(8,128)(2,1)}), bf16[32,12,8,128]{3,2,1,0:T(8,128)(2,1)S(1)}, u32[]{:S(2)}, u32[]{:S(2)}) async-start(bf16[32,12,8,128]{3,2,1,0:T(8,128)(2,1)} %back.1), calls=%async_computation.2 | async-start | bytes 1572864 | tf_op jit(solution)/shard_map/all_to_all | solution.py:651
  79.8 5.5 %collective-permute-start.1 = (bf16[3,6,128,128]{3,2,1,0:T(8,128)(2,1)S(1)}, bf16[3,6,128,128]{3,2,1,0:T(8,128)(2,1)S(1)}, u32[]{:S(2)}, u32[]{:S(2)}) collective-permute-start(bf16[3,6,128,128]{3,2,1,0:T(8,128)(2,1)S(1)} %get-tuple-element.49), channel_id=1, source_target_pairs={{0,1},{1,0},{2,3},{3,2},{4,5},{5,4},{6,7},{7,6},{8,9},{9,8},{10,11... | collective-permute-start | bytes 1769480 | tf_op jit(solution)/shard_map/ppermute | solution.py:665
  100.2 12.6 %all-to-all-start.3 = ((f32[16,24,128]{2,1,0:T(8,128)}), f32[16,24,128]{2,1,0:T(8,128)S(1)}, u32[]{:S(2)}, u32[]{:S(2)}) async-start(f32[16,24,128]{2,1,0:T(8,128)} %get-tuple-element.56), calls=%async_computation.3 | async-start | bytes 393216 | tf_op jit(solution)/shard_map/all_to_all | solution.py:681
  106.1 3.1 %collective-permute-start.2 = (bf16[16,768]{1,0:T(8,128)(2,1)S(1)}, bf16[16,768]{1,0:T(8,128)(2,1)S(1)}, u32[]{:S(2)}, u32[]{:S(2)}) collective-permute-start(bf16[16,768]{1,0:T(8,128)(2,1)S(1)} %get-tuple-element.55.own), channel_id=1, source_target_pairs={{0,1},{1,0},{2,3},{3,2},{4,5},{5,4},{6,7},{7,6},{8,9},{9,8},{10,11... | collective-permute-start | bytes 73736 | tf_op jit(solution)/shard_map/ppermute | solution.py:682

commit v5 on v4

--- a/solution.py
+++ b/solution.py
@@ -68,8 +68,26 @@
     return (scaled * cosine + swap(scaled) * sine).astype(BF)
 
 
+def raw_unit_and_turn(rows, gain, cosine, sine):
+    ones = jnp.ones((DH, DH), BF)
+    squares = rows * rows
+    high = squares.astype(BF)
+    low = (squares - high.astype(F32)).astype(BF)
+    total = dot_nn(high, ones) + dot_nn(low, ones)
+    swapped = swap(rows)
+    yield
+    scale = lax.rsqrt(total * (1.0 / DH) + EPS)
+    turned = scale * (rows * (gain * cosine) + swapped * (swap(gain) * sine))
+    return rows * scale, turned.astype(BF)
+
+
 def turn_back(grad, cosine, sine):
     return grad * cosine - swap(grad) * sine
+
+
+def gain_sum(grad, cosine_part, sine_part):
+    own = jnp.sum(grad * cosine_part, axis=0, keepdims=True)
+    return own + swap(jnp.sum(grad * sine_part, axis=0, keepdims=True))
 
 
 def norm_back(scaled_grad, unit_rows, scale, gain):
@@ -258,9 +276,7 @@
         aq, ac = part_rows(gathered[:, 2 * j].astype(F32).reshape(2 * DH, DH))
         ac = (ac * tables[2]).astype(BF)
         yield
-        rows, _ = unit(aq)
-        yield
-        query = turn(rows, gains[pl.ds(2 * H + base + j, 1), :], tables[0], tables[1])
+        _, query = yield from raw_unit_and_turn(aq, gains[pl.ds(2 * H + base + j, 1), :], tables[0], tables[1])
         yield
         cross = dot_nt(keys[j, 0], query)
         dprob = dot_nt(keys[j, 1], ac)
@@ -336,11 +352,10 @@
         ac = (ac * mask_a).astype(BF)
         yield
         unit_ak, _ = unit(ak)
-        unit_aq, _ = unit(aq)
+        unit_aq, low_aq = yield from raw_unit_and_turn(aq, gain_aq, cos_a, sin_a)
         unit_vq, scale_vq = unit(queries[j, 0].astype(F32))
         yield
         low_ak = turn(unit_ak, gains[pl.ds(3 * H + base + j, 1), :], cos_a, sin_a)
-        low_aq = turn(unit_aq, gain_aq, cos_a, sin_a)
         audio[j, 0] = low_aq
         audio[j, 1] = ac
         shared[rows_of(j, UNIT_AQ, DH), :] = unit_aq
@@ -398,7 +413,7 @@
 
 def back_kernel(part_far, totals, shared, merged_far, merged, gain_rows, done):
     coming = fetch([(part_far, merged.at[:, 3:9])], done)
-    copies, found = [], []
+    copies = []
     gain_rows[...] = shared[GAIN_SUMS:ALL_ROWS]
     blocks = [jnp.sum(totals[:, at], axis=0) for at in range(3)]
     rows = [blocks[r // 4][r % 4 : r % 4 + 1] for r in range(2 * HALF_HEADS)]
@@ -408,8 +423,11 @@
         cos_v, sin_v = shared[COS_V:SIN_V], shared[SIN_V:COS_A]
         cos_a, sin_a = shared[COS_A:SIN_A], shared[SIN_A:GAINS]
         unit_aq, unit_vk = shared[start + UNIT_AQ : start + UNIT_VK], shared[start + UNIT_VK : start + HEAD_ROWS]
-        low_vk = turn(unit_vk, shared[GAIN_VK + j : GAIN_VK + j + 1], cos_v, sin_v)
-        low_aq = turn(unit_aq, shared[GAIN_AQ + j : GAIN_AQ + j + 1], cos_a, sin_a)
+        gain_vk, gain_aq = shared[GAIN_VK + j : GAIN_VK + j + 1], shared[GAIN_AQ + j : GAIN_AQ + j + 1]
+        vk_cos, vk_sin = unit_vk * cos_v, swap(unit_vk) * sin_v
+        aq_cos, aq_sin = unit_aq * cos_a, swap(unit_aq) * sin_a
+        low_vk = (vk_cos * gain_vk + vk_sin * swap(gain_vk)).astype(BF)
+        low_aq = (aq_cos * gain_aq + aq_sin * swap(gain_aq)).astype(BF)
         yield
         inverse = 1.0 / rows[j]
         delta = rows[HALF_HEADS + j] * inverse
@@ -419,21 +437,17 @@
         dk = dot_nn(dscore, low_aq)
         dq = dot_tn(dscore, low_vk)
         yield
-        back = turn_back(dk * SCALE, cos_v, sin_v)
-        gain_rows[6 + j : 7 + j, :] = jnp.sum(back * unit_vk, axis=0, keepdims=True)
+        gain_rows[6 + j : 7 + j, :] = gain_sum(dk, vk_cos, vk_sin) * SCALE
         yield
         dq = dq * SCALE
-        back = turn_back(dq, cos_a, sin_a)
-        gain_rows[12 + j : 13 + j, :] = jnp.sum(back * unit_aq, axis=0, keepdims=True)
+        gain_rows[12 + j : 13 + j, :] = gain_sum(dq, aq_cos, aq_sin)
         return dq
 
-    for at in range(2):
-        three = range(3 * at, 3 * at + 3)
-        found += side_by_side(one_head(j) for j in three)
-        for pair in ((0,), (1, 2))[at]:
-            left, right = join_rows(found[2 * pair], found[2 * pair + 1])
-            merged[0:16, pair] = left.reshape(16, 8, DH).astype(BF)
-            merged[16:32, pair] = right.reshape(16, 8, DH).astype(BF)
+    found = side_by_side(one_head(j) for j in range(HALF_HEADS))
+    for pair in range(3):
+        left, right = join_rows(found[2 * pair], found[2 * pair + 1])
+        merged[0:16, pair] = left.reshape(16, 8, DH).astype(BF)
+        merged[16:32, pair] = right.reshape(16, 8, DH).astype(BF)
     finish(coming)
     copies += fetch([(merged.at[:, 0:9], merged_far.at[:, 0:9])], done.at[1:2])
     for at in range(3):

time: 114 us -> 114 us (level)
  no operation moved by 1% of the time
where the time goes in v5:
time: 114 us; the launch traced here: 113 us
  starting transfers between devices  45.8 us (40%)
  waiting for transfers between devices  36.9 us (32%)
  Pallas kernels  23.2 us (20%)
  local copies, waits for them, and re-layouts  4.67 us (4%)
  between operations  2.17 us (2%)
    pallas_call x10, Pallas kernels, call(): pl.pallas_call(kernel, name=name, out_shape=[shape_of(*out) for out in ou...  23.2 us
    all_to_all x1, starting transfers between devices, local(): gathered = to_group(payload)  16.5 us
    all_to_all x1, waiting for transfers between devices, local(): got = to_group(merged)  12.6 us
    all_to_all x1, waiting for transfers between devices, local(): gathered = to_group(payload)  12.1 us
    all_to_all x1, starting transfers between devices, local(): totals = to_group(sums)  8.2 us
    all_to_all x1, starting transfers between devices, local(): got = to_group(merged)  6.43 us
    all_to_all x1, starting transfers between devices, local(): gain_got = lax.all_to_all(gain_rows, ('dp', 'aseq'), 0, 0, tiled=True)  5.9 us
    all_to_all x1, waiting for transfers between devices, local(): totals = to_group(sums)  5.35 us
  transfers between devices with their start and end apart: 7, of which 7 were waited for; matrix products, arithmetic and copies ran while one was open for 0% of the time, Pallas kernels for 14%

profile of v5, /device:TPU:1, one launch (start us, length us, event | category | flops | bytes accessed | tf_op | source)
XLA Modules:
  0.0 112.7 jit_solution(15039852796803050184)
XLA Ops:
  0.6 0.0 copy-start.6
  0.7 0.0 copy-start.8
  0.7 1.8 %payload.1 = bf16[32,13,8,128]{3,2,1,0:T(8,128)(2,1)} custom-call(s32[1,4]{1,0:T(1,128)} %apos_far.3, bf16[1,4,1536]{2,1,0:T(4,128)(2,1)} %aq_far.3, bf16[1,4,1536]{2,1,0:T(4,128)(2,1)} %ac_far.1, bf16[1,4,1536]{2,1,0:T(4,128)(2,1)} %ak_far.3, bf16[1,4,1536]{2,1,0:T(4,128)(2,1)} %av_far.1), custom_call_target="tpu_custom_call" | custom-call | tf_op jit(solution)/shard_map/payload/pallas_call | solution.py:568
  2.6 16.5 %all-to-all-start = ((bf16[32,13,8,128]{3,2,1,0:T(8,128)(2,1)}), bf16[32,13,8,128]{3,2,1,0:T(8,128)(2,1)S(1)}, u32[]{:S(2)}, u32[]{:S(2)}) async-start(bf16[32,13,8,128]{3,2,1,0:T(8,128)(2,1)} %payload.1), calls=%async_computation | async-start | bytes 1703936 | tf_op jit(solution)/shard_map/all_to_all | solution.py:612
  19.1 0.0 copy-start
  19.1 1.0 copy-done
  20.1 1.0 copy-done.1
  21.1 1.0 copy-done.2
  22.1 1.0 copy-done.3
  23.1 0.7 copy-done.7
  23.7 0.1 send.1
  23.8 2.9 %collective-permute-start = (bf16[528,768]{1,0:T(8,128)(2,1)S(1)}, bf16[528,768]{1,0:T(8,128)(2,1)S(1)}, u32[]{:S(2)}, u32[]{:S(2)}) collective-permute-start(bf16[528,768]{1,0:T(8,128)(2,1)S(1)} %send.1), channel_id=1, source_target_pairs={{0,1},{1,0},{2,3},{3,2},{4,5},{5,4},{6,7},{7,6},{8,9},{9,8},{10,11... | collective-permute-start | bytes 2433032 | tf_op jit(solution)/shard_map/ppermute | solution.py:615
  28.0 0.6 collective-permute-done.got
  28.6 4.0 %video.1 = (bf16[6,2,256,128]{3,2,1,0:T(8,128)(2,1)S(1)}, bf16[6,3,256,128]{3,2,1,0:T(8,128)(2,1)}, bf16[6,2,256,128]{3,2,1,0:T(8,128)(2,1)}, bf16[6,256,128]{2,...) custom-call(s32[1]{0:T(128)S(6)} %copy.27.vlen, bf16[128,1536]{1,0:T(8,128)(2,1)S(1)} %bitcast.20, ...), custom_call_target="tpu_custom_call" | custom-call | tf_op jit(solution)/shard_map/video/pallas_call | solution.py:568
  32.6 12.1 %all-to-all-done.gathered = bf16[32,13,8,128]{3,2,1,0:T(8,128)(2,1)S(1)} async-done(((bf16[32,13,8,128]{3,2,1,0:T(8,128)(2,1)}), bf16[32,13,8,128]{3,2,1,0:T(8,128)(2,1)S(1)}, u32[]{:S(2)}, u32[]{:S(2)}) %all-to-all-start) | async-done | bytes 852000 | tf_op jit(solution)/shard_map/all_to_all | solution.py:612
  44.7 1.7 %scores.1 = (f32[32,3,4,128]{3,2,1,0:T(4,128)}, bf16[32,13,8,128]{3,2,1,0:T(8,128)(2,1)}) custom-call(s32[1]{0:T(128)S(6)} %copy.28.alen, s32[1]{0:T(128)S(6)} %copy.27.vlen, bf16[32,13,8,128]{3,2,1,0:T(8,128)(2,1)S(1)} %all-to-all-done.gathered, bf16[6,2,256,128]{3,2,1,0:T(8,128)(2,1)S(1)} %get-tuple-element.41.keys, f32[1,128]{1,0:T(1,128)S(1)} %copy-done.6, ...), custom_call_target="tpu_custom_call" | custom-call | tf_op jit(solution)/shard_map/scores/pallas_call | solution.py:568
  46.4 8.2 %all-to-all-start.1 = ((f32[32,3,4,128]{3,2,1,0:T(4,128)}), f32[32,3,4,128]{3,2,1,0:T(4,128)S(1)}, u32[]{:S(2)}, u32[]{:S(2)}) async-start(f32[32,3,4,128]{3,2,1,0:T(4,128)} %get-tuple-element.46), calls=%async_computation.1 | async-start | bytes 393216 | tf_op jit(solution)/shard_map/all_to_all | solution.py:639
  54.6 6.1 %queries.1 = (f32[6184,128]{1,0:T(8,128)S(1)}, bf16[32,6,8,128]{3,2,1,0:T(8,128)(2,1)}, bf16[6,256,128]{2,1,0:T(8,128)(2,1)}, bf16[6,2,128,128]{3,2,1,0:T(8,128)(2,1)}) custom-call(s32[1]{0:T(128)S(6)} %copy.28.alen, s32[1]{0:T(128)S(6)} %copy.27.vlen, bf16[6,3,256,128]{3,2,1,0:T(8,128)(2,1)} %get-tuple-element.37.queries_far, ...), custom_call_target="tpu_custom_call" | custom-call | tf_op jit(solution)/shard_map/queries/pallas_call | solution.py:568
  60.8 5.3 %all-to-all-done.1.totals = f32[32,3,4,128]{3,2,1,0:T(4,128)S(1)} async-done(((f32[32,3,4,128]{3,2,1,0:T(4,128)}), f32[32,3,4,128]{3,2,1,0:T(4,128)S(1)}, u32[]{:S(2)}, u32[]{:S(2)}) %all-to-all-start.1) | async-done | bytes 196640 | tf_op jit(solution)/shard_map/all_to_all | solution.py:639
  66.1 2.0 %back.1 = bf16[32,12,8,128]{3,2,1,0:T(8,128)(2,1)} custom-call(bf16[32,6,8,128]{3,2,1,0:T(8,128)(2,1)} %get-tuple-element.53.part_far, f32[32,3,4,128]{3,2,1,0:T(4,128)S(1)} %all-to-all-done.1.totals, f32[6184,128]{1,0:T(8,128)S(1)} %get-tuple-element.54.shared), custom_call_target="tpu_custom_call" | custom-call | tf_op jit(solution)/shard_map/back/pallas_call | solution.py:568
  68.1 6.4 %all-to-all-start.2 = ((bf16[32,12,8,128]{3,2,1,0:T(8,128)(2,1)}), bf16[32,12,8,128]{3,2,1,0:T(8,128)(2,1)S(1)}, u32[]{:S(2)}, u32[]{:S(2)}) async-start(bf16[32,12,8,128]{3,2,1,0:T(8,128)(2,1)} %back.1), calls=%async_computation.2 | async-start | bytes 1572864 | tf_op jit(solution)/shard_map/all_to_all | solution.py:665
  74.6 4.5 %keys.1 = (bf16[6,128,128]{2,1,0:T(8,128)(2,1)S(1)}, bf16[6,128,128]{2,1,0:T(8,128)(2,1)S(1)}, bf16[3,6,128,128]{3,2,1,0:T(8,128)(2,1)S(1)}) custom-call(s32[1]{0:T(128)S(6)} %copy.27.vlen, bf16[6,256,128]{2,1,0:T(8,128)(2,1)} %get-tuple-element.44.raw_vk_far, bf16[6,2,256,128]{3,2,1,0:T(8,128)(2,1)} %get-tuple-element.38.keys_far, f32[768,128]{1,0:T(8,128)} %bitcast.28, ...), custom_call_target="tpu_custom_call" | custom-call | tf_op jit(solution)/shard_map/keys/pallas_call | solution.py:568
  79.0 3.9 %collective-permute-start.1 = (bf16[3,6,128,128]{3,2,1,0:T(8,128)(2,1)S(1)}, bf16[3,6,128,128]{3,2,1,0:T(8,128)(2,1)S(1)}, u32[]{:S(2)}, u32[]{:S(2)}) collective-permute-start(bf16[3,6,128,128]{3,2,1,0:T(8,128)(2,1)S(1)} %get-tuple-element.49), channel_id=1, source_target_pairs={{0,1},{1,0},{2,3},{3,2},{4,5},{5,4},{6,7},{7,6},{8,9},{9,8},{10,11... | collective-permute-start | bytes 1769480 | tf_op jit(solution)/shard_map/ppermute | solution.py:679
  82.9 1.6 %collective-permute-done.1.got = bf16[3,6,128,128]{3,2,1,0:T(8,128)(2,1)S(1)} collective-permute-done((bf16[3,6,128,128]{3,2,1,0:T(8,128)(2,1)S(1)}, bf16[3,6,128,128]{3,2,1,0:T(8,128)(2,1)S(1)}, u32[]{:S(2)}, u32[]{:S(2)}) %collective-permute-start.1) | collective-permute-done | bytes 589856 | tf_op jit(solution)/shard_map/ppermute | solution.py:679
  84.5 1.3 %place.1 = (bf16[128,1536]{1,0:T(8,128)(2,1)}, bf16[128,1536]{1,0:T(8,128)(2,1)}, bf16[128,1536]{1,0:T(8,128)(2,1)}) custom-call(bf16[6,256,128]{2,1,0:T(8,128)(2,1)S(1)} %copy-done.4, bf16[6,128,128]{2,1,0:T(8,128)(2,1)S(1)} %get-tuple-element.47.key_own, bf16[6,128,128]{2,1,0:T(8,128)(2,1)S(1)} %get-tuple-element.48.value_own, ...), custom_call_target="tpu_custom_call" | custom-call | tf_op jit(solution)/shard_map/place/pallas_call | solution.py:568
  85.8 12.6 %all-to-all-done.2.got = bf16[32,12,8,128]{3,2,1,0:T(8,128)(2,1)S(1)} async-done(((bf16[32,12,8,128]{3,2,1,0:T(8,128)(2,1)}), bf16[32,12,8,128]{3,2,1,0:T(8,128)(2,1)S(1)}, u32[]{:S(2)}, u32[]{:S(2)}) %all-to-all-start.2) | async-done | bytes 786464 | tf_op jit(solution)/shard_map/all_to_all | solution.py:665
  98.4 1.0 audio.1
  99.5 5.9 %all-to-all-start.3 = ((f32[16,24,128]{2,1,0:T(8,128)}), f32[16,24,128]{2,1,0:T(8,128)S(1)}, u32[]{:S(2)}, u32[]{:S(2)}) async-start(f32[16,24,128]{2,1,0:T(8,128)} %get-tuple-element.56), calls=%async_computation.3 | async-start | bytes 393216 | tf_op jit(solution)/shard_map/all_to_all | solution.py:695
  105.4 2.0 %collective-permute-start.2 = (bf16[16,768]{1,0:T(8,128)(2,1)S(1)}, bf16[16,768]{1,0:T(8,128)(2,1)S(1)}, u32[]{:S(2)}, u32[]{:S(2)}) collective-permute-start(bf16[16,768]{1,0:T(8,128)(2,1)S(1)} %get-tuple-element.55.own), channel_id=1, source_target_pairs={{0,1},{1,0},{2,3},{3,2},{4,5},{5,4},{6,7},{7,6},{8,9},{9,8},{10,11... | collective-permute-start | bytes 73736 | tf_op jit(solution)/shard_map/ppermute | solution.py:696
  107.4 1.1 collective-permute-done.2.other
  108.4 3.6 %all-to-all-done.3.gains = f32[16,24,128]{2,1,0:T(8,128)S(1)} async-done(((f32[16,24,128]{2,1,0:T(8,128)}), f32[16,24,128]{2,1,0:T(8,128)S(1)}, u32[]{:S(2)}, u32[]{:S(2)}) %all-to-all-start.3) | async-done | bytes 196640 | tf_op jit(solution)/shard_map/all_to_all | solution.py:695
  112.1 0.6 last.1
  (19 shorter events, 0.0 us)
Async XLA Ops:
  0.6 28.0 %copy-start.6 = (f32[1,128]{1,0:T(1,128)S(1)}, f32[1,128]{1,0:T(1,128)}, u32[]{:S(2)}) copy-start(f32[1,128]{1,0:T(1,128)} %constant.2.clone.freqs.freqs_far) | copy-start | bytes 1540
  0.7 27.9 %copy-start.8 = (s32[1,128]{1,0:T(1,128)S(1)}, s32[1,128]{1,0:T(1,128)}, u32[]{:S(2)}) copy-start(s32[1,128]{1,0:T(1,128)} %pos_own.1) | copy-start | bytes 1540
  0.7 27.3 %copy-start.9 = (f32[1536]{0:T(1024)S(1)}, f32[1536]{0:T(1024)}, u32[]{:S(2)}) copy-start(f32[1536]{0:T(1024)} %param.32) | copy-start | bytes 18436
  0.7 27.3 %copy-start.10 = (f32[1536]{0:T(1024)S(1)}, f32[1536]{0:T(1024)}, u32[]{:S(2)}) copy-start(f32[1536]{0:T(1024)} %param.31) | copy-start | bytes 18436
  0.7 27.3 %copy-start.11 = (f32[1536]{0:T(1024)S(1)}, f32[1536]{0:T(1024)}, u32[]{:S(2)}) copy-start(f32[1536]{0:T(1024)} %param.30) | copy-start | bytes 18436
  0.7 27.3 %copy-start.12 = (f32[1536]{0:T(1024)S(1)}, f32[1536]{0:T(1024)}, u32[]{:S(2)}) copy-start(f32[1536]{0:T(1024)} %param.29) | copy-start | bytes 18436
  2.6 42.1 %all-to-all-start = ((bf16[32,13,8,128]{3,2,1,0:T(8,128)(2,1)}), bf16[32,13,8,128]{3,2,1,0:T(8,128)(2,1)S(1)}, u32[]{:S(2)}, u32[]{:S(2)}) async-start(bf16[32,13,8,128]{3,2,1,0:T(8,128)(2,1)} %payload.1), calls=%async_computation | async-start | bytes 1703936 | tf_op jit(solution)/shard_map/all_to_all | solution.py:612
  19.1 1.0 copy-start
  20.1 1.0 copy-start.1
  21.1 1.0 copy-start.2
  22.1 1.0 copy-start.3
  23.1 0.7 copy-start.7
  23.8 4.8 %collective-permute-start = (bf16[528,768]{1,0:T(8,128)(2,1)S(1)}, bf16[528,768]{1,0:T(8,128)(2,1)S(1)}, u32[]{:S(2)}, u32[]{:S(2)}) collective-permute-start(bf16[528,768]{1,0:T(8,128)(2,1)S(1)} %send.1), channel_id=1, source_target_pairs={{0,1},{1,0},{2,3},{3,2},{4,5},{5,4},{6,7},{7,6},{8,9},{9,8},{10,11... | collective-permute-start | bytes 2433032 | tf_op jit(solution)/shard_map/ppermute | solution.py:615
  28.0 46.5 %copy-start.5 = (f32[48,128]{1,0:T(8,128)}, f32[48,128]{1,0:T(8,128)S(1)}, u32[]{:S(2)}) copy-start(f32[48,128]{1,0:T(8,128)S(1)} %pad_maximum_fusion.gains.gains_far) | copy-start | bytes 73732
  46.4 19.7 %all-to-all-start.1 = ((f32[32,3,4,128]{3,2,1,0:T(4,128)}), f32[32,3,4,128]{3,2,1,0:T(4,128)S(1)}, u32[]{:S(2)}, u32[]{:S(2)}) async-start(f32[32,3,4,128]{3,2,1,0:T(4,128)} %get-tuple-element.46), calls=%async_computation.1 | async-start | bytes 393216 | tf_op jit(solution)/shard_map/all_to_all | solution.py:639
  68.1 16.4 %copy-start.4 = (bf16[6,256,128]{2,1,0:T(8,128)(2,1)S(1)}, bf16[6,256,128]{2,1,0:T(8,128)(2,1)}, u32[]{:S(2)}) copy-start(bf16[6,256,128]{2,1,0:T(8,128)(2,1)} %get-tuple-element.43.grad_far.query_own) | copy-start | bytes 1179652
  68.1 30.3 %all-to-all-start.2 = ((bf16[32,12,8,128]{3,2,1,0:T(8,128)(2,1)}), bf16[32,12,8,128]{3,2,1,0:T(8,128)(2,1)S(1)}, u32[]{:S(2)}, u32[]{:S(2)}) async-start(bf16[32,12,8,128]{3,2,1,0:T(8,128)(2,1)} %back.1), calls=%async_computation.2 | async-start | bytes 1572864 | tf_op jit(solution)/shard_map/all_to_all | solution.py:665
  79.0 5.5 %collective-permute-start.1 = (bf16[3,6,128,128]{3,2,1,0:T(8,128)(2,1)S(1)}, bf16[3,6,128,128]{3,2,1,0:T(8,128)(2,1)S(1)}, u32[]{:S(2)}, u32[]{:S(2)}) collective-permute-start(bf16[3,6,128,128]{3,2,1,0:T(8,128)(2,1)S(1)} %get-tuple-element.49), channel_id=1, source_target_pairs={{0,1},{1,0},{2,3},{3,2},{4,5},{5,4},{6,7},{7,6},{8,9},{9,8},{10,11... | collective-permute-start | bytes 1769480 | tf_op jit(solution)/shard_map/ppermute | solution.py:679
  99.5 12.6 %all-to-all-start.3 = ((f32[16,24,128]{2,1,0:T(8,128)}), f32[16,24,128]{2,1,0:T(8,128)S(1)}, u32[]{:S(2)}, u32[]{:S(2)}) async-start(f32[16,24,128]{2,1,0:T(8,128)} %get-tuple-element.56), calls=%async_computation.3 | async-start | bytes 393216 | tf_op jit(solution)/shard_map/all_to_all | solution.py:695
  105.4 3.1 %collective-permute-start.2 = (bf16[16,768]{1,0:T(8,128)(2,1)S(1)}, bf16[16,768]{1,0:T(8,128)(2,1)S(1)}, u32[]{:S(2)}, u32[]{:S(2)}) collective-permute-start(bf16[16,768]{1,0:T(8,128)(2,1)S(1)} %get-tuple-element.55.own), channel_id=1, source_target_pairs={{0,1},{1,0},{2,3},{3,2},{4,5},{5,4},{6,7},{7,6},{8,9},{9,8},{10,11... | collective-permute-start | bytes 73736 | tf_op jit(solution)/shard_map/ppermute | solution.py:696

commit v6 on v5

--- a/solution.py
+++ b/solution.py
@@ -20,6 +20,9 @@
 HALF_HEADS = H // 2
 WIDTH = HALF_HEADS * DH
 
+PLACES_Z, PLACES_Y = 8, 4
+ORDER = [PLACES_Y * (p % PLACES_Z) + p // PLACES_Z for p in range(PLACES_Z * PLACES_Y)]
+
 
 def frequencies():
     freqs = np.power(np.float64(THETA), -(np.arange(HALF, dtype=np.float64) / HALF))
@@ -117,8 +120,8 @@
 
 def audio_index():
     row = lax.broadcasted_iota(jnp.int32, (DH, DH), 0)
-    inside = row & 7
-    return jnp.where(inside < 4, 0, 60) + (row >> 3) * 4 + inside
+    at = (row >> 3) + jnp.where((row & 7) < 4, 0, 16)
+    return (PLACES_Y * (at & (PLACES_Z - 1)) + (at >> 3)) * 4 + (row & 3)
 
 
 def dot_nt(a, b):
@@ -588,7 +591,9 @@
     groups = lax.axis_size("vseq")
     clips = lax.axis_size("dp")
     exchange = functools.partial(lax.ppermute, axis_name="aseq", perm=[(0, 1), (1, 0)])
-    to_group = functools.partial(lax.all_to_all, axis_name="vseq", split_axis=0, concat_axis=0, tiled=True)
+    to_group = functools.partial(
+        lax.all_to_all, axis_name="vseq", split_axis=0, concat_axis=0, axis_index_groups=[ORDER], tiled=True
+    )
     freqs = frequencies()
     gains = jnp.concatenate([gain_vq, gain_vk, gain_aq, gain_ak]).reshape(4 * H, DH)
     video = [video_query[0], video_key[0], video_value[0], video_grad[0]]

time: 114 us -> 114 us (level)
  starting transfers between devices: 45.8 us -> 44.5 us
  waiting for transfers between devices: 36.9 us -> 38.1 us
    all_to_all x1, waiting for transfers between devices: 12.6 us -> 13.9 us  [local(): got = to_group(merged)]
where the time goes in v6:
time: 114 us; the launch traced here: 113 us
  starting transfers between devices  44.5 us (39%)
  waiting for transfers between devices  38.1 us (33%)
  Pallas kernels  23.1 us (20%)
  local copies, waits for them, and re-layouts  4.67 us (4%)
  between operations  2.17 us (2%)
    pallas_call x10, Pallas kernels, call(): pl.pallas_call(kernel, name=name, out_shape=[shape_of(*out) for out in ou...  23.1 us
    all_to_all x1, starting transfers between devices, local(): gathered = to_group(payload)  16.5 us
    all_to_all x1, waiting for transfers between devices, local(): got = to_group(merged)  13.9 us
    all_to_all x1, waiting for transfers between devices, local(): gathered = to_group(payload)  11.8 us
    all_to_all x1, starting transfers between devices, local(): totals = to_group(sums)  7.82 us
    all_to_all x1, starting transfers between devices, local(): got = to_group(merged)  6.19 us
    all_to_all x1, waiting for transfers between devices, local(): totals = to_group(sums)  5.59 us
    all_to_all x1, starting transfers between devices, local(): gain_got = lax.all_to_all(gain_rows, ('dp', 'aseq'), 0, 0, tiled=True)  5.41 us
  transfers between devices with their start and end apart: 7, of which 7 were waited for; matrix products, arithmetic and copies ran while one was open for 0% of the time, Pallas kernels for 14%

profile of v6, /device:TPU:1, one launch (start us, length us, event | category | flops | bytes accessed | tf_op | source)
XLA Modules:
  0.0 112.6 jit_solution(14462455656213982903)
XLA Ops:
  0.6 0.0 copy-start.6
  0.7 0.0 copy-start.8
  0.7 1.8 %payload.1 = bf16[32,13,8,128]{3,2,1,0:T(8,128)(2,1)} custom-call(s32[1,4]{1,0:T(1,128)} %apos_far.3, bf16[1,4,1536]{2,1,0:T(4,128)(2,1)} %aq_far.3, bf16[1,4,1536]{2,1,0:T(4,128)(2,1)} %ac_far.1, bf16[1,4,1536]{2,1,0:T(4,128)(2,1)} %ak_far.3, bf16[1,4,1536]{2,1,0:T(4,128)(2,1)} %av_far.1), custom_call_target="tpu_custom_call" | custom-call | tf_op jit(solution)/shard_map/payload/pallas_call | solution.py:571
  2.6 16.5 %all-to-all-start = ((bf16[32,13,8,128]{3,2,1,0:T(8,128)(2,1)}), bf16[32,13,8,128]{3,2,1,0:T(8,128)(2,1)S(1)}, u32[]{:S(2)}, u32[]{:S(2)}) async-start(bf16[32,13,8,128]{3,2,1,0:T(8,128)(2,1)} %payload.1), calls=%async_computation | async-start | bytes 1703936 | tf_op jit(solution)/shard_map/all_to_all | solution.py:617
  19.1 0.0 copy-start
  19.1 1.0 copy-done
  20.1 1.0 copy-done.1
  21.1 1.0 copy-done.2
  22.1 1.0 copy-done.3
  23.1 0.7 copy-done.7
  23.7 0.1 send.1
  23.8 2.9 %collective-permute-start = (bf16[528,768]{1,0:T(8,128)(2,1)S(1)}, bf16[528,768]{1,0:T(8,128)(2,1)S(1)}, u32[]{:S(2)}, u32[]{:S(2)}) collective-permute-start(bf16[528,768]{1,0:T(8,128)(2,1)S(1)} %send.1), channel_id=1, source_target_pairs={{0,1},{1,0},{2,3},{3,2},{4,5},{5,4},{6,7},{7,6},{8,9},{9,8},{10,11... | collective-permute-start | bytes 2433032 | tf_op jit(solution)/shard_map/ppermute | solution.py:620
  28.0 0.6 collective-permute-done.got
  28.6 4.0 %video.1 = (bf16[6,2,256,128]{3,2,1,0:T(8,128)(2,1)S(1)}, bf16[6,3,256,128]{3,2,1,0:T(8,128)(2,1)}, bf16[6,2,256,128]{3,2,1,0:T(8,128)(2,1)}, bf16[6,256,128]{2,...) custom-call(s32[1]{0:T(128)S(6)} %copy.27.vlen, bf16[128,1536]{1,0:T(8,128)(2,1)S(1)} %bitcast.20, ...), custom_call_target="tpu_custom_call" | custom-call | tf_op jit(solution)/shard_map/video/pallas_call | solution.py:571
  32.6 11.8 %all-to-all-done.gathered = bf16[32,13,8,128]{3,2,1,0:T(8,128)(2,1)S(1)} async-done(((bf16[32,13,8,128]{3,2,1,0:T(8,128)(2,1)}), bf16[32,13,8,128]{3,2,1,0:T(8,128)(2,1)S(1)}, u32[]{:S(2)}, u32[]{:S(2)}) %all-to-all-start) | async-done | bytes 852000 | tf_op jit(solution)/shard_map/all_to_all | solution.py:617
  44.5 1.7 %scores.1 = (f32[32,3,4,128]{3,2,1,0:T(4,128)}, bf16[32,13,8,128]{3,2,1,0:T(8,128)(2,1)}) custom-call(s32[1]{0:T(128)S(6)} %copy.28.alen, s32[1]{0:T(128)S(6)} %copy.27.vlen, bf16[32,13,8,128]{3,2,1,0:T(8,128)(2,1)S(1)} %all-to-all-done.gathered, bf16[6,2,256,128]{3,2,1,0:T(8,128)(2,1)S(1)} %get-tuple-element.41.keys, f32[1,128]{1,0:T(1,128)S(1)} %copy-done.6, ...), custom_call_target="tpu_custom_call" | custom-call | tf_op jit(solution)/shard_map/scores/pallas_call | solution.py:571
  46.2 7.8 %all-to-all-start.1 = ((f32[32,3,4,128]{3,2,1,0:T(4,128)}), f32[32,3,4,128]{3,2,1,0:T(4,128)S(1)}, u32[]{:S(2)}, u32[]{:S(2)}) async-start(f32[32,3,4,128]{3,2,1,0:T(4,128)} %get-tuple-element.46), calls=%async_computation.1 | async-start | bytes 393216 | tf_op jit(solution)/shard_map/all_to_all | solution.py:644
  54.0 6.1 %queries.1 = (f32[6184,128]{1,0:T(8,128)S(1)}, bf16[32,6,8,128]{3,2,1,0:T(8,128)(2,1)}, bf16[6,256,128]{2,1,0:T(8,128)(2,1)}, bf16[6,2,128,128]{3,2,1,0:T(8,128)(2,1)}) custom-call(s32[1]{0:T(128)S(6)} %copy.28.alen, s32[1]{0:T(128)S(6)} %copy.27.vlen, bf16[6,3,256,128]{3,2,1,0:T(8,128)(2,1)} %get-tuple-element.37.queries_far, ...), custom_call_target="tpu_custom_call" | custom-call | tf_op jit(solution)/shard_map/queries/pallas_call | solution.py:571
  60.2 5.6 %all-to-all-done.1.totals = f32[32,3,4,128]{3,2,1,0:T(4,128)S(1)} async-done(((f32[32,3,4,128]{3,2,1,0:T(4,128)}), f32[32,3,4,128]{3,2,1,0:T(4,128)S(1)}, u32[]{:S(2)}, u32[]{:S(2)}) %all-to-all-start.1) | async-done | bytes 196640 | tf_op jit(solution)/shard_map/all_to_all | solution.py:644
  65.8 2.0 %back.1 = bf16[32,12,8,128]{3,2,1,0:T(8,128)(2,1)} custom-call(bf16[32,6,8,128]{3,2,1,0:T(8,128)(2,1)} %get-tuple-element.53.part_far, f32[32,3,4,128]{3,2,1,0:T(4,128)S(1)} %all-to-all-done.1.totals, f32[6184,128]{1,0:T(8,128)S(1)} %get-tuple-element.54.shared), custom_call_target="tpu_custom_call" | custom-call | tf_op jit(solution)/shard_map/back/pallas_call | solution.py:571
  67.7 6.2 %all-to-all-start.2 = ((bf16[32,12,8,128]{3,2,1,0:T(8,128)(2,1)}), bf16[32,12,8,128]{3,2,1,0:T(8,128)(2,1)S(1)}, u32[]{:S(2)}, u32[]{:S(2)}) async-start(bf16[32,12,8,128]{3,2,1,0:T(8,128)(2,1)} %back.1), calls=%async_computation.2 | async-start | bytes 1572864 | tf_op jit(solution)/shard_map/all_to_all | solution.py:670
  73.9 4.5 %keys.1 = (bf16[6,128,128]{2,1,0:T(8,128)(2,1)S(1)}, bf16[6,128,128]{2,1,0:T(8,128)(2,1)S(1)}, bf16[3,6,128,128]{3,2,1,0:T(8,128)(2,1)S(1)}) custom-call(s32[1]{0:T(128)S(6)} %copy.27.vlen, bf16[6,256,128]{2,1,0:T(8,128)(2,1)} %get-tuple-element.44.raw_vk_far, bf16[6,2,256,128]{3,2,1,0:T(8,128)(2,1)} %get-tuple-element.38.keys_far, f32[768,128]{1,0:T(8,128)} %bitcast.28, ...), custom_call_target="tpu_custom_call" | custom-call | tf_op jit(solution)/shard_map/keys/pallas_call | solution.py:571
  78.4 3.7 %collective-permute-start.1 = (bf16[3,6,128,128]{3,2,1,0:T(8,128)(2,1)S(1)}, bf16[3,6,128,128]{3,2,1,0:T(8,128)(2,1)S(1)}, u32[]{:S(2)}, u32[]{:S(2)}) collective-permute-start(bf16[3,6,128,128]{3,2,1,0:T(8,128)(2,1)S(1)} %get-tuple-element.49), channel_id=1, source_target_pairs={{0,1},{1,0},{2,3},{3,2},{4,5},{5,4},{6,7},{7,6},{8,9},{9,8},{10,11... | collective-permute-start | bytes 1769480 | tf_op jit(solution)/shard_map/ppermute | solution.py:684
  82.1 1.6 %collective-permute-done.1.got = bf16[3,6,128,128]{3,2,1,0:T(8,128)(2,1)S(1)} collective-permute-done((bf16[3,6,128,128]{3,2,1,0:T(8,128)(2,1)S(1)}, bf16[3,6,128,128]{3,2,1,0:T(8,128)(2,1)S(1)}, u32[]{:S(2)}, u32[]{:S(2)}) %collective-permute-start.1) | collective-permute-done | bytes 589856 | tf_op jit(solution)/shard_map/ppermute | solution.py:684
  83.7 1.3 %place.1 = (bf16[128,1536]{1,0:T(8,128)(2,1)}, bf16[128,1536]{1,0:T(8,128)(2,1)}, bf16[128,1536]{1,0:T(8,128)(2,1)}) custom-call(bf16[6,256,128]{2,1,0:T(8,128)(2,1)S(1)} %copy-done.4, bf16[6,128,128]{2,1,0:T(8,128)(2,1)S(1)} %get-tuple-element.47.key_own, bf16[6,128,128]{2,1,0:T(8,128)(2,1)S(1)} %get-tuple-element.48.value_own, ...), custom_call_target="tpu_custom_call" | custom-call | tf_op jit(solution)/shard_map/place/pallas_call | solution.py:571
  85.0 13.9 %all-to-all-done.2.got = bf16[32,12,8,128]{3,2,1,0:T(8,128)(2,1)S(1)} async-done(((bf16[32,12,8,128]{3,2,1,0:T(8,128)(2,1)}), bf16[32,12,8,128]{3,2,1,0:T(8,128)(2,1)S(1)}, u32[]{:S(2)}, u32[]{:S(2)}) %all-to-all-start.2) | async-done | bytes 786464 | tf_op jit(solution)/shard_map/all_to_all | solution.py:670
  98.9 1.0 audio.1
  99.9 5.4 %all-to-all-start.3 = ((f32[16,24,128]{2,1,0:T(8,128)}), f32[16,24,128]{2,1,0:T(8,128)S(1)}, u32[]{:S(2)}, u32[]{:S(2)}) async-start(f32[16,24,128]{2,1,0:T(8,128)} %get-tuple-element.56), calls=%async_computation.3 | async-start | bytes 393216 | tf_op jit(solution)/shard_map/all_to_all | solution.py:700
  105.3 2.0 %collective-permute-start.2 = (bf16[16,768]{1,0:T(8,128)(2,1)S(1)}, bf16[16,768]{1,0:T(8,128)(2,1)S(1)}, u32[]{:S(2)}, u32[]{:S(2)}) collective-permute-start(bf16[16,768]{1,0:T(8,128)(2,1)S(1)} %get-tuple-element.55.own), channel_id=1, source_target_pairs={{0,1},{1,0},{2,3},{3,2},{4,5},{5,4},{6,7},{7,6},{8,9},{9,8},{10,11... | collective-permute-start | bytes 73736 | tf_op jit(solution)/shard_map/ppermute | solution.py:701
  107.3 1.1 collective-permute-done.2.other
  108.4 3.6 %all-to-all-done.3.gains = f32[16,24,128]{2,1,0:T(8,128)S(1)} async-done(((f32[16,24,128]{2,1,0:T(8,128)}), f32[16,24,128]{2,1,0:T(8,128)S(1)}, u32[]{:S(2)}, u32[]{:S(2)}) %all-to-all-start.3) | async-done | bytes 196640 | tf_op jit(solution)/shard_map/all_to_all | solution.py:700
  112.0 0.6 last.1
  (19 shorter events, 0.0 us)
Async XLA Ops:
  0.6 28.0 %copy-start.6 = (f32[1,128]{1,0:T(1,128)S(1)}, f32[1,128]{1,0:T(1,128)}, u32[]{:S(2)}) copy-start(f32[1,128]{1,0:T(1,128)} %constant.2.clone.freqs.freqs_far) | copy-start | bytes 1540
  0.7 27.9 %copy-start.8 = (s32[1,128]{1,0:T(1,128)S(1)}, s32[1,128]{1,0:T(1,128)}, u32[]{:S(2)}) copy-start(s32[1,128]{1,0:T(1,128)} %pos_own.1) | copy-start | bytes 1540
  0.7 27.3 %copy-start.9 = (f32[1536]{0:T(1024)S(1)}, f32[1536]{0:T(1024)}, u32[]{:S(2)}) copy-start(f32[1536]{0:T(1024)} %param.32) | copy-start | bytes 18436
  0.7 27.3 %copy-start.10 = (f32[1536]{0:T(1024)S(1)}, f32[1536]{0:T(1024)}, u32[]{:S(2)}) copy-start(f32[1536]{0:T(1024)} %param.31) | copy-start | bytes 18436
  0.7 27.3 %copy-start.11 = (f32[1536]{0:T(1024)S(1)}, f32[1536]{0:T(1024)}, u32[]{:S(2)}) copy-start(f32[1536]{0:T(1024)} %param.30) | copy-start | bytes 18436
  0.7 27.3 %copy-start.12 = (f32[1536]{0:T(1024)S(1)}, f32[1536]{0:T(1024)}, u32[]{:S(2)}) copy-start(f32[1536]{0:T(1024)} %param.29) | copy-start | bytes 18436
  2.6 41.9 %all-to-all-start = ((bf16[32,13,8,128]{3,2,1,0:T(8,128)(2,1)}), bf16[32,13,8,128]{3,2,1,0:T(8,128)(2,1)S(1)}, u32[]{:S(2)}, u32[]{:S(2)}) async-start(bf16[32,13,8,128]{3,2,1,0:T(8,128)(2,1)} %payload.1), calls=%async_computation | async-start | bytes 1703936 | tf_op jit(solution)/shard_map/all_to_all | solution.py:617
  19.1 1.0 copy-start
  20.1 1.0 copy-start.1
  21.1 1.0 copy-start.2
  22.1 1.0 copy-start.3
  23.1 0.7 copy-start.7
  23.8 4.8 %collective-permute-start = (bf16[528,768]{1,0:T(8,128)(2,1)S(1)}, bf16[528,768]{1,0:T(8,128)(2,1)S(1)}, u32[]{:S(2)}, u32[]{:S(2)}) collective-permute-start(bf16[528,768]{1,0:T(8,128)(2,1)S(1)} %send.1), channel_id=1, source_target_pairs={{0,1},{1,0},{2,3},{3,2},{4,5},{5,4},{6,7},{7,6},{8,9},{9,8},{10,11... | collective-permute-start | bytes 2433032 | tf_op jit(solution)/shard_map/ppermute | solution.py:620
  28.0 45.9 %copy-start.5 = (f32[48,128]{1,0:T(8,128)}, f32[48,128]{1,0:T(8,128)S(1)}, u32[]{:S(2)}) copy-start(f32[48,128]{1,0:T(8,128)S(1)} %pad_maximum_fusion.gains.gains_far) | copy-start | bytes 73732
  46.2 19.6 %all-to-all-start.1 = ((f32[32,3,4,128]{3,2,1,0:T(4,128)}), f32[32,3,4,128]{3,2,1,0:T(4,128)S(1)}, u32[]{:S(2)}, u32[]{:S(2)}) async-start(f32[32,3,4,128]{3,2,1,0:T(4,128)} %get-tuple-element.46), calls=%async_computation.1 | async-start | bytes 393216 | tf_op jit(solution)/shard_map/all_to_all | solution.py:644
  67.7 16.0 %copy-start.4 = (bf16[6,256,128]{2,1,0:T(8,128)(2,1)S(1)}, bf16[6,256,128]{2,1,0:T(8,128)(2,1)}, u32[]{:S(2)}) copy-start(bf16[6,256,128]{2,1,0:T(8,128)(2,1)} %get-tuple-element.43.grad_far.query_own) | copy-start | bytes 1179652
  67.7 31.1 %all-to-all-start.2 = ((bf16[32,12,8,128]{3,2,1,0:T(8,128)(2,1)}), bf16[32,12,8,128]{3,2,1,0:T(8,128)(2,1)S(1)}, u32[]{:S(2)}, u32[]{:S(2)}) async-start(bf16[32,12,8,128]{3,2,1,0:T(8,128)(2,1)} %back.1), calls=%async_computation.2 | async-start | bytes 1572864 | tf_op jit(solution)/shard_map/all_to_all | solution.py:670
  78.4 5.3 %collective-permute-start.1 = (bf16[3,6,128,128]{3,2,1,0:T(8,128)(2,1)S(1)}, bf16[3,6,128,128]{3,2,1,0:T(8,128)(2,1)S(1)}, u32[]{:S(2)}, u32[]{:S(2)}) collective-permute-start(bf16[3,6,128,128]{3,2,1,0:T(8,128)(2,1)S(1)} %get-tuple-element.49), channel_id=1, source_target_pairs={{0,1},{1,0},{2,3},{3,2},{4,5},{5,4},{6,7},{7,6},{8,9},{9,8},{10,11... | collective-permute-start | bytes 1769480 | tf_op jit(solution)/shard_map/ppermute | solution.py:684
  99.9 12.1 %all-to-all-start.3 = ((f32[16,24,128]{2,1,0:T(8,128)}), f32[16,24,128]{2,1,0:T(8,128)S(1)}, u32[]{:S(2)}, u32[]{:S(2)}) async-start(f32[16,24,128]{2,1,0:T(8,128)} %get-tuple-element.56), calls=%async_computation.3 | async-start | bytes 393216 | tf_op jit(solution)/shard_map/all_to_all | solution.py:700
  105.3 3.1 %collective-permute-start.2 = (bf16[16,768]{1,0:T(8,128)(2,1)S(1)}, bf16[16,768]{1,0:T(8,128)(2,1)S(1)}, u32[]{:S(2)}, u32[]{:S(2)}) collective-permute-start(bf16[16,768]{1,0:T(8,128)(2,1)S(1)} %get-tuple-element.55.own), channel_id=1, source_target_pairs={{0,1},{1,0},{2,3},{3,2},{4,5},{5,4},{6,7},{7,6},{8,9},{9,8},{10,11... | collective-permute-start | bytes 73736 | tf_op jit(solution)/shard_map/ppermute | solution.py:701
